TPU v7x, 128 devices: a whole 4x4x4 slice. The times are simulated.
128 devices in a mesh: dev: 128 (over y, z, x, core).
Axes of the slice: x: 4, y: 4, z: 4, core: 2. Of those that a mesh axis runs over, the one named last changes fastest.
Arguments:
- params: float32 [59, 524288], P(None, 'dev'), may hold values from -40 to 40, as said below
- moment_one: float32 [59, 524288], P(None, 'dev'), may hold values from -3 to 3
- moment_two: float32 [59, 524288], P(None, 'dev'), may hold values from 0.01 to 1
- visible: int32 [2048, 512], P('dev'), may hold values from -1 to 524287, as said below
- counts: int32 [2048, 4], P('dev'), may hold values from 0 to 128, as said below
- tile_pos: int32 [2048], P('dev'), may hold values from 0 to 2047, as said below
- target: bfloat16 [2048, 3, 256], P('dev'), may hold values from 0 to 1
Outputs:
- tile_loss: float32 [2048], P('dev')
- new_params: float32 [59, 524288], P(None, 'dev')
- new_moment_one: float32 [59, 524288], P(None, 'dev')
- new_moment_two: float32 [59, 524288], P(None, 'dev')
Inputs may be any that keep to these rules, and one draw needn't show every extreme that they name: `visible`: row r holds the ids of the Gaussians that tile r composites, in compositing order; slot j is live when j % 128 < counts[r, j // 128], and a dead slot holds -1. Gaussian i is owned by device i // 4096. Among the live slots of the rows of one device at most 64 distinct ids belong to one owner, and on every device some owner has exactly 64. `counts`: the live slots of a row come first: block 0 holds 128, every block before a row's last live block holds 128 and every block after it 0. A permutation: rendered tile r is the screen tile in column tile_pos[r] % 64 and row tile_pos[r] // 64 of tiles. `params`: row 2 lies between 3 and 30.
All inputs are finite; a program needn't handle non-finite values.
Results may differ from a plain program's by a relative error of at most 0.0003.
Values sent between devices are 32-bit elements; how exact they have to be, the bound alone decides.
No kernel may reach another device: no remote copies, remote signals or barrier semaphores. Data moves between devices by JAX's collectives and lax.ppermute only.
A program may use at most 192 MiB of HBM per device.

v0:
```python
from functools import partial

import jax
import jax.numpy as jnp
from jax import lax
from jax.sharding import PartitionSpec as P

TILES_X = 64
ADAM_STEP = 1000


SH_ZERO = 0.28209479177387814
SH_ONE = 0.4886025119029199
SH_TWO = (
    1.0925484305920792,
    -1.0925484305920792,
    0.31539156525252005,
    -1.0925484305920792,
    0.5462742152960396,
)
SH_THREE = (
    -0.5900435899266435,
    2.890611442640554,
    -0.4570457994644658,
    0.3731763325901154,
    -0.4570457994644658,
    1.445305721320277,
    -0.5900435899266435,
)
BETA_ONE = 0.9
BETA_TWO = 0.999
ADAM_EPS = 1e-15


def harmonics(dir_x, dir_y, dir_z):
    sq_x = dir_x * dir_x
    sq_y = dir_y * dir_y
    sq_z = dir_z * dir_z
    return [
        SH_ZERO * jnp.ones_like(dir_x),
        -SH_ONE * dir_y,
        SH_ONE * dir_z,
        -SH_ONE * dir_x,
        SH_TWO[0] * dir_x * dir_y,
        SH_TWO[1] * dir_y * dir_z,
        SH_TWO[2] * (2.0 * sq_z - sq_x - sq_y),
        SH_TWO[3] * dir_x * dir_z,
        SH_TWO[4] * (sq_x - sq_y),
        SH_THREE[0] * dir_y * (3.0 * sq_x - sq_y),
        SH_THREE[1] * dir_x * dir_y * dir_z,
        SH_THREE[2] * dir_y * (4.0 * sq_z - sq_x - sq_y),
        SH_THREE[3] * dir_z * (2.0 * sq_z - 3.0 * sq_x - 3.0 * sq_y),
        SH_THREE[4] * dir_x * (4.0 * sq_z - sq_x - sq_y),
        SH_THREE[5] * dir_z * (sq_x - sq_y),
        SH_THREE[6] * dir_x * (sq_x - 3.0 * sq_y),
    ]


def project(param_rows, screen_width, screen_height):
    mean_x, mean_y, depths = (param_rows[0], param_rows[1], param_rows[2])
    scale_x = jnp.exp(param_rows[3])
    scale_y = jnp.exp(param_rows[4])
    scale_z = jnp.exp(param_rows[5])
    quat_len = jnp.maximum(
        jnp.sqrt(param_rows[6] ** 2 + param_rows[7] ** 2 + param_rows[8] ** 2 + param_rows[9] ** 2),
        0.5,
    )
    quat_w = param_rows[6] / quat_len
    quat_x = param_rows[7] / quat_len
    quat_y = param_rows[8] / quat_len
    quat_z = param_rows[9] / quat_len
    rot_xx = 1.0 - 2.0 * (quat_y * quat_y + quat_z * quat_z)
    rot_xy = 2.0 * (quat_x * quat_y - quat_w * quat_z)
    rot_xz = 2.0 * (quat_x * quat_z + quat_w * quat_y)
    rot_yx = 2.0 * (quat_x * quat_y + quat_w * quat_z)
    rot_yy = 1.0 - 2.0 * (quat_x * quat_x + quat_z * quat_z)
    rot_yz = 2.0 * (quat_y * quat_z - quat_w * quat_x)
    rot_zx = 2.0 * (quat_x * quat_z - quat_w * quat_y)
    rot_zy = 2.0 * (quat_y * quat_z + quat_w * quat_x)
    rot_zz = 1.0 - 2.0 * (quat_x * quat_x + quat_y * quat_y)
    m_xx, m_xy, m_xz = (rot_xx * scale_x, rot_xy * scale_y, rot_xz * scale_z)
    m_yx, m_yy, m_yz = (rot_yx * scale_x, rot_yy * scale_y, rot_yz * scale_z)
    m_zx, m_zy, m_zz = (rot_zx * scale_x, rot_zy * scale_y, rot_zz * scale_z)
    cov_xx = m_xx * m_xx + m_xy * m_xy + m_xz * m_xz
    cov_xy = m_xx * m_yx + m_xy * m_yy + m_xz * m_yz
    cov_xz = m_xx * m_zx + m_xy * m_zy + m_xz * m_zz
    cov_yy = m_yx * m_yx + m_yy * m_yy + m_yz * m_yz
    cov_yz = m_yx * m_zx + m_yy * m_zy + m_yz * m_zz
    cov_zz = m_zx * m_zx + m_zy * m_zy + m_zz * m_zz
    focal = 1.2 * screen_width
    inverse = 1.0 / depths
    jac_xx = focal * inverse
    jac_xz = -focal * mean_x * inverse * inverse
    jac_yy = focal * inverse
    jac_yz = -focal * mean_y * inverse * inverse
    plane_a = (
        jac_xx * jac_xx * cov_xx + 2.0 * jac_xx * jac_xz * cov_xz + jac_xz * jac_xz * cov_zz + 0.3
    )
    plane_b = (
        jac_xx * jac_yy * cov_xy
        + jac_xx * jac_yz * cov_xz
        + jac_xz * jac_yy * cov_yz
        + jac_xz * jac_yz * cov_zz
    )
    plane_c = (
        jac_yy * jac_yy * cov_yy + 2.0 * jac_yy * jac_yz * cov_yz + jac_yz * jac_yz * cov_zz + 0.3
    )
    determ = plane_a * plane_c - plane_b * plane_b
    screen_u = focal * mean_x * inverse + 0.5 * screen_width
    screen_v = focal * mean_y * inverse + 0.5 * screen_height
    distance = jnp.sqrt(mean_x * mean_x + mean_y * mean_y + depths * depths)
    basis = harmonics(mean_x / distance, mean_y / distance, depths / distance)
    colours = []
    for channel in range(3):
        total = 0.5 + basis[0] * param_rows[11 + channel]
        for degree in range(1, 16):
            total = total + basis[degree] * param_rows[11 + 3 * degree + channel]
        colours.append(total)
    return jnp.stack(
        [
            screen_u,
            screen_v,
            plane_c / determ,
            -plane_b / determ,
            plane_a / determ,
            jax.nn.sigmoid(param_rows[10]),
            colours[0],
            colours[1],
            colours[2],
        ]
    )


def pixel_coords(tile_pos):
    offset = jnp.arange(256, dtype=jnp.int32)
    pix_x = (tile_pos % TILES_X)[:, None] * 16 + (offset % 16)[None, :]
    pix_y = (tile_pos // TILES_X)[:, None] * 16 + (offset // 16)[None, :]
    return (pix_x.astype(jnp.float32), pix_y.astype(jnp.float32))


def opacities(features, slot_live, pix_x, pix_y):
    delta_x = pix_x[:, :, None] - features[0][:, None, :]
    delta_y = pix_y[:, :, None] - features[1][:, None, :]
    exponent = (
        0.5
        * (
            features[2][:, None, :] * delta_x * delta_x
            + features[4][:, None, :] * delta_y * delta_y
        )
        + features[3][:, None, :] * delta_x * delta_y
    )
    alphas = 0.99 * features[5][:, None, :] * jnp.exp(-exponent) * slot_live[:, None, :]
    return (alphas, jnp.log(1.0 - alphas))


def render_tiles(block_feats, block_mask, pix_x, pix_y, block_live):
    blocks_n = block_mask.shape[0]
    tiles_n = block_mask.shape[1]
    position = jnp.arange(128)
    strictly = (position[:, None] < position[None, :]).astype(jnp.float32)

    @jax.checkpoint
    def compute(state_in, features, slot_live):
        log_left, colors = state_in
        alphas, log_keep = opacities(features, slot_live, pix_x, pix_y)
        before = jnp.einsum("kpg,gh->kph", log_keep, strictly, precision=lax.Precision.HIGHEST)
        weights = alphas * jnp.exp(log_left[:, :, None] + before)
        colors = colors + jnp.einsum(
            "kpg,ckg->kcp", weights, features[6:9], precision=lax.Precision.HIGHEST
        )
        return (log_left + jnp.sum(log_keep, axis=2), colors)

    def one_block(state, block_index):
        features = lax.dynamic_index_in_dim(block_feats, block_index, 1, keepdims=False)
        slot_live = lax.dynamic_index_in_dim(block_mask, block_index, 0, keepdims=False)
        active = block_live[block_index]

        def skipped(state_in, features_in, live_in):
            return state_in

        return (lax.cond(active, compute, skipped, state, features, slot_live), None)

    start_state = (
        jnp.zeros((tiles_n, 256), jnp.float32),
        jnp.zeros((tiles_n, 3, 256), jnp.float32),
    )
    (log_left, colors), unused = lax.scan(
        one_block, start_state, jnp.arange(blocks_n, dtype=jnp.int32)
    )
    return colors


def learn_rates():
    position = jnp.arange(59)
    rate_rows = jnp.where(
        position < 3,
        0.0016,
        jnp.where(
            position < 6,
            0.005,
            jnp.where(
                position < 10,
                0.001,
                jnp.where(position < 11, 0.05, jnp.where(position < 14, 0.0025, 0.000125)),
            ),
        ),
    )
    return rate_rows.astype(jnp.float32)[:, None]


def adam(params, gradients, moment_one, moment_two):
    moment_new = BETA_ONE * moment_one + (1.0 - BETA_ONE) * gradients
    square_new = BETA_TWO * moment_two + (1.0 - BETA_TWO) * gradients * gradients
    fix_one = 1.0 - BETA_ONE**ADAM_STEP
    fix_two = 1.0 - BETA_TWO**ADAM_STEP
    update = moment_new / fix_one / (jnp.sqrt(square_new / fix_two) + ADAM_EPS)
    return (params - learn_rates() * update, moment_new, square_new)


def shards(params, moment_one, moment_two, visible, counts, tile_pos, target):
    devices = lax.axis_size("dev")
    tiles_here, list_len = visible.shape
    blocks_here = list_len // 128
    gauss_here = params.shape[1]
    bucket = tiles_here * list_len // devices
    screen_width = TILES_X * 16.0
    screen_height = devices * tiles_here // TILES_X * 16.0
    live = (jnp.arange(128, dtype=jnp.int32)[None, None, :] < counts[:, :, None]).reshape(
        tiles_here, list_len
    )
    sentinel = devices * gauss_here
    flat_keys = jnp.where(live, visible, sentinel).reshape(-1)
    sort_order = jnp.argsort(flat_keys, stable=True)
    keys_sorted = flat_keys[sort_order]
    previous = jnp.concatenate([jnp.full((1,), -1, jnp.int32), keys_sorted[:-1]])
    is_first = (keys_sorted != previous) & (keys_sorted < sentinel)
    owners = keys_sorted // gauss_here
    local_ids = keys_sorted % gauss_here
    unique_rank = jnp.cumsum(is_first.astype(jnp.int32)) - 1
    owner_grid = owners[:, None] == jnp.arange(devices, dtype=jnp.int32)[None, :]
    per_owner = jnp.sum((owner_grid & is_first[:, None]).astype(jnp.int32), axis=0)
    first_slot = jnp.cumsum(per_owner) - per_owner
    first_here = jnp.sum(jnp.where(owner_grid, first_slot[None, :], 0), axis=1)
    buffer_pos = jnp.where(keys_sorted < sentinel, owners * bucket + unique_rank - first_here, 0)
    write_pos = jnp.where(is_first, buffer_pos, devices * bucket)
    request = (
        jnp.zeros((devices * bucket,), jnp.int32)
        .at[write_pos]
        .set(local_ids, mode="drop")
        .reshape(devices, bucket)
    )
    slot_pos = jnp.zeros_like(buffer_pos).at[sort_order].set(buffer_pos)
    block_pos = jnp.transpose(slot_pos.reshape(tiles_here, blocks_here, 128), (1, 0, 2)).reshape(-1)
    wanted = lax.all_to_all(request, "dev", split_axis=0, concat_axis=0, tiled=True)
    picked = jnp.take(params, wanted.reshape(-1), axis=1)
    outgoing = picked.reshape(picked.shape[0], devices, -1)
    returned = lax.all_to_all(outgoing, "dev", split_axis=1, concat_axis=1, tiled=True)
    arrived = returned
    asked_ids = wanted[None]
    arrived = arrived.reshape(arrived.shape[0], devices * bucket)
    pix_x, pix_y = pixel_coords(tile_pos)
    target_f = target.astype(jnp.float32)
    block_mask = (
        jnp.arange(128, dtype=jnp.int32)[None, None, :] < jnp.transpose(counts)[:, :, None]
    ).astype(jnp.float32)
    block_live = jnp.any(counts > 0, axis=0)

    def losses_of(buffer_feats):
        block_feats = jnp.take(buffer_feats, block_pos, axis=1).reshape(
            9, blocks_here, tiles_here, 128
        )
        colors = render_tiles(block_feats, block_mask, pix_x, pix_y, block_live)
        errors = colors - target_f
        return jnp.sum(errors * errors, axis=(1, 2)) / 16.0

    project_here = partial(project, screen_width=screen_width, screen_height=screen_height)

    def raw_losses(buffer_rows):
        return losses_of(project_here(buffer_rows))

    tile_loss, pull_back = jax.vjp(raw_losses, arrived)
    (slot_grads,) = pull_back(jnp.ones_like(tile_loss))
    received = lax.all_to_all(
        slot_grads.reshape(slot_grads.shape[0], devices, bucket),
        "dev",
        split_axis=1,
        concat_axis=1,
        tiled=True,
    )
    row_grads = received.reshape(received.shape[0], -1)
    gradients = jnp.zeros_like(params).at[:, asked_ids.reshape(-1)].add(row_grads)
    new_params, moment_new, square_new = adam(params, gradients, moment_one, moment_two)
    return (tile_loss, new_params, moment_new, square_new)


def solution(mesh):
    placed = (
        P(None, "dev"),
        P(None, "dev"),
        P(None, "dev"),
        P("dev", None),
        P("dev", None),
        P("dev"),
        P("dev", None, None),
    )
    return jax.shard_map(
        shards,
        mesh=mesh,
        in_specs=placed,
        out_specs=(P("dev"), P(None, "dev"), P(None, "dev"), P(None, "dev")),
        check_vma=False,
    )
```

profile of v0, /device:TPU:1, one launch (start us, length us, event | category | flops | bytes accessed | tf_op | source)
XLA Modules:
  0.0 752.2 jit_solution(4749231453078916584)
XLA Ops:
  9.1 45.5 %gather_fusion = s32[8192]{0:T(1024)S(1)} fusion(s32[8192]{0:T(1024)S(1)} %bitcast.128, s32[8192]{0:T(1024)S(1)} %get-tuple-element.1015), kind=kCustom, calls=%fused_computation | custom fusion | bytes 98304 | tf_op jit(solution)/shard_map/gather | solution.py:234
  61.5 30.5 %scatter_custom_fusion.1 = s32[8192]{0:T(1024)S(1)} fusion(s32[8192]{0:T(1024)S(1)} %bitcast.203, s32[8192]{0:T(1024)S(1)} %get-tuple-element.1020, s32[]{:T(128)} %copy.558), kind=kCustom, calls=%fused_computation.419 | custom fusion | bytes 32772 | tf_op jit(solution)/shard_map/scatter | solution.py:249
  92.7 11.5 %all-to-all-start = ((s32[128,1,64]{2,1,0:T(1,128)}), s32[128,1,64]{2,1,0:T(1,128)S(1)}, u32[]{:S(2)}, u32[]{:S(2)}) async-start(s32[128,1,64]{2,1,0:T(1,128)} %bitcast.49), calls=%async_computation | async-start | bytes 131072 | tf_op jit(solution)/shard_map/all_to_all | solution.py:254
  104.9 31.0 %scatter_custom_fusion = s32[8192]{0:T(1024)S(1)} fusion(s32[8192]{0:T(1024)S(1)} %get-tuple-element.1014, s32[8192]{0:T(1024)S(1)} %get-tuple-element.878, s32[]{:T(128)} %copy.558), kind=kCustom, calls=%fused_computation.417 | custom fusion | bytes 32772 | tf_op jit(solution)/shard_map/scatter | solution.py:252
  139.2 27.7 %gather_fusion.1 = f32[8192,59]{1,0:T(8,128)} fusion(f32[59,4096]{0,1:T(8,128)S(1)} %copy.357, s32[8192]{0:T(1024)S(1)} %broadcast_clamp_fusion), kind=kCustom, calls=%fused_computation.1 | custom fusion | bytes 3899392 | tf_op jit(solution)/shard_map/jit(_take)/gather | solution.py:255
  184.8 9.8 %all-to-all-start.1 = ((f32[128,1,3776]{2,1,0:T(1,128)}), f32[128,1,3776]{2,1,0:T(1,128)S(1)}, u32[]{:S(2)}, u32[]{:S(2)}) async-start(f32[128,1,3776]{2,1,0:T(1,128)} %reshape.4659), calls=%async_computation.1 | async-start | bytes 3932160 | tf_op jit(solution)/shard_map/all_to_all | solution.py:257
  195.2 28.5 %all-to-all-done.1 = f32[128,1,3776]{2,1,0:T(1,128)S(1)} async-done(((f32[128,1,3776]{2,1,0:T(1,128)}), f32[128,1,3776]{2,1,0:T(1,128)S(1)}, u32[]{:S(2)}, u32[]{:S(2)}) %all-to-all-start.1) | async-done | bytes 1933344 | tf_op jit(solution)/shard_map/all_to_all | solution.py:257
  224.3 7.2 reduce.239
  236.2 8.1 %slice_reduce_fusion.14 = (f32[128,64]{1,0:T(8,128)}, f32[128,64]{1,0:T(8,128)S(1)}, f32[128,64]{1,0:T(8,128)S(1)}, f32[128,64]{1,0:T(8,128)S(1)}, f32[128,64]{1...) fusion(f32[59,128,64]{2,0,1:T(8,128)} %bitcast.132), kind=kLoop, calls=%fused_computation.173 | loop fusion | flops 16384 | bytes 1179648 | tf_op jit(solution)/shard_map/jvp()/slice | solution.py:117
  247.6 8.0 %slice_reduce_fusion.29 = (f32[128,64]{1,0:T(8,128)S(1)}, f32[128,64]{1,0:T(8,128)S(1)}, f32[128,64]{1,0:T(8,128)S(1)}, f32[128,64]{1,0:T(8,128)S(1)}, f32[128,6...) fusion(f32[59,128,64]{2,0,1:T(8,128)} %bitcast.134), kind=kLoop, calls=%fused_computation.191 | loop fusion | flops 16384 | bytes 1179648 | tf_op jit(solution)/shard_map/jvp()/slice | solution.py:117
  255.6 7.9 %slice_reduce_fusion.44 = (f32[128,64]{1,0:T(8,128)S(1)}, f32[128,64]{1,0:T(8,128)S(1)}, f32[128,64]{1,0:T(8,128)S(1)}, f32[128,64]{1,0:T(8,128)S(1)}, f32[128,6...) fusion(f32[59,128,64]{2,0,1:T(8,128)} %bitcast.135), kind=kLoop, calls=%fused_computation.209 | loop fusion | flops 16384 | bytes 1179648 | tf_op jit(solution)/shard_map/jvp()/slice | solution.py:117
  303.1 29.9 %gather_fusion.2 = f32[8192,9]{1,0:T(8,128)} fusion(f32[9,8192]{0,1:T(8,128)} %copy.363, s32[8192]{0:T(1024)S(1)} %copy-done.113), kind=kCustom, calls=%fused_computation.2 | custom fusion | bytes 622592 | tf_op jit(solution)/shard_map/jvp(jit(_take))/gather | solution.py:269
  336.3 42.9 %while.49 = (s32[]{:T(128)}, f32[16,256]{1,0:T(8,128)S(1)}, f32[16,3,256]{2,1,0:T(4,128)S(1)}, s32[4]{0:T(128)S(1)}, s32[4]{0:T(128)S(1)}, /*index=5*/f32[4,16,2...) while((s32[]{:T(128)}, f32[16,256]{1,0:T(8,128)S(1)}, ...), condition=%wide.region_13.14_spmd.clone.clone, body=%wide.region_9.13_spmd.clone.clone.sunk | while | flops 848902144 | bytes 5712824 | solution.py:187
  340.0 12.0 %conditional.7 = (f32[16,256]{1,0:T(8,128)S(1)}, f32[16,3,256]{2,1,0:T(4,128)S(1)}, f32[1,16,256]{2,1,0:T(8,128)S(1)}, f32[1,16,256]{2,1,0:T(8,128)S(1)}, f32[1,...) conditional(s32[]{:T(128)} %bitcast.125, ...), branch_computations={%region_10.10_spmd, %region_11.12_spmd} | conditional | flops 848836608 | bytes 5071028 | solution.py:181
  356.2 12.0 %conditional.7 = (f32[16,256]{1,0:T(8,128)S(1)}, f32[16,3,256]{2,1,0:T(4,128)S(1)}, f32[1,16,256]{2,1,0:T(8,128)S(1)}, f32[1,16,256]{2,1,0:T(8,128)S(1)}, f32[1,...) conditional(s32[]{:T(128)} %bitcast.125, ...), branch_computations={%region_10.10_spmd, %region_11.12_spmd} | conditional | flops 848836608 | bytes 5071028 | solution.py:181
  379.4 49.7 %while.48 = (s32[]{:T(128)}, f32[9,4,16,128]{3,2,1,0:T(8,128)S(1)}, f32[16,256]{1,0:T(8,128)S(1)}, f32[16,3,256]{2,1,0:T(4,128)S(1)}, s32[4]{0:T(128)S(1)}, /*in...) while((s32[]{:T(128)}, f32[9,4,16,128]{3,2,1,0:T(8,128)S(1)}, ...), condition=%wide.region_25.26_spmd, body=%wide.region_15.25_spmd.sunk | while | flops 1699866624 | bytes 12468533 | solution.py:187
  386.6 19.0 %conditional.6 = (f32[16,256]{1,0:T(8,128)S(1)}, f32[16,3,256]{2,1,0:T(4,128)S(1)}, f32[9,1,16,128]{3,0,2,1:T(8,128)S(1)}) conditional(s32[]{:T(128)} %bitcast.123, (f32[16,256]{1,0:T(8,128)S(1)}, f32[16,3,256]{2,1,0:T(4,128)S(1)}) %tuple.343, (f32[4,16,256]{2,1,0:T(8,128)S(1)}, s32[]{:T(128)}, f32[4,16,256]{2,1,0:T(8,128)S(1)}, ...), branch_computations={%region_16.16_spmd, %region_17.24_spmd} | conditional | flops 1699848192 | bytes 11894828 | solution.py:181
  408.2 19.0 %conditional.6 = (f32[16,256]{1,0:T(8,128)S(1)}, f32[16,3,256]{2,1,0:T(4,128)S(1)}, f32[9,1,16,128]{3,0,2,1:T(8,128)S(1)}) conditional(s32[]{:T(128)} %bitcast.123, (f32[16,256]{1,0:T(8,128)S(1)}, f32[16,3,256]{2,1,0:T(4,128)S(1)}) %tuple.343, (f32[4,16,256]{2,1,0:T(8,128)S(1)}, s32[]{:T(128)}, f32[4,16,256]{2,1,0:T(8,128)S(1)}, ...), branch_computations={%region_16.16_spmd, %region_17.24_spmd} | conditional | flops 1699848192 | bytes 11894828 | solution.py:181
  432.1 54.4 %scatter_custom_fusion.2 = f32[9,8192]{0,1:T(8,128)} fusion(s32[8192]{0:T(1024)} %bitcast.200, f32[8192,9]{1,0:T(8,128)} %copy.367, f32[]{:T(128)} %constant.314.clone.1), kind=kCustom, calls=%fused_computation.135 | custom fusion | flops 73728 | bytes 295424 | tf_op jit(solution)/shard_map/transpose(jvp(jit(_take)))/scatter-add | solution.py:269
  486.5 33.9 %fusion.200 = (f32[1,8192]{0,1:T(8,128)}, f32[1,8192]{0,1:T(8,128)}, f32[1,8192]{0,1:T(8,128)}, f32[1,8192]{0,1:T(8,128)}, f32[1,8192]{0,1:T(8,128)}, /*index=5*...) fusion(f32[9,8192]{0,1:T(8,128)} %scatter_custom_fusion.2), kind=kLoop, calls=%fused_computation.498 | loop fusion | bytes 589824 | tf_op jit(solution)/shard_map/transpose(jvp())/unstack | solution.py:119
  581.8 60.3 %all-to-all-start.2 = ((f32[128,1,3776]{2,1,0:T(1,128)}), f32[128,1,3776]{2,1,0:T(1,128)S(1)}, u32[]{:S(2)}, u32[]{:S(2)}) async-start(f32[128,1,3776]{2,1,0:T(1,128)} %reshape.4661), calls=%async_computation.2 | async-start | bytes 3932160 | tf_op jit(solution)/shard_map/all_to_all | solution.py:283
  642.7 28.5 %all-to-all-done.2 = f32[128,1,3776]{2,1,0:T(1,128)S(1)} async-done(((f32[128,1,3776]{2,1,0:T(1,128)}), f32[128,1,3776]{2,1,0:T(1,128)S(1)}, u32[]{:S(2)}, u32[]{:S(2)}) %all-to-all-start.2) | async-done | bytes 1933344 | tf_op jit(solution)/shard_map/all_to_all | solution.py:283
  671.2 7.2 reduce.240
  695.4 50.7 %scatter_custom_fusion.3 = f32[59,4096]{0,1:T(8,128)S(1)} fusion(s32[8192]{0:T(1024)} %bitcast.198, f32[8192,59]{1,0:T(8,128)} %copy.379, f32[]{:T(128)} %constant.314.clone.1), kind=kCustom, calls=%fused_computation.142 | custom fusion | flops 483328 | bytes 967168 | tf_op jit(solution)/shard_map/scatter-add | solution.py:291
  (580 shorter events, 256.1 us)
Async XLA Ops:
  9.1 95.1 %copy-start.129 = (s32[16,4]{0,1:T(4,128)S(1)}, s32[16,4]{0,1:T(4,128)}, u32[]{:S(2)}) copy-start(s32[16,4]{0,1:T(4,128)} %param.19) | copy-start | bytes 772
  9.1 126.8 %copy-start.135 = (s32[16]{0:T(128)S(1)}, s32[16]{0:T(128)}, u32[]{:S(2)}) copy-start(s32[16]{0:T(128)} %param.20) | copy-start | bytes 196
  54.6 81.9 %copy-start = (f32[59,4096]{1,0:T(8,128)S(1)}, f32[59,4096]{1,0:T(8,128)}, u32[]{:S(2)}) copy-start(f32[59,4096]{1,0:T(8,128)} %param.15) | copy-start | bytes 2899972
  92.7 45.2 %all-to-all-start = ((s32[128,1,64]{2,1,0:T(1,128)}), s32[128,1,64]{2,1,0:T(1,128)S(1)}, u32[]{:S(2)}, u32[]{:S(2)}) async-start(s32[128,1,64]{2,1,0:T(1,128)} %bitcast.49), calls=%async_computation | async-start | bytes 131072 | tf_op jit(solution)/shard_map/all_to_all | solution.py:254
  139.2 27.7 %copy-start.123 = (s32[8192,1]{0,1:T(1,128)}, s32[8192,1]{0,1:T(1,128)S(1)}, u32[]{:S(2)}) copy-start(s32[8192,1]{0,1:T(1,128)S(1)} %compare_select_fusion.1) | copy-start | bytes 98308
  184.8 38.9 %all-to-all-start.1 = ((f32[128,1,3776]{2,1,0:T(1,128)}), f32[128,1,3776]{2,1,0:T(1,128)S(1)}, u32[]{:S(2)}, u32[]{:S(2)}) async-start(f32[128,1,3776]{2,1,0:T(1,128)} %reshape.4659), calls=%async_computation.1 | async-start | bytes 3932160 | tf_op jit(solution)/shard_map/all_to_all | solution.py:257
  194.6 41.6 %copy-start.124 = (s32[8192,1]{0,1:T(1,128)}, s32[8192,1]{0,1:T(1,128)S(1)}, u32[]{:S(2)}) copy-start(s32[8192,1]{0,1:T(1,128)S(1)} %compare_select_fusion) | copy-start | bytes 98308
  265.2 28.9 %copy-start.96 = (f32[1,8192]{1,0:T(1,128)}, f32[1,8192]{1,0:T(1,128)S(1)}, u32[]{:S(2)}) copy-start(f32[1,8192]{1,0:T(1,128)S(1)} %squeeze.296) | copy-start | bytes 98308
  265.3 28.8 %copy-start.98 = (f32[1,8192]{1,0:T(1,128)}, f32[1,8192]{1,0:T(1,128)S(1)}, u32[]{:S(2)}) copy-start(f32[1,8192]{1,0:T(1,128)S(1)} %squeeze.297) | copy-start | bytes 98308
  266.3 27.9 %copy-start.100 = (f32[1,8192]{1,0:T(1,128)}, f32[1,8192]{1,0:T(1,128)S(1)}, u32[]{:S(2)}) copy-start(f32[1,8192]{1,0:T(1,128)S(1)} %squeeze.298) | copy-start | bytes 98308
  266.4 27.8 %copy-start.102 = (f32[1,8192]{1,0:T(1,128)}, f32[1,8192]{1,0:T(1,128)S(1)}, u32[]{:S(2)}) copy-start(f32[1,8192]{1,0:T(1,128)S(1)} %squeeze.299) | copy-start | bytes 98308
  267.3 26.8 %copy-start.104 = (f32[1,8192]{1,0:T(1,128)}, f32[1,8192]{1,0:T(1,128)S(1)}, u32[]{:S(2)}) copy-start(f32[1,8192]{1,0:T(1,128)S(1)} %squeeze.300) | copy-start | bytes 98308
  267.4 26.7 %copy-start.106 = (f32[1,8192]{1,0:T(1,128)}, f32[1,8192]{1,0:T(1,128)S(1)}, u32[]{:S(2)}) copy-start(f32[1,8192]{1,0:T(1,128)S(1)} %squeeze.301) | copy-start | bytes 98308
  268.4 25.7 %copy-start.108 = (f32[1,8192]{1,0:T(1,128)}, f32[1,8192]{1,0:T(1,128)S(1)}, u32[]{:S(2)}) copy-start(f32[1,8192]{1,0:T(1,128)S(1)} %squeeze.302) | copy-start | bytes 98308
  269.4 24.8 %copy-start.110 = (f32[1,8192]{1,0:T(1,128)}, f32[1,8192]{1,0:T(1,128)S(1)}, u32[]{:S(2)}) copy-start(f32[1,8192]{1,0:T(1,128)S(1)} %squeeze.303) | copy-start | bytes 98308
  279.0 17.4 %copy-start.47 = (f32[1,8192]{1,0:T(1,128)}, f32[1,8192]{1,0:T(1,128)S(1)}, u32[]{:S(2)}) copy-start(f32[1,8192]{1,0:T(1,128)S(1)} %squeeze.281) | copy-start | bytes 98308
  279.1 17.3 %copy-start.49 = (f32[1,8192]{1,0:T(1,128)}, f32[1,8192]{1,0:T(1,128)S(1)}, u32[]{:S(2)}) copy-start(f32[1,8192]{1,0:T(1,128)S(1)} %squeeze.282) | copy-start | bytes 98308
  279.3 17.2 %copy-start.51 = (f32[1,8192]{1,0:T(1,128)}, f32[1,8192]{1,0:T(1,128)S(1)}, u32[]{:S(2)}) copy-start(f32[1,8192]{1,0:T(1,128)S(1)} %squeeze.283) | copy-start | bytes 98308
  279.4 17.1 %copy-start.53 = (f32[1,8192]{1,0:T(1,128)}, f32[1,8192]{1,0:T(1,128)S(1)}, u32[]{:S(2)}) copy-start(f32[1,8192]{1,0:T(1,128)S(1)} %squeeze.284) | copy-start | bytes 98308
  279.5 17.0 %copy-start.55 = (f32[1,8192]{1,0:T(1,128)}, f32[1,8192]{1,0:T(1,128)S(1)}, u32[]{:S(2)}) copy-start(f32[1,8192]{1,0:T(1,128)S(1)} %squeeze.285) | copy-start | bytes 98308
  279.6 16.9 %copy-start.57 = (f32[1,8192]{1,0:T(1,128)}, f32[1,8192]{1,0:T(1,128)S(1)}, u32[]{:S(2)}) copy-start(f32[1,8192]{1,0:T(1,128)S(1)} %squeeze.286) | copy-start | bytes 98308
  279.7 16.8 %copy-start.59 = (f32[1,8192]{1,0:T(1,128)}, f32[1,8192]{1,0:T(1,128)S(1)}, u32[]{:S(2)}) copy-start(f32[1,8192]{1,0:T(1,128)S(1)} %squeeze.287) | copy-start | bytes 98308
  336.2 42.9 %copy-start.132 = (bf16[16,3,256]{2,0,1:T(8,128)(2,1)S(1)}, bf16[16,3,256]{2,0,1:T(8,128)(2,1)}, u32[]{:S(2)}) copy-start(bf16[16,3,256]{2,0,1:T(8,128)(2,1)} %param.21) | copy-start | bytes 73732
  581.8 89.3 %all-to-all-start.2 = ((f32[128,1,3776]{2,1,0:T(1,128)}), f32[128,1,3776]{2,1,0:T(1,128)S(1)}, u32[]{:S(2)}, u32[]{:S(2)}) async-start(f32[128,1,3776]{2,1,0:T(1,128)} %reshape.4661), calls=%async_computation.2 | async-start | bytes 3932160 | tf_op jit(solution)/shard_map/all_to_all | solution.py:283
  (117 other events, 657.9 us)
where the time goes:
time: 761 us; the launch traced here: 752 us
  local copies, waits for them, and re-layouts  338 us (44%)
  other arithmetic  203 us (27%)
  starting transfers between devices  81.6 us (11%)
  waiting for transfers between devices  57 us (7%)
  matrix products  54 us (7%)
  loops' own time  14.4 us (2%)
    all_to_all x1, starting transfers between devices, shards(): lax.all_to_all(slot_grads.reshape(slot_grads.shape[0], devices, bucket),...  60.3 us
    scatter-add x1, other arithmetic, losses_of(): jnp.take(buffer_feats, block_pos, axis=1)  54.4 us
    scatter-add x1, other arithmetic, shards(): jnp.zeros_like(params).at[:, asked_ids.reshape(-1)].add(row_grads)  50.7 us
    unnamed x295, local copies, waits for them, and re-layouts  48.9 us
    gather x1, local copies, waits for them, and re-layouts, shards(): keys_sorted = flat_keys[sort_order]  45.5 us
    another operation x3, local copies, waits for them, and re-layouts, project(): jnp.stack([screen_u, screen_v, plane_c / determ, -plane_b / determ, plane...  37.7 us
    gather x2, local copies, waits for them, and re-layouts, shards(): picked = jnp.take(params, wanted.reshape(-1), axis=1)  33.3 us
    gather x2, local copies, waits for them, and re-layouts, losses_of(): jnp.take(buffer_feats, block_pos, axis=1)  32.8 us
  transfers between devices with their start and end apart: 3, of which 2 were waited for; matrix products, arithmetic and copies ran while one was open for 5% of the time, Pallas kernels for 0%

commit v1 on v0

v1 whole, which is shorter than its diff:
```python
import numpy as np
import jax
import jax.numpy as jnp
from jax import lax
from jax.experimental import pallas as pl
from jax.experimental.pallas import tpu as pltpu
from jax.sharding import PartitionSpec as P

N_DEV = 128
G_DEV = 4096
CAP = 64
TILES_X = 64
ADAM_STEP = 1000
SENTINEL = N_DEV * G_DEV
SCREEN_W = 1024.0
SCREEN_H = 512.0

SH_ZERO = 0.28209479177387814
SH_ONE = 0.4886025119029199
SH_TWO = (
    1.0925484305920792,
    -1.0925484305920792,
    0.31539156525252005,
    -1.0925484305920792,
    0.5462742152960396,
)
SH_THREE = (
    -0.5900435899266435,
    2.890611442640554,
    -0.4570457994644658,
    0.3731763325901154,
    -0.4570457994644658,
    1.445305721320277,
    -0.5900435899266435,
)
BETA_ONE = 0.9
BETA_TWO = 0.999
ADAM_EPS = 1e-15
LOG2_E = 1.4426950408889634

F32 = jnp.float32
BF16 = jnp.bfloat16
VMEM = pl.BlockSpec(memory_space=pltpu.VMEM)


def harmonics(dir_x, dir_y, dir_z):
    sq_x = dir_x * dir_x
    sq_y = dir_y * dir_y
    sq_z = dir_z * dir_z
    return [
        -SH_ONE * dir_y,
        SH_ONE * dir_z,
        -SH_ONE * dir_x,
        SH_TWO[0] * dir_x * dir_y,
        SH_TWO[1] * dir_y * dir_z,
        SH_TWO[2] * (2.0 * sq_z - sq_x - sq_y),
        SH_TWO[3] * dir_x * dir_z,
        SH_TWO[4] * (sq_x - sq_y),
        SH_THREE[0] * dir_y * (3.0 * sq_x - sq_y),
        SH_THREE[1] * dir_x * dir_y * dir_z,
        SH_THREE[2] * dir_y * (4.0 * sq_z - sq_x - sq_y),
        SH_THREE[3] * dir_z * (2.0 * sq_z - 3.0 * sq_x - 3.0 * sq_y),
        SH_THREE[4] * dir_x * (4.0 * sq_z - sq_x - sq_y),
        SH_THREE[5] * dir_z * (sq_x - sq_y),
        SH_THREE[6] * dir_x * (sq_x - 3.0 * sq_y),
    ]


def directions(mean_x, mean_y, depths):
    distance = jnp.sqrt(mean_x * mean_x + mean_y * mean_y + depths * depths)
    return harmonics(mean_x / distance, mean_y / distance, depths / distance)


def geometry(rows):
    mean_x, mean_y, depths = (rows[0], rows[1], rows[2])
    scale_x = jnp.exp(rows[3])
    scale_y = jnp.exp(rows[4])
    scale_z = jnp.exp(rows[5])
    quat_len = jnp.maximum(
        jnp.sqrt(rows[6] * rows[6] + rows[7] * rows[7] + rows[8] * rows[8] + rows[9] * rows[9]),
        0.5,
    )
    quat_w = rows[6] / quat_len
    quat_x = rows[7] / quat_len
    quat_y = rows[8] / quat_len
    quat_z = rows[9] / quat_len
    rot_xx = 1.0 - 2.0 * (quat_y * quat_y + quat_z * quat_z)
    rot_xy = 2.0 * (quat_x * quat_y - quat_w * quat_z)
    rot_xz = 2.0 * (quat_x * quat_z + quat_w * quat_y)
    rot_yx = 2.0 * (quat_x * quat_y + quat_w * quat_z)
    rot_yy = 1.0 - 2.0 * (quat_x * quat_x + quat_z * quat_z)
    rot_yz = 2.0 * (quat_y * quat_z - quat_w * quat_x)
    rot_zx = 2.0 * (quat_x * quat_z - quat_w * quat_y)
    rot_zy = 2.0 * (quat_y * quat_z + quat_w * quat_x)
    rot_zz = 1.0 - 2.0 * (quat_x * quat_x + quat_y * quat_y)
    m_xx, m_xy, m_xz = (rot_xx * scale_x, rot_xy * scale_y, rot_xz * scale_z)
    m_yx, m_yy, m_yz = (rot_yx * scale_x, rot_yy * scale_y, rot_yz * scale_z)
    m_zx, m_zy, m_zz = (rot_zx * scale_x, rot_zy * scale_y, rot_zz * scale_z)
    cov_xx = m_xx * m_xx + m_xy * m_xy + m_xz * m_xz
    cov_xy = m_xx * m_yx + m_xy * m_yy + m_xz * m_yz
    cov_xz = m_xx * m_zx + m_xy * m_zy + m_xz * m_zz
    cov_yy = m_yx * m_yx + m_yy * m_yy + m_yz * m_yz
    cov_yz = m_yx * m_zx + m_yy * m_zy + m_yz * m_zz
    cov_zz = m_zx * m_zx + m_zy * m_zy + m_zz * m_zz
    focal = 1.2 * SCREEN_W
    inverse = 1.0 / depths
    jac_xx = focal * inverse
    jac_xz = -focal * mean_x * inverse * inverse
    jac_yy = focal * inverse
    jac_yz = -focal * mean_y * inverse * inverse
    plane_a = (
        jac_xx * jac_xx * cov_xx + 2.0 * jac_xx * jac_xz * cov_xz + jac_xz * jac_xz * cov_zz + 0.3
    )
    plane_b = (
        jac_xx * jac_yy * cov_xy
        + jac_xx * jac_yz * cov_xz
        + jac_xz * jac_yy * cov_yz
        + jac_xz * jac_yz * cov_zz
    )
    plane_c = (
        jac_yy * jac_yy * cov_yy + 2.0 * jac_yy * jac_yz * cov_yz + jac_yz * jac_yz * cov_zz + 0.3
    )
    determ = plane_a * plane_c - plane_b * plane_b
    return (
        focal * mean_x * inverse + 0.5 * SCREEN_W,
        focal * mean_y * inverse + 0.5 * SCREEN_H,
        plane_c / determ,
        -plane_b / determ,
        plane_a / determ,
    )


def split(value):
    high = value.astype(BF16)
    return (high, (value - high.astype(F32)).astype(BF16))


def dot_nt(left, right):
    return lax.dot_general(left, right, (((1,), (1,)), ((), ())), preferred_element_type=F32)


def dot_nn(left, right):
    return jnp.dot(left, right, preferred_element_type=F32)


def one_hot(index_row, size):
    rows = lax.broadcasted_iota(jnp.int32, (size, index_row.shape[1]), 0)
    return jnp.where(rows == index_row, 1.0, 0.0).astype(BF16)


def iota(shape, axis):
    return lax.broadcasted_iota(jnp.int32, shape, axis)


def rows_first(ref, out_ref):
    for base in range(0, 59, 8):
        size = min(8, 59 - base)
        for piece in range(32):
            out_ref[pl.ds(base * 32 + piece, size, stride=32), :] = ref[
                base : base + size, piece * 128 : (piece + 1) * 128
            ]


def plan_kernel(sorted_ref, keys_ref, request_ref, rank_ref, owner_s, rank_s, first_s, local_s):
    keys = sorted_ref[...]
    lane = iota((64, 128), 1)
    before = pltpu.roll(keys, 1, 1)
    before = jnp.where(lane == 0, pltpu.roll(before, 1, 0), before)
    position = iota((64, 128), 0) * 128 + lane
    fresh = ((keys != before) | (position == 0)) & (keys < SENTINEL)
    fresh_f = jnp.where(fresh, 1.0, 0.0).astype(F32)
    fresh_h = fresh_f.astype(BF16)
    upto = jnp.where(iota((128, 128), 0) <= iota((128, 128), 1), 1.0, 0.0).astype(BF16)
    ones = jnp.ones((128, 128), BF16)
    lower = jnp.where(iota((64, 64), 1) < iota((64, 64), 0), 1.0, 0.0).astype(BF16)
    within = dot_nn(fresh_h, upto)
    totals = dot_nn(fresh_h, ones).astype(BF16)
    count = within + dot_nn(lower, totals)
    owner = keys >> 12
    owner_s[...] = owner
    first_s[...] = fresh_f
    local_s[...] = keys & (G_DEV - 1)

    def pair(ref, index):
        return jnp.concatenate(
            [ref[pl.ds(2 * index, 1), :], ref[pl.ds(2 * index + 1, 1), :]], axis=1
        )

    def smaller(index, total):
        owners = pair(owner_s, index)
        is_less = jnp.where(owners < iota((128, 256), 0), 1.0, 0.0).astype(BF16)
        firsts = jnp.broadcast_to(pair(first_s, index), (8, 256)).astype(BF16)
        return total + dot_nt(firsts, is_less)

    first_of = lax.fori_loop(0, 32, smaller, jnp.zeros((8, 128), F32), unroll=4)
    offsets = jnp.broadcast_to(first_of[0:1], (64, 128)).astype(jnp.int32)
    offset = jnp.take_along_axis(offsets, owner & 127, axis=1, mode="promise_in_bounds")
    rank_s[...] = count.astype(jnp.int32) - 1 - offset

    def fill(index, total):
        owners = pair(owner_s, index)
        ranks = pair(rank_s, index)
        firsts = pair(first_s, index) > 0.0
        local = pair(local_s, index)
        match = (ranks == iota((64, 256), 0)) & firsts
        high = jnp.where(match, (local >> 6).astype(F32), 0.0).astype(BF16)
        low = jnp.where(match, (local & 63).astype(F32), 0.0).astype(BF16)
        used = jnp.where(match, 1.0, 0.0).astype(BF16)
        parts = jnp.concatenate([high, low, used], axis=0)
        return total + dot_nt(parts, one_hot(owners, 128))

    filled = lax.fori_loop(0, 32, fill, jnp.zeros((192, 128), F32), unroll=2)
    locals_of = (filled[0:64] * 64.0 + filled[64:128]).astype(jnp.int32)
    table = jnp.where(filled[128:192] > 0.5, locals_of, -1)
    padded = jnp.concatenate([locals_of, jnp.zeros((64, 128), jnp.int32)], axis=0)
    request_ref[...] = jnp.transpose(padded)

    slots = keys_ref[...]
    slot_owner = (slots >> 12) & 127
    slot_local = slots & (G_DEV - 1)
    rank = jnp.zeros((64, 128), jnp.int32)
    for place in range(64):
        row = jnp.broadcast_to(table[place : place + 1], (64, 128))
        found = jnp.take_along_axis(row, slot_owner, axis=1, mode="promise_in_bounds")
        rank = jnp.where(found == slot_local, place, rank)
    rank_ref[...] = rank


def plan(keys_sorted, keys):
    return pl.pallas_call(
        plan_kernel,
        out_shape=(
            jax.ShapeDtypeStruct((128, 128), jnp.int32),
            jax.ShapeDtypeStruct((64, 128), jnp.int32),
        ),
        in_specs=[VMEM, VMEM],
        out_specs=(VMEM, VMEM),
        scratch_shapes=[
            pltpu.VMEM((64, 128), jnp.int32),
            pltpu.VMEM((64, 128), jnp.int32),
            pltpu.VMEM((64, 128), F32),
            pltpu.VMEM((64, 128), jnp.int32),
        ],
        compiler_params=pltpu.CompilerParams(vmem_limit_bytes=32 * 1024 * 1024),
    )(keys_sorted, keys)


def project_kernel(params_ref, feats_ref, rows_s):
    rows_first(params_ref, rows_s)

    def row(index):
        return rows_s[index * 32 : (index + 1) * 32, :]

    rows = [row(index) for index in range(10)]
    feats = list(geometry(rows))
    feats.append(1.0 / (1.0 + jnp.exp(-row(10))))
    basis = directions(rows[0], rows[1], rows[2])
    for channel in range(3):
        total = 0.5 + SH_ZERO * row(11 + channel)
        for degree in range(1, 16):
            total = total + basis[degree - 1] * row(11 + 3 * degree + channel)
        feats.append(total)
    for index in range(9):
        feats_ref[index * 32 : (index + 1) * 32, :] = feats[index]


def project(params):
    return pl.pallas_call(
        project_kernel,
        out_shape=jax.ShapeDtypeStruct((288, 128), F32),
        in_specs=[VMEM],
        out_specs=VMEM,
        scratch_shapes=[pltpu.VMEM((59 * 32, 128), F32)],
        compiler_params=pltpu.CompilerParams(vmem_limit_bytes=32 * 1024 * 1024),
    )(params)


def serve_kernel(feats_ref, wanted_ref, out_ref, place_s):
    wanted = jnp.transpose(wanted_ref[...])[0:64]
    high = wanted >> 7
    low = wanted & 127
    for feature in range(9):
        total = jnp.zeros((64, 128), F32)
        for piece in range(32):
            row = jnp.broadcast_to(
                feats_ref[feature * 32 + piece : feature * 32 + piece + 1, :], (64, 128)
            )
            found = jnp.take_along_axis(row, low, axis=1, mode="promise_in_bounds")
            total = jnp.where(high == piece, found, total)
        place_s[feature * 64 : (feature + 1) * 64, :] = total
    place_s[576:640, :] = jnp.zeros((64, 128), F32)
    for part in range(5):
        out_ref[pl.ds(part, 128, stride=5), :] = jnp.transpose(
            place_s[part * 128 : (part + 1) * 128, :]
        )


def serve(feats, wanted):
    return pl.pallas_call(
        serve_kernel,
        out_shape=jax.ShapeDtypeStruct((640, 128), F32),
        in_specs=[VMEM, VMEM],
        out_specs=VMEM,
        scratch_shapes=[pltpu.VMEM((640, 128), F32)],
        compiler_params=pltpu.CompilerParams(vmem_limit_bytes=32 * 1024 * 1024),
    )(feats, wanted)


def pixel_basis():
    pixel = np.arange(256)
    across = (pixel % 16) - 7.5
    down = (pixel // 16) - 7.5
    six = np.stack([across * across, across * down, down * down, across, down, np.ones(256)])
    basis = np.zeros((24, 256), np.float32)
    basis[0:18] = np.tile(six, (3, 1))
    moments = np.zeros((16, 256), np.float32)
    moments[0:6] = six
    return (jnp.asarray(basis, BF16), jnp.asarray(moments, BF16))


def render_kernel(
    arrived_ref,
    keys_ref,
    rank_ref,
    centre_ref,
    target_ref,
    basis_ref,
    moment_ref,
    out_ref,
    loss_ref,
    table_s,
    coef_s,
    alpha_s,
    weight_s,
    sums_s,
    grads_s,
):
    for part in range(5):
        table_s[part * 128 : (part + 1) * 128, :] = jnp.transpose(
            arrived_ref[pl.ds(part, 128, stride=5), :]
        )
    keys = keys_ref[...]
    rank = rank_ref[...]
    live = keys < SENTINEL
    owner = (keys >> 12) & 127
    feats = []
    for feature in range(9):
        total = jnp.zeros((64, 128), F32)
        for place in range(64):
            row = jnp.broadcast_to(
                table_s[feature * 64 + place : feature * 64 + place + 1, :], (64, 128)
            )
            found = jnp.take_along_axis(row, owner, axis=1, mode="promise_in_bounds")
            total = jnp.where(rank == place, found, total)
        feats.append(total)
    half = iota((64, 128), 0) < 32
    tile = jnp.where(
        half,
        jnp.broadcast_to(centre_ref[0:1, :], (64, 128)),
        jnp.broadcast_to(centre_ref[1:2, :], (64, 128)),
    )
    rel_u = feats[0] - ((tile & (TILES_X - 1)).astype(F32) * 16.0 + 7.5)
    rel_v = feats[1] - ((tile >> 6).astype(F32) * 16.0 + 7.5)
    conic_1, conic_2, conic_3 = (feats[2], feats[3], feats[4])
    h_1 = 0.5 * conic_1
    h_3 = 0.5 * conic_3
    pull_u = conic_1 * rel_u + conic_2 * rel_v
    pull_v = conic_3 * rel_v + conic_2 * rel_u
    centre_e = 0.5 * (conic_1 * rel_u * rel_u + conic_3 * rel_v * rel_v) + conic_2 * rel_u * rel_v
    level = jnp.log2(0.99 * feats[5])
    coefs = [
        -LOG2_E * h_1,
        -LOG2_E * conic_2,
        -LOG2_E * h_3,
        LOG2_E * pull_u,
        LOG2_E * pull_v,
        level - LOG2_E * centre_e,
    ]
    for index in range(6):
        value = jnp.where(live, coefs[index], -1024.0 if index == 5 else 0.0)
        high = value.astype(BF16).astype(F32)
        rest = value - high
        middle = rest.astype(BF16).astype(F32)
        coef_s[pl.ds(index, 64, stride=24), :] = high
        coef_s[pl.ds(index + 6, 64, stride=24), :] = middle
        coef_s[pl.ds(index + 12, 64, stride=24), :] = rest - middle
    for channel in range(3):
        value = feats[6 + channel]
        high = value.astype(BF16).astype(F32)
        coef_s[pl.ds(18 + channel, 64, stride=24), :] = high
        coef_s[pl.ds(21 + channel, 64, stride=24), :] = value - high

    diagonal = (iota((8, 128), 1) & 7) == iota((8, 128), 0)

    def spread(coef, base):
        return jnp.concatenate(
            [
                jnp.where(
                    diagonal,
                    jnp.broadcast_to(coef[base + channel : base + channel + 1], (8, 128)),
                    0.0,
                )
                for channel in range(3)
            ],
            axis=0,
        )

    for group in range(2):

        def forward(index, state):
            left, colors = state
            chunk = group * 32 + index
            coef = coef_s[pl.ds(pl.multiple_of(chunk * 24, 8), 24), :]
            powers = dot_nn(jnp.transpose(coef).astype(BF16), basis_ref[...])
            alpha = jnp.exp2(powers)
            rows = pl.ds(pl.multiple_of(index * 128, 128), 128)
            alpha_s[rows, :] = alpha
            parts = []
            for slot in range(16):
                weight = alpha[slot * 8 : (slot + 1) * 8] * left
                left = left - weight
                parts.append(weight)
            weights = jnp.concatenate(parts, axis=0)
            weight_s[rows, :] = weights
            high, low = split(weights)
            col_high = spread(coef, 18).astype(BF16)
            col_low = spread(coef, 21).astype(BF16)
            colors = (
                colors
                + dot_nn(col_high, high)
                + dot_nn(col_low, high)
                + dot_nn(col_high, low)
            )
            return (left, colors)

        left, colors = lax.fori_loop(
            0, 32, forward, (jnp.ones((8, 256), F32), jnp.zeros((24, 256), F32))
        )
        errors = colors - target_ref[group * 24 : (group + 1) * 24, :]
        squares = errors * errors
        total = jnp.sum(squares[0:8] + squares[8:16] + squares[16:24], axis=1, keepdims=True)
        loss_ref[group * 8 : (group + 1) * 8, :] = jnp.broadcast_to(total / 16.0, (8, 128))
        err = errors * 0.125
        err_high, err_low = split(err)
        err_three = jnp.concatenate([err_high, err_low, err_high], axis=0)

        def backward(step, behind):
            index = 31 - step
            chunk = group * 32 + index
            coef = coef_s[pl.ds(pl.multiple_of(chunk * 24, 8), 24), :]
            col_high = spread(coef, 18)
            col_low = spread(coef, 21)
            col_three = jnp.concatenate([col_high, col_high, col_low], axis=0)
            shades = dot_nn(jnp.transpose(col_three).astype(BF16), err_three)
            rows = pl.ds(pl.multiple_of(index * 128, 128), 128)
            alpha = alpha_s[rows, :]
            weights = weight_s[rows, :]
            parts = []
            for slot in range(15, -1, -1):
                cut = slice(slot * 8, (slot + 1) * 8)
                gap = shades[cut] - behind
                parts.append(weights[cut] * gap)
                behind = behind + alpha[cut] * gap
            pulls = jnp.concatenate(parts[::-1], axis=0)
            pull_high, pull_low = split(pulls)
            sums = dot_nt(moment_ref[...], pull_high) + dot_nt(moment_ref[...], pull_low)
            high, low = split(weights)
            tints = dot_nt(err_high, high) + dot_nt(err_low, high) + dot_nt(err_high, low)
            sums_s[pl.ds(pl.multiple_of(chunk * 16, 8), 8), :] = sums[0:8]
            for channel in range(3):
                own = jnp.where(diagonal, tints[channel * 8 : (channel + 1) * 8], 0.0)
                sums_s[pl.ds(chunk * 16 + 8 + channel, 1), :] = jnp.sum(
                    own, axis=0, keepdims=True
                )
            return behind

        lax.fori_loop(0, 32, backward, jnp.zeros((8, 256), F32))

    def sums_of(index):
        return sums_s[pl.ds(index, 64, stride=16), :]

    m_xx, m_xy, m_yy, m_x, m_y, m_0 = [sums_of(index) for index in range(6)]
    s_x = m_x - rel_u * m_0
    s_y = m_y - rel_v * m_0
    s_xx = m_xx - 2.0 * rel_u * m_x + rel_u * rel_u * m_0
    s_yy = m_yy - 2.0 * rel_v * m_y + rel_v * rel_v * m_0
    s_xy = m_xy - rel_u * m_y - rel_v * m_x + rel_u * rel_v * m_0
    slot_grads = [
        conic_1 * s_x + conic_2 * s_y,
        conic_3 * s_y + conic_2 * s_x,
        -0.5 * s_xx,
        -s_xy,
        -0.5 * s_yy,
        m_0,
        sums_of(8),
        sums_of(9),
        sums_of(10),
    ]
    for index in range(9):
        grads_s[pl.ds(index, 64, stride=16), :] = jnp.where(live, slot_grads[index], 0.0)
    grads_s[pl.ds(9, 64, stride=16), :] = ((rank >> 5) * 128 + owner).astype(F32)
    grads_s[pl.ds(10, 64, stride=16), :] = (rank & 31).astype(F32)

    def gather_rows(index, size, lanes, total):
        both = jnp.concatenate(
            [
                grads_s[pl.ds(pl.multiple_of(index * 32, 8), 16), :],
                grads_s[pl.ds(pl.multiple_of(index * 32 + 16, 8), 16), :],
            ],
            axis=1,
        )
        return scatter_step(both, size, total)

    def scatter(index, total):
        return gather_rows(index, 32, 256, total)

    collected = lax.fori_loop(0, 32, scatter, jnp.zeros((288, 256), F32))
    for feature in range(9):
        piece = collected[feature * 32 : (feature + 1) * 32]
        table_s[feature * 64 : feature * 64 + 32, :] = piece[:, 0:128]
        table_s[feature * 64 + 32 : feature * 64 + 64, :] = piece[:, 128:256]
    table_s[576:640, :] = jnp.zeros((64, 128), F32)
    for part in range(5):
        out_ref[pl.ds(part, 128, stride=5), :] = jnp.transpose(
            table_s[part * 128 : (part + 1) * 128, :]
        )


def scatter_step(both, size, total):
    lanes = one_hot(both[9:10].astype(jnp.int32), 256)
    match = iota((size, 256), 0) == both[10:11].astype(jnp.int32)
    high = both.astype(BF16).astype(F32)
    low = both - high
    masked = [
        jnp.where(match, jnp.broadcast_to(part[feature : feature + 1], (size, 256)), 0.0)
        for part in (high, low)
        for feature in range(9)
    ]
    found = dot_nt(jnp.concatenate(masked, axis=0).astype(BF16), lanes)
    return total + found[0 : 9 * size] + found[9 * size : 18 * size]


def render(arrived, keys, rank, centre, target):
    basis, moments = pixel_basis()
    return pl.pallas_call(
        render_kernel,
        out_shape=(
            jax.ShapeDtypeStruct((640, 128), F32),
            jax.ShapeDtypeStruct((16, 128), F32),
        ),
        in_specs=[VMEM] * 7,
        out_specs=(VMEM, VMEM),
        scratch_shapes=[
            pltpu.VMEM((640, 128), F32),
            pltpu.VMEM((64 * 24, 128), F32),
            pltpu.VMEM((4096, 256), F32),
            pltpu.VMEM((4096, 256), F32),
            pltpu.VMEM((64 * 16, 128), F32),
            pltpu.VMEM((64 * 16, 128), F32),
        ],
        compiler_params=pltpu.CompilerParams(vmem_limit_bytes=48 * 1024 * 1024),
    )(arrived, keys, rank, centre, target, basis, moments)


def learn_rate(index):
    if index < 3:
        return 0.0016
    if index < 6:
        return 0.005
    if index < 10:
        return 0.001
    if index < 11:
        return 0.05
    return 0.0025 if index < 14 else 0.000125


def update_kernel(
    received_ref,
    wanted_ref,
    params_ref,
    one_ref,
    two_ref,
    rates_ref,
    new_params_ref,
    new_one_ref,
    new_two_ref,
    rows_s,
    grads_s,
    table_s,
):
    wanted = jnp.transpose(wanted_ref[...])[0:64]
    piece = wanted >> 7
    for part in range(5):
        turned = jnp.transpose(received_ref[pl.ds(part, 128, stride=5), :])
        table_s[pl.ds(2 * part, 64, stride=16), :] = turned[0:64]
        if part < 4:
            table_s[pl.ds(2 * part + 1, 64, stride=16), :] = turned[64:128]
    table_s[pl.ds(9, 64, stride=16), :] = ((piece >> 4) * 128 + (wanted & 127)).astype(F32)
    table_s[pl.ds(10, 64, stride=16), :] = (piece & 15).astype(F32)

    def scatter(index, total):
        both = jnp.concatenate(
            [
                table_s[pl.ds(pl.multiple_of(index * 32, 8), 16), :],
                table_s[pl.ds(pl.multiple_of(index * 32 + 16, 8), 16), :],
            ],
            axis=1,
        )
        return scatter_step(both, 16, total)

    collected = lax.fori_loop(0, 32, scatter, jnp.zeros((144, 256), F32))

    def grad_of(feature):
        part = collected[feature * 16 : (feature + 1) * 16]
        return jnp.concatenate([part[:, 0:128], part[:, 128:256]], axis=0)

    rows_first(params_ref, rows_s)

    def row(index):
        return rows_s[index * 32 : (index + 1) * 32, :]

    def put(index, value):
        grads_s[index * 32 : (index + 1) * 32, :] = value

    rows = [row(index) for index in range(10)]
    unused, pull_geometry = jax.vjp(geometry, rows)
    (geo_grads,) = pull_geometry(tuple(grad_of(feature) for feature in range(5)))
    put(10, grad_of(5) * (1.0 / (1.0 + jnp.exp(row(10)))))
    basis, pull_basis = jax.vjp(directions, rows[0], rows[1], rows[2])
    tints = [grad_of(6 + channel) for channel in range(3)]
    basis_grads = []
    for channel in range(3):
        put(11 + channel, SH_ZERO * tints[channel])
    for degree in range(1, 16):
        total = None
        for channel in range(3):
            index = 11 + 3 * degree + channel
            put(index, basis[degree - 1] * tints[channel])
            term = row(index) * tints[channel]
            total = term if total is None else total + term
        basis_grads.append(total)
    mean_grads = pull_basis(basis_grads)
    for index in range(10):
        put(index, geo_grads[index] + mean_grads[index] if index < 3 else geo_grads[index])

    fix_one = 1.0 / (1.0 - BETA_ONE**ADAM_STEP)
    fix_two = 1.0 / (1.0 - BETA_TWO**ADAM_STEP)
    for base in range(0, 59, 8):
        size = min(8, 59 - base)
        rate = jnp.broadcast_to(rates_ref[base : base + size, 0:1], (size, 128))
        for piece in range(32):
            cut = (slice(base, base + size), slice(piece * 128, (piece + 1) * 128))
            grad = grads_s[pl.ds(base * 32 + piece, size, stride=32), :]
            one = BETA_ONE * one_ref[cut] + (1.0 - BETA_ONE) * grad
            two = BETA_TWO * two_ref[cut] + (1.0 - BETA_TWO) * grad * grad
            new_one_ref[cut] = one
            new_two_ref[cut] = two
            step = one * fix_one / (jnp.sqrt(two * fix_two) + ADAM_EPS)
            new_params_ref[cut] = params_ref[cut] - rate * step


def update(received, wanted, params, moment_one, moment_two):
    rates = np.zeros((64, 128), np.float32)
    rates[0:59] = np.array([learn_rate(index) for index in range(59)], np.float32)[:, None]
    whole = jax.ShapeDtypeStruct((59, G_DEV), F32)
    return pl.pallas_call(
        update_kernel,
        out_shape=(whole, whole, whole),
        in_specs=[VMEM] * 6,
        out_specs=(VMEM, VMEM, VMEM),
        scratch_shapes=[
            pltpu.VMEM((59 * 32, 128), F32),
            pltpu.VMEM((59 * 32, 128), F32),
            pltpu.VMEM((64 * 16, 128), F32),
        ],
        compiler_params=pltpu.CompilerParams(vmem_limit_bytes=48 * 1024 * 1024),
    )(received, wanted, params, moment_one, moment_two, jnp.asarray(rates))


def slot_keys(visible, counts):
    live = jnp.arange(128, dtype=jnp.int32)[None, None, :] < counts[:, :, None]
    keys = jnp.where(live.reshape(visible.shape), visible, SENTINEL)
    return jnp.transpose(keys.reshape(2, 8, 512), (0, 2, 1)).reshape(64, 128)


def exchange(array):
    flat = array.reshape(N_DEV, 1, -1)
    flat = lax.all_to_all(flat, "dev", split_axis=0, concat_axis=0, tiled=True)
    return flat.reshape(array.shape)


def shards(params, moment_one, moment_two, visible, counts, tile_pos, target):
    keys = slot_keys(visible, counts)
    keys_sorted = lax.sort(keys.reshape(-1), is_stable=False).reshape(64, 128)
    request, rank = plan(keys_sorted, keys)
    feats = project(params)
    wanted = exchange(request)
    arrived = exchange(serve(feats, wanted))
    centre = jnp.tile(tile_pos.reshape(2, 8), (1, 16))
    colours = target.astype(F32).reshape(2, 8, 3, 256)
    colours = jnp.transpose(colours, (0, 2, 1, 3)).reshape(48, 256)
    grads, loss = render(arrived, keys, rank, centre, colours)
    received = exchange(grads)
    outs = update(received, wanted, params, moment_one, moment_two)
    return (loss[:, 0], *outs)


def solution(mesh):
    placed = (
        P(None, "dev"),
        P(None, "dev"),
        P(None, "dev"),
        P("dev", None),
        P("dev", None),
        P("dev"),
        P("dev", None, None),
    )
    return jax.shard_map(
        shards,
        mesh=mesh,
        in_specs=placed,
        out_specs=(P("dev"), P(None, "dev"), P(None, "dev"), P(None, "dev")),
        check_vma=False,
    )
```

time: 761 us -> 171 us (0.22); the launches traced: 752 us -> 170 us
  local copies, waits for them, and re-layouts: 338 us -> 10.6 us
  other arithmetic: 203 us -> 6.35 us
  Pallas kernels: 0 us -> 104 us
  starting transfers between devices: 81.6 us -> 20.7 us
  matrix products: 54 us -> 0 us
  waiting for transfers between devices: 57 us -> 27.7 us
  loops' own time: 14.4 us -> 0 us
    gather x5 -> x0, local copies, waits for them, and re-layouts: 112 us -> none  [the longest x1 45.5 us: shards(): keys_sorted = flat_keys[sort_order]]
    scatter-add x2 -> x0, other arithmetic: 105 us -> none  [the longest x1 54.4 us: losses_of(): jnp.take(buffer_feats, block_pos, axis=1)]
    pallas_call x0 -> x5, Pallas kernels: none -> 104 us  [the longest x1 77 us: render(): pl.pallas_call(render_kernel, out_shape=(jax.ShapeDtypeStruct((640, 128),...]
    scatter x2 -> x0, local copies, waits for them, and re-layouts: 61.5 us -> none  [the longest x1 31 us: shards(): slot_pos = jnp.zeros_like(buffer_pos).at[sort_order].set(buffer_pos)]
    all_to_all x3, starting transfers between devices: 81.6 us -> 20.7 us  [exchange(): flat = lax.all_to_all(flat, 'dev', split_axis=0, concat_axis=0, tiled=True)]
    dot_general x12 -> x0, matrix products: 54 us -> none  [the longest x6 31.3 us: compute(): jnp.einsum('kpg,gh->kph', log_keep, strictly, precision=lax.Precision.HIG...]
    unnamed x295 -> x33, local copies, waits for them, and re-layouts: 48.9 us -> 6.46 us
    another operation x11 -> x4, local copies, waits for them, and re-layouts: 40.6 us -> 2.4 us  [the longest x3 2.15 us: shards(): centre = jnp.tile(tile_pos.reshape(2, 8), (1, 16))]
  transfers between devices with their start and end apart: 3 -> 3, of which waited for: 2 -> 3; matrix products, arithmetic and copies ran while one was open for 5% -> 2% of each run, Pallas kernels for 0% -> 0%
where the time goes in v1:
time: 171 us; the launch traced here: 170 us
  Pallas kernels  104 us (61%)
  waiting for transfers between devices  27.7 us (16%)
  starting transfers between devices  20.7 us (12%)
  local copies, waits for them, and re-layouts  10.6 us (6%)
  other arithmetic  6.35 us (4%)
    pallas_call x1, Pallas kernels, render(): pl.pallas_call(render_kernel, out_shape=(jax.ShapeDtypeStruct((640, 128),...  77 us
    all_to_all x3, waiting for transfers between devices, exchange(): flat = lax.all_to_all(flat, 'dev', split_axis=0, concat_axis=0, tiled=True)  27.7 us
    all_to_all x3, starting transfers between devices, exchange(): flat = lax.all_to_all(flat, 'dev', split_axis=0, concat_axis=0, tiled=True)  20.7 us
    pallas_call x1, Pallas kernels, update(): pl.pallas_call(update_kernel, out_shape=(whole, whole, whole), in_specs=[...  11.6 us
    pallas_call x1, Pallas kernels, serve(): pl.pallas_call(serve_kernel, out_shape=jax.ShapeDtypeStruct((640, 128), F...  7.57 us
    pallas_call x1, Pallas kernels, plan(): pl.pallas_call(plan_kernel, out_shape=(jax.ShapeDtypeStruct((128, 128), j...  7.33 us
    unnamed x33, local copies, waits for them, and re-layouts  6.46 us
    sort x1, other arithmetic, shards(): keys_sorted = lax.sort(keys.reshape(-1), is_stable=False).reshape(64, 128)  5.59 us
  transfers between devices with their start and end apart: 3, of which 3 were waited for; matrix products, arithmetic and copies ran while one was open for 2% of the time, Pallas kernels for 0%

profile of v1, /device:TPU:1, one launch (start us, length us, event | category | flops | bytes accessed | tf_op | source)
XLA Modules:
  0.0 170.4 jit_solution(18423615545095571635)
XLA Ops:
  0.7 0.6 copy-done.15
  2.2 5.6 %sort.7 = s32[8192]{0:T(1024)S(1)} sort(s32[8192]{0:T(1024)S(1)} %reshape_reshape.3), dimensions={0}, to_apply=%region_0.1 | sort | flops 106496 | bytes 65536 | tf_op jit(solution)/shard_map/sort | solution.py:694
  7.8 7.3 %shard_map.130 = (s32[128,128]{1,0:T(8,128)}, s32[64,128]{1,0:T(8,128)S(1)}) custom-call(s32[64,128]{1,0:T(8,128)S(1)} %bitcast.31, s32[64,128]{1,0:T(8,128)S(1)} %reshape.54.keys_ref), custom_call_target="tpu_custom_call" | custom-call | tf_op jit(solution)/shard_map/pallas_call | solution.py:230
  15.8 11.5 %all-to-all-start = ((s32[128,1,128]{2,1,0:T(1,128)}), s32[128,1,128]{2,1,0:T(1,128)S(1)}, u32[]{:S(2)}, u32[]{:S(2)}) async-start(s32[128,1,128]{2,1,0:T(1,128)} %bitcast.5), calls=%async_computation | async-start | bytes 131072 | tf_op jit(solution)/shard_map/all_to_all | solution.py:688
  27.3 0.7 shard_map.129.feats_ref
  28.0 8.7 %all-to-all-done = s32[128,1,128]{2,1,0:T(1,128)S(1)} async-done(((s32[128,1,128]{2,1,0:T(1,128)}), s32[128,1,128]{2,1,0:T(1,128)S(1)}, u32[]{:S(2)}, u32[]{:S(2)}) %all-to-all-start) | async-done | bytes 65568 | tf_op jit(solution)/shard_map/all_to_all | solution.py:688
  36.7 7.6 %shard_map.131 = f32[640,128]{1,0:T(8,128)} custom-call(f32[288,128]{1,0:T(8,128)S(1)} %shard_map.129.feats_ref, s32[128,128]{1,0:T(8,128)S(1)} %bitcast.27), custom_call_target="tpu_custom_call" | custom-call | tf_op jit(solution)/shard_map/pallas_call | solution.py:299
  44.3 4.6 %all-to-all-start.1 = ((f32[128,1,640]{2,1,0:T(1,128)}), f32[128,1,640]{2,1,0:T(1,128)S(1)}, u32[]{:S(2)}, u32[]{:S(2)}) async-start(f32[128,1,640]{2,1,0:T(1,128)} %bitcast.7), calls=%async_computation.1 | async-start | bytes 655360 | tf_op jit(solution)/shard_map/all_to_all | solution.py:688
  48.9 0.7 tile.10
  50.2 0.8 tile.12.centre_ref
  51.0 0.7 bitcast_convert_fusion
  51.8 0.6 copy.24
  52.4 8.1 %all-to-all-done.1 = f32[128,1,640]{2,1,0:T(1,128)S(1)} async-done(((f32[128,1,640]{2,1,0:T(1,128)}), f32[128,1,640]{2,1,0:T(1,128)S(1)}, u32[]{:S(2)}, u32[]{:S(2)}) %all-to-all-start.1) | async-done | bytes 327712 | tf_op jit(solution)/shard_map/all_to_all | solution.py:688
  60.5 0.8 copy-done.5
  61.3 0.8 copy-done.6
  62.1 0.8 copy-done.9
  62.8 0.7 copy-done.11
  63.5 77.0 %shard_map.132 = (f32[640,128]{1,0:T(8,128)S(1)}, f32[16,128]{1,0:T(8,128)S(1)}) custom-call(f32[640,128]{1,0:T(8,128)S(1)} %bitcast.26, s32[64,128]{1,0:T(8,128)S(1)} %copy-done.5, s32[64,128]{1,0:T(8,128)S(1)} %copy-done.9, s32[2,128]{1,0:T(2,128)S(1)} %tile.12.centre_ref, f32[48,256]{1,0:T(8,128)S(1)} %bitcast.30, bf16[24,256]{1,0:T(8,128)(2,1)S(1)} %copy-done.10, ...), custom_call_target="tpu_custom_call" | custom-call | tf_op jit(solution)/shard_map/pallas_call | solution.py:545
  140.5 0.7 copy-done.3
  141.8 4.6 %all-to-all-start.2 = ((f32[128,1,640]{2,1,0:T(1,128)}), f32[128,1,640]{2,1,0:T(1,128)S(1)}, u32[]{:S(2)}, u32[]{:S(2)}) async-start(f32[128,1,640]{2,1,0:T(1,128)} %bitcast.29), calls=%async_computation.2 | async-start | bytes 655360 | tf_op jit(solution)/shard_map/all_to_all | solution.py:688
  146.4 0.6 slice_reduce_fusion
  147.0 11.0 %all-to-all-done.2 = f32[128,1,640]{2,1,0:T(1,128)S(1)} async-done(((f32[128,1,640]{2,1,0:T(1,128)}), f32[128,1,640]{2,1,0:T(1,128)S(1)}, u32[]{:S(2)}, u32[]{:S(2)}) %all-to-all-start.2) | async-done | bytes 327712 | tf_op jit(solution)/shard_map/all_to_all | solution.py:688
  158.0 0.8 copy-done.7
  158.8 11.6 %shard_map.133 = (f32[59,4096]{1,0:T(8,128)}, f32[59,4096]{1,0:T(8,128)}, f32[59,4096]{1,0:T(8,128)}) custom-call(f32[640,128]{1,0:T(8,128)S(1)} %bitcast.25, s32[128,128]{1,0:T(8,128)S(1)} %bitcast.28, f32[59,4096]{1,0:T(8,128)S(1)} %copy-done, f32[59,4096]{1,0:T(8,128)S(1)} %copy-done.1, f32[59,4096]{1,0:T(8,128)S(1)} %copy-done.2, f32[64,128]{1,0:T(8,128)S(1)} %copy-done.7), custom_call_target="tpu_custom_call" | custom-call | tf_op jit(solution)/shard_map/pallas_call | solution.py:666
  (33 shorter events, 2.7 us)
Async XLA Ops:
  0.6 0.7 copy-start.15
  0.6 0.8 copy-start.14
  0.7 26.6 %copy-start = (f32[59,4096]{1,0:T(8,128)S(1)}, f32[59,4096]{1,0:T(8,128)}, u32[]{:S(2)}) copy-start(f32[59,4096]{1,0:T(8,128)} %params_ref.3) | copy-start | bytes 2899972
  2.0 5.9 %copy-start.4 = (s32[64,128]{1,0:T(8,128)}, s32[64,128]{1,0:T(8,128)S(1)}, u32[]{:S(2)}) copy-start(s32[64,128]{1,0:T(8,128)S(1)} %reshape.54.keys_ref) | copy-start | bytes 98308
  15.1 0.6 copy-start.8
  15.8 20.9 %all-to-all-start = ((s32[128,1,128]{2,1,0:T(1,128)}), s32[128,1,128]{2,1,0:T(1,128)S(1)}, u32[]{:S(2)}, u32[]{:S(2)}) async-start(s32[128,1,128]{2,1,0:T(1,128)} %bitcast.5), calls=%async_computation | async-start | bytes 131072 | tf_op jit(solution)/shard_map/all_to_all | solution.py:688
  27.3 33.2 %copy-start.10 = (bf16[24,256]{1,0:T(8,128)(2,1)S(1)}, bf16[24,256]{1,0:T(8,128)(2,1)}, u32[]{:S(2)}) copy-start(bf16[24,256]{1,0:T(8,128)(2,1)} %constant.8.clone.basis_ref) | copy-start | bytes 36868
  36.7 121.4 %copy-start.2 = (f32[59,4096]{1,0:T(8,128)S(1)}, f32[59,4096]{1,0:T(8,128)}, u32[]{:S(2)}) copy-start(f32[59,4096]{1,0:T(8,128)} %two_ref.1) | copy-start | bytes 2899972
  44.3 113.8 %copy-start.1 = (f32[59,4096]{1,0:T(8,128)S(1)}, f32[59,4096]{1,0:T(8,128)}, u32[]{:S(2)}) copy-start(f32[59,4096]{1,0:T(8,128)} %one_ref.1) | copy-start | bytes 2899972
  44.3 16.2 %all-to-all-start.1 = ((f32[128,1,640]{2,1,0:T(1,128)}), f32[128,1,640]{2,1,0:T(1,128)S(1)}, u32[]{:S(2)}, u32[]{:S(2)}) async-start(f32[128,1,640]{2,1,0:T(1,128)} %bitcast.7), calls=%async_computation.1 | async-start | bytes 655360 | tf_op jit(solution)/shard_map/all_to_all | solution.py:688
  60.5 0.8 copy-start.5
  61.3 0.8 copy-start.6
  62.1 0.8 copy-start.9
  62.8 0.7 copy-start.11
  140.5 0.7 copy-start.3
  141.2 0.6 copy-start.12
  141.8 4.6 %copy-start.13 = (f32[16,128]{1,0:T(8,128)S(1)}, f32[16,128]{1,0:T(8,128)}, u32[]{:S(2)}) copy-start(f32[16,128]{1,0:T(8,128)} %copy-done.12) | copy-start | bytes 24580
  141.8 16.2 %all-to-all-start.2 = ((f32[128,1,640]{2,1,0:T(1,128)}), f32[128,1,640]{2,1,0:T(1,128)S(1)}, u32[]{:S(2)}, u32[]{:S(2)}) async-start(f32[128,1,640]{2,1,0:T(1,128)} %bitcast.29), calls=%async_computation.2 | async-start | bytes 655360 | tf_op jit(solution)/shard_map/all_to_all | solution.py:688
  158.0 0.8 copy-start.7

commit v2 on v1

--- a/solution.py
+++ b/solution.py
@@ -41,6 +41,13 @@
 F32 = jnp.float32
 BF16 = jnp.bfloat16
 VMEM = pl.BlockSpec(memory_space=pltpu.VMEM)
+FU = 4
+BU = 4
+PU = 8
+GU = 4
+SU = 8
+MROWS = 1024
+MU = 1
 
 
 def harmonics(dir_x, dir_y, dir_z):
@@ -161,88 +168,129 @@
             ]
 
 
-def plan_kernel(sorted_ref, keys_ref, request_ref, rank_ref, owner_s, rank_s, first_s, local_s):
+def pair(ref, index):
+    return jnp.concatenate(
+        [ref[pl.ds(2 * index, 1), :], ref[pl.ds(2 * index + 1, 1), :]], axis=1
+    )
+
+
+def plan_kernel(sorted_ref, request_ref, table_ref, owner_s, rank_s, local_s):
     keys = sorted_ref[...]
     lane = iota((64, 128), 1)
-    before = pltpu.roll(keys, 1, 1)
-    before = jnp.where(lane == 0, pltpu.roll(before, 1, 0), before)
-    position = iota((64, 128), 0) * 128 + lane
-    fresh = ((keys != before) | (position == 0)) & (keys < SENTINEL)
-    fresh_f = jnp.where(fresh, 1.0, 0.0).astype(F32)
-    fresh_h = fresh_f.astype(BF16)
+    line = iota((64, 128), 0)
+
+    def earlier(value):
+        shifted = pltpu.roll(value, 1, 1)
+        return jnp.where(lane == 0, pltpu.roll(shifted, 1, 0), shifted)
+
+    first_slot = (lane == 0) & (line == 0)
+    before = earlier(keys)
+    fresh = ((keys != before) | first_slot) & (keys < SENTINEL)
+    fresh_h = jnp.where(fresh, 1.0, 0.0).astype(BF16)
     upto = jnp.where(iota((128, 128), 0) <= iota((128, 128), 1), 1.0, 0.0).astype(BF16)
     ones = jnp.ones((128, 128), BF16)
     lower = jnp.where(iota((64, 64), 1) < iota((64, 64), 0), 1.0, 0.0).astype(BF16)
-    within = dot_nn(fresh_h, upto)
     totals = dot_nn(fresh_h, ones).astype(BF16)
-    count = within + dot_nn(lower, totals)
+    count = (dot_nn(fresh_h, upto) + dot_nn(lower, totals)).astype(jnp.int32) - 1
     owner = keys >> 12
+    opens = (owner != (before >> 12)) | first_slot
+    base = jnp.where(opens, count, 0)
+    for step in (1, 2, 4, 8, 16, 32, 64):
+        base = jnp.maximum(base, jnp.where(lane >= step, pltpu.roll(base, step, 1), 0))
+    above = jnp.broadcast_to(jnp.max(base, axis=1, keepdims=True), (64, 128))
+    above = jnp.where(line >= 1, pltpu.roll(above, 1, 0), 0)
+    for step in (1, 2, 4, 8, 16, 32):
+        above = jnp.maximum(above, jnp.where(line >= step, pltpu.roll(above, step, 0), 0))
+    rank = count - jnp.maximum(base, above)
     owner_s[...] = owner
-    first_s[...] = fresh_f
+    rank_s[...] = jnp.where(fresh, rank, -1)
     local_s[...] = keys & (G_DEV - 1)
 
-    def pair(ref, index):
-        return jnp.concatenate(
-            [ref[pl.ds(2 * index, 1), :], ref[pl.ds(2 * index + 1, 1), :]], axis=1
-        )
-
-    def smaller(index, total):
-        owners = pair(owner_s, index)
-        is_less = jnp.where(owners < iota((128, 256), 0), 1.0, 0.0).astype(BF16)
-        firsts = jnp.broadcast_to(pair(first_s, index), (8, 256)).astype(BF16)
-        return total + dot_nt(firsts, is_less)
-
-    first_of = lax.fori_loop(0, 32, smaller, jnp.zeros((8, 128), F32), unroll=4)
-    offsets = jnp.broadcast_to(first_of[0:1], (64, 128)).astype(jnp.int32)
-    offset = jnp.take_along_axis(offsets, owner & 127, axis=1, mode="promise_in_bounds")
-    rank_s[...] = count.astype(jnp.int32) - 1 - offset
-
     def fill(index, total):
-        owners = pair(owner_s, index)
-        ranks = pair(rank_s, index)
-        firsts = pair(first_s, index) > 0.0
         local = pair(local_s, index)
-        match = (ranks == iota((64, 256), 0)) & firsts
-        high = jnp.where(match, (local >> 6).astype(F32), 0.0).astype(BF16)
-        low = jnp.where(match, (local & 63).astype(F32), 0.0).astype(BF16)
-        used = jnp.where(match, 1.0, 0.0).astype(BF16)
-        parts = jnp.concatenate([high, low, used], axis=0)
-        return total + dot_nt(parts, one_hot(owners, 128))
-
-    filled = lax.fori_loop(0, 32, fill, jnp.zeros((192, 128), F32), unroll=2)
+        match = pair(rank_s, index) == iota((64, 256), 0)
+        high = jnp.where(match, (local >> 6).astype(F32), 0.0)
+        low = jnp.where(match, (local & 63).astype(F32), 0.0)
+        parts = jnp.concatenate([high, low], axis=0).astype(BF16)
+        return total + dot_nt(parts, one_hot(pair(owner_s, index), 128))
+
+    filled = lax.fori_loop(0, 32, fill, jnp.zeros((128, 128), F32), unroll=PU)
     locals_of = (filled[0:64] * 64.0 + filled[64:128]).astype(jnp.int32)
-    table = jnp.where(filled[128:192] > 0.5, locals_of, -1)
+    table_ref[...] = locals_of
     padded = jnp.concatenate([locals_of, jnp.zeros((64, 128), jnp.int32)], axis=0)
     request_ref[...] = jnp.transpose(padded)
 
-    slots = keys_ref[...]
-    slot_owner = (slots >> 12) & 127
-    slot_local = slots & (G_DEV - 1)
-    rank = jnp.zeros((64, 128), jnp.int32)
-    for place in range(64):
-        row = jnp.broadcast_to(table[place : place + 1], (64, 128))
-        found = jnp.take_along_axis(row, slot_owner, axis=1, mode="promise_in_bounds")
-        rank = jnp.where(found == slot_local, place, rank)
-    rank_ref[...] = rank
-
-
-def plan(keys_sorted, keys):
+
+def plan(keys_sorted):
     return pl.pallas_call(
         plan_kernel,
         out_shape=(
             jax.ShapeDtypeStruct((128, 128), jnp.int32),
             jax.ShapeDtypeStruct((64, 128), jnp.int32),
         ),
-        in_specs=[VMEM, VMEM],
+        in_specs=[VMEM],
         out_specs=(VMEM, VMEM),
-        scratch_shapes=[
-            pltpu.VMEM((64, 128), jnp.int32),
-            pltpu.VMEM((64, 128), jnp.int32),
-            pltpu.VMEM((64, 128), F32),
-            pltpu.VMEM((64, 128), jnp.int32),
-        ],
+        scratch_shapes=[pltpu.VMEM((64, 128), jnp.int32)] * 3,
         compiler_params=pltpu.CompilerParams(vmem_limit_bytes=32 * 1024 * 1024),
-    )(keys_sorted, keys)
+    )(keys_sorted)
+
+
+def find_kernel(table_ref, keys_ref, centre_ref, slots_ref):
+    keys = keys_ref[...]
+    owner = (keys >> 12) & 127
+    local = keys & (G_DEV - 1)
+    rank = jnp.zeros((64, 128), jnp.int32)
+    for place in range(63, -1, -1):
+        row = jnp.broadcast_to(table_ref[place : place + 1, :], (64, 128))
+        found = jnp.take_along_axis(row, owner, axis=1, mode="promise_in_bounds")
+        rank = jnp.where(found == local, place, rank)
+    tile = jnp.where(
+        iota((64, 128), 0) < 32,
+        jnp.broadcast_to(centre_ref[0:1, :], (64, 128)),
+        jnp.broadcast_to(centre_ref[1:2, :], (64, 128)),
+    )
+    slots_ref[0:64, :] = (rank >> 5) * 128 + owner
+    slots_ref[64:128, :] = rank & 31
+    slots_ref[128:192, :] = jnp.where(keys < SENTINEL, tile, -1)
+
+
+def find(table, keys, centre):
+    return pl.pallas_call(
+        find_kernel,
+        out_shape=jax.ShapeDtypeStruct((192, 128), jnp.int32),
+        in_specs=[VMEM] * 3,
+        out_specs=VMEM,
+        compiler_params=pltpu.CompilerParams(vmem_limit_bytes=32 * 1024 * 1024),
+    )(table, keys, centre)
+
+
+def gather_all(table_ref, high_ref, low_ref, out_ref, size):
+    def step(index, carry):
+        lanes = one_hot(pair(high_ref, index), 256)
+        match = pair(low_ref, index) == iota((size, 256), 0)
+        found = dot_nn(table_ref[...], lanes)
+        for feature in range(9):
+            parts = [
+                found[(9 * part + feature) * size : (9 * part + feature + 1) * size]
+                for part in range(3)
+            ]
+            picked = jnp.where(match, (parts[0] + parts[1]) + parts[2], 0.0)
+            line = jnp.sum(picked, axis=0, keepdims=True)
+            out_ref[pl.ds(64 * feature + 2 * index, 1), :] = line[:, 0:128]
+            out_ref[pl.ds(64 * feature + 2 * index + 1, 1), :] = line[:, 128:256]
+        return carry
+
+    lax.fori_loop(0, 32, step, 0, unroll=GU)
+
+
+def three_parts(value, table_ref, feature, size):
+    high = value.astype(BF16)
+    rest = value - high.astype(F32)
+    middle = rest.astype(BF16)
+    low = (rest - middle.astype(F32)).astype(BF16)
+    for part, piece in enumerate((high, middle, low)):
+        base = (9 * part + feature) * size
+        table_ref[base : base + size, :] = piece
 
 
 def project_kernel(params_ref, feats_ref, rows_s):
@@ -275,19 +323,14 @@
     )(params)
 
 
-def serve_kernel(feats_ref, wanted_ref, out_ref, place_s):
+def serve_kernel(feats_ref, wanted_ref, out_ref, place_s, table_s, high_s, low_s):
     wanted = jnp.transpose(wanted_ref[...])[0:64]
-    high = wanted >> 7
-    low = wanted & 127
+    high_s[...] = (wanted >> 11) * 128 + (wanted & 127)
+    low_s[...] = (wanted >> 7) & 15
     for feature in range(9):
-        total = jnp.zeros((64, 128), F32)
-        for piece in range(32):
-            row = jnp.broadcast_to(
-                feats_ref[feature * 32 + piece : feature * 32 + piece + 1, :], (64, 128)
-            )
-            found = jnp.take_along_axis(row, low, axis=1, mode="promise_in_bounds")
-            total = jnp.where(high == piece, found, total)
-        place_s[feature * 64 : (feature + 1) * 64, :] = total
+        rows = feats_ref[feature * 32 : (feature + 1) * 32, :]
+        three_parts(jnp.concatenate([rows[0:16], rows[16:32]], axis=1), table_s, feature, 16)
+    gather_all(table_s, high_s, low_s, place_s, 16)
     place_s[576:640, :] = jnp.zeros((64, 128), F32)
     for part in range(5):
         out_ref[pl.ds(part, 128, stride=5), :] = jnp.transpose(
@@ -301,64 +344,70 @@
         out_shape=jax.ShapeDtypeStruct((640, 128), F32),
         in_specs=[VMEM, VMEM],
         out_specs=VMEM,
-        scratch_shapes=[pltpu.VMEM((640, 128), F32)],
+        scratch_shapes=[
+            pltpu.VMEM((640, 128), F32),
+            pltpu.VMEM((27 * 16, 256), BF16),
+            pltpu.VMEM((64, 128), jnp.int32),
+            pltpu.VMEM((64, 128), jnp.int32),
+        ],
         compiler_params=pltpu.CompilerParams(vmem_limit_bytes=32 * 1024 * 1024),
     )(feats, wanted)
 
 
 def pixel_basis():
-    pixel = np.arange(256)
-    across = (pixel % 16) - 7.5
-    down = (pixel // 16) - 7.5
-    six = np.stack([across * across, across * down, down * down, across, down, np.ones(256)])
-    basis = np.zeros((24, 256), np.float32)
-    basis[0:18] = np.tile(six, (3, 1))
-    moments = np.zeros((16, 256), np.float32)
-    moments[0:6] = six
-    return (jnp.asarray(basis, BF16), jnp.asarray(moments, BF16))
+    pixel = iota((24, 256), 1)
+    across = (pixel & 15).astype(F32) - 7.5
+    down = (pixel >> 4).astype(F32) - 7.5
+    kind = iota((24, 256), 0)
+    kind = jnp.where(kind >= 12, kind - 12, jnp.where(kind >= 6, kind - 6, kind))
+    return select_monomial(kind, across, down)
+
+
+def select_monomial(kind, across, down):
+    value = jnp.where(kind == 0, across * across, 0.0)
+    value = jnp.where(kind == 1, across * down, value)
+    value = jnp.where(kind == 2, down * down, value)
+    value = jnp.where(kind == 3, across, value)
+    value = jnp.where(kind == 4, down, value)
+    return jnp.where(kind == 5, 1.0, value).astype(BF16)
 
 
 def render_kernel(
     arrived_ref,
-    keys_ref,
-    rank_ref,
-    centre_ref,
+    slots_ref,
     target_ref,
-    basis_ref,
-    moment_ref,
     out_ref,
     loss_ref,
+    places_s,
     table_s,
     coef_s,
     alpha_s,
     weight_s,
     sums_s,
     grads_s,
+    weights_s,
+    parts_s,
 ):
     for part in range(5):
         table_s[part * 128 : (part + 1) * 128, :] = jnp.transpose(
             arrived_ref[pl.ds(part, 128, stride=5), :]
         )
-    keys = keys_ref[...]
-    rank = rank_ref[...]
-    live = keys < SENTINEL
-    owner = (keys >> 12) & 127
-    feats = []
     for feature in range(9):
-        total = jnp.zeros((64, 128), F32)
-        for place in range(64):
-            row = jnp.broadcast_to(
-                table_s[feature * 64 + place : feature * 64 + place + 1, :], (64, 128)
-            )
-            found = jnp.take_along_axis(row, owner, axis=1, mode="promise_in_bounds")
-            total = jnp.where(rank == place, found, total)
-        feats.append(total)
-    half = iota((64, 128), 0) < 32
-    tile = jnp.where(
-        half,
-        jnp.broadcast_to(centre_ref[0:1, :], (64, 128)),
-        jnp.broadcast_to(centre_ref[1:2, :], (64, 128)),
-    )
+        base = feature * 64
+        three_parts(
+            jnp.concatenate(
+                [table_s[base : base + 32, :], table_s[base + 32 : base + 64, :]], axis=1
+            ),
+            places_s,
+            feature,
+            32,
+        )
+    gather_all(
+        places_s, slots_ref.at[pl.ds(0, 64), :], slots_ref.at[pl.ds(64, 64), :], table_s, 32
+    )
+    feats = [table_s[feature * 64 : (feature + 1) * 64, :] for feature in range(9)]
+    tile = slots_ref[128:192, :]
+    live = tile >= 0
     rel_u = feats[0] - ((tile & (TILES_X - 1)).astype(F32) * 16.0 + 7.5)
     rel_v = feats[1] - ((tile >> 6).astype(F32) * 16.0 + 7.5)
     conic_1, conic_2, conic_3 = (feats[2], feats[3], feats[4])
@@ -390,14 +439,33 @@
         coef_s[pl.ds(18 + channel, 64, stride=24), :] = high
         coef_s[pl.ds(21 + channel, 64, stride=24), :] = value - high
 
-    diagonal = (iota((8, 128), 1) & 7) == iota((8, 128), 0)
+    def chunk_rows(group, index):
+        return pl.ds(pl.multiple_of(group * 4096 + index * 256, 256), 256)
+
+    def coef_of(group, index):
+        base = group * 32 + index * 2
+        return jnp.concatenate(
+            [
+                coef_s[pl.ds(pl.multiple_of((base + half) * 24, 8), 24), :]
+                for half in range(2)
+            ],
+            axis=1,
+        )
+
+    basis = pixel_basis()
+    pixel = iota((256, 128), 0)
+    moments = select_monomial(
+        iota((256, 128), 1), (pixel & 15).astype(F32) - 7.5, (pixel >> 4).astype(F32) - 7.5
+    )
+
+    diagonal = (iota((8, 256), 1) & 7) == iota((8, 256), 0)
 
     def spread(coef, base):
         return jnp.concatenate(
             [
                 jnp.where(
                     diagonal,
-                    jnp.broadcast_to(coef[base + channel : base + channel + 1], (8, 128)),
+                    jnp.broadcast_to(coef[base + channel : base + channel + 1], (8, 256)),
                     0.0,
                 )
                 for channel in range(3)
@@ -405,76 +473,107 @@
             axis=0,
         )
 
-    for group in range(2):
-
-        def forward(index, state):
-            left, colors = state
-            chunk = group * 32 + index
-            coef = coef_s[pl.ds(pl.multiple_of(chunk * 24, 8), 24), :]
-            powers = dot_nn(jnp.transpose(coef).astype(BF16), basis_ref[...])
-            alpha = jnp.exp2(powers)
-            rows = pl.ds(pl.multiple_of(index * 128, 128), 128)
+    def forward(index, state):
+        results = []
+        for group in range(2):
+            left, colors = state[2 * group : 2 * group + 2]
+            coef = coef_of(group, index)
+            alpha = jnp.exp2(dot_nn(jnp.transpose(coef).astype(BF16), basis))
+            rows = chunk_rows(group, index)
             alpha_s[rows, :] = alpha
             parts = []
-            for slot in range(16):
+            for slot in range(32):
                 weight = alpha[slot * 8 : (slot + 1) * 8] * left
                 left = left - weight
                 parts.append(weight)
             weights = jnp.concatenate(parts, axis=0)
             weight_s[rows, :] = weights
             high, low = split(weights)
-            col_high = spread(coef, 18).astype(BF16)
-            col_low = spread(coef, 21).astype(BF16)
-            colors = (
-                colors
-                + dot_nn(col_high, high)
-                + dot_nn(col_low, high)
-                + dot_nn(col_high, low)
-            )
-            return (left, colors)
-
-        left, colors = lax.fori_loop(
-            0, 32, forward, (jnp.ones((8, 256), F32), jnp.zeros((24, 256), F32))
-        )
-        errors = colors - target_ref[group * 24 : (group + 1) * 24, :]
+            parts_s[rows, 512:768] = high
+            parts_s[rows, 768:1024] = low
+            col_high = spread(coef, 18)
+            col_low = spread(coef, 21)
+            both = dot_nn(jnp.concatenate([col_high, col_low], axis=0).astype(BF16), high)
+            colors = colors + both[0:24] + both[24:48] + dot_nn(col_high.astype(BF16), low)
+            results += [left, colors]
+        return tuple(results)
+
+    start = (jnp.ones((8, 256), F32), jnp.zeros((24, 256), F32))
+    state = lax.fori_loop(0, 16, forward, start + start, unroll=FU)
+    err_all = []
+    for group in range(2):
+        errors = state[2 * group + 1] - target_ref[group * 24 : (group + 1) * 24, :]
         squares = errors * errors
         total = jnp.sum(squares[0:8] + squares[8:16] + squares[16:24], axis=1, keepdims=True)
         loss_ref[group * 8 : (group + 1) * 8, :] = jnp.broadcast_to(total / 16.0, (8, 128))
-        err = errors * 0.125
-        err_high, err_low = split(err)
-        err_three = jnp.concatenate([err_high, err_low, err_high], axis=0)
-
-        def backward(step, behind):
-            index = 31 - step
-            chunk = group * 32 + index
-            coef = coef_s[pl.ds(pl.multiple_of(chunk * 24, 8), 24), :]
+        err_high, err_low = split(errors * 0.125)
+        err_all.append(jnp.concatenate([err_high, err_low, err_high], axis=0))
+        turned = jnp.transpose(
+            jnp.concatenate(
+                [jnp.zeros((8, 256), F32), err_high.astype(F32), err_low.astype(F32)]
+                + [jnp.zeros((72, 256), F32)],
+                axis=0,
+            )
+        )
+        lane = iota((256, 128), 1)
+        weights_s[group, 0:256, :] = moments
+        weights_s[group, 256:512, :] = moments
+        weights_s[group, 512:768, :] = turned.astype(BF16)
+        weights_s[group, 768:1024, :] = jnp.where(lane < 32, turned, 0.0).astype(BF16)
+
+    def backward(step, state):
+        index = 15 - step
+        results = []
+        for group in range(2):
+            behind = state[group]
+            err_three = err_all[group]
+            coef = coef_of(group, index)
             col_high = spread(coef, 18)
             col_low = spread(coef, 21)
             col_three = jnp.concatenate([col_high, col_high, col_low], axis=0)
             shades = dot_nn(jnp.transpose(col_three).astype(BF16), err_three)
-            rows = pl.ds(pl.multiple_of(index * 128, 128), 128)
+            rows = chunk_rows(group, index)
             alpha = alpha_s[rows, :]
             weights = weight_s[rows, :]
             parts = []
-            for slot in range(15, -1, -1):
+            for slot in range(31, -1, -1):
                 cut = slice(slot * 8, (slot + 1) * 8)
                 gap = shades[cut] - behind
                 parts.append(weights[cut] * gap)
                 behind = behind + alpha[cut] * gap
             pulls = jnp.concatenate(parts[::-1], axis=0)
             pull_high, pull_low = split(pulls)
-            sums = dot_nt(moment_ref[...], pull_high) + dot_nt(moment_ref[...], pull_low)
-            high, low = split(weights)
-            tints = dot_nt(err_high, high) + dot_nt(err_low, high) + dot_nt(err_high, low)
-            sums_s[pl.ds(pl.multiple_of(chunk * 16, 8), 8), :] = sums[0:8]
-            for channel in range(3):
-                own = jnp.where(diagonal, tints[channel * 8 : (channel + 1) * 8], 0.0)
-                sums_s[pl.ds(chunk * 16 + 8 + channel, 1), :] = jnp.sum(
-                    own, axis=0, keepdims=True
-                )
-            return behind
-
-        lax.fori_loop(0, 32, backward, jnp.zeros((8, 256), F32))
+            parts_s[rows, 0:256] = pull_high
+            parts_s[rows, 256:512] = pull_low
+            results.append(behind)
+        return tuple(results)
+
+    zero = jnp.zeros((8, 256), F32)
+    lax.fori_loop(0, 16, backward, (zero, zero), unroll=BU)
+
+    for group in range(2):
+
+        def reduce_pixels(index, carry):
+            rows = pl.ds(pl.multiple_of(group * 4096 + index * MROWS, MROWS), MROWS)
+            sums = dot_nn(parts_s[rows, :], weights_s[group])
+            for part in range(MROWS // 128):
+                turned = jnp.transpose(sums[part * 128 : (part + 1) * 128])
+                base = (group * 32 + index * (MROWS // 128) + part) * 16
+                tints = turned[8:32] + turned[32:56]
+                own = [
+                    jnp.sum(
+                        jnp.where(diagonal[:, 0:128], tints[ch * 8 : (ch + 1) * 8], 0.0),
+                        axis=0,
+                        keepdims=True,
+                    )
+                    for ch in range(3)
+                ]
+                sums_s[pl.ds(pl.multiple_of(base, 8), 8), :] = turned[0:8]
+                for channel in range(3):
+                    sums_s[pl.ds(base + 8 + channel, 1), :] = own[channel]
+            return carry
+
+        lax.fori_loop(0, 4096 // MROWS, reduce_pixels, 0, unroll=MU)
 
     def sums_of(index):
         return sums_s[pl.ds(index, 64, stride=16), :]
@@ -498,23 +597,13 @@
     ]
     for index in range(9):
         grads_s[pl.ds(index, 64, stride=16), :] = jnp.where(live, slot_grads[index], 0.0)
-    grads_s[pl.ds(9, 64, stride=16), :] = ((rank >> 5) * 128 + owner).astype(F32)
-    grads_s[pl.ds(10, 64, stride=16), :] = (rank & 31).astype(F32)
-
-    def gather_rows(index, size, lanes, total):
-        both = jnp.concatenate(
-            [
-                grads_s[pl.ds(pl.multiple_of(index * 32, 8), 16), :],
-                grads_s[pl.ds(pl.multiple_of(index * 32 + 16, 8), 16), :],
-            ],
-            axis=1,
-        )
-        return scatter_step(both, size, total)
+    grads_s[pl.ds(9, 64, stride=16), :] = slots_ref[0:64, :].astype(F32)
+    grads_s[pl.ds(10, 64, stride=16), :] = slots_ref[64:128, :].astype(F32)
 
     def scatter(index, total):
-        return gather_rows(index, 32, 256, total)
-
-    collected = lax.fori_loop(0, 32, scatter, jnp.zeros((288, 256), F32))
+        return scatter_step(two_rows(grads_s, index), 32, total)
+
+    collected = lax.fori_loop(0, 32, scatter, jnp.zeros((288, 256), F32), unroll=SU)
     for feature in range(9):
         piece = collected[feature * 32 : (feature + 1) * 32]
         table_s[feature * 64 : feature * 64 + 32, :] = piece[:, 0:128]
@@ -524,6 +613,16 @@
         out_ref[pl.ds(part, 128, stride=5), :] = jnp.transpose(
             table_s[part * 128 : (part + 1) * 128, :]
         )
+
+
+def two_rows(ref, index):
+    return jnp.concatenate(
+        [
+            ref[pl.ds(pl.multiple_of(index * 32, 16), 16), :],
+            ref[pl.ds(pl.multiple_of(index * 32 + 16, 16), 16), :],
+        ],
+        axis=1,
+    )
 
 
 def scatter_step(both, size, total):
@@ -540,26 +639,28 @@
     return total + found[0 : 9 * size] + found[9 * size : 18 * size]
 
 
-def render(arrived, keys, rank, centre, target):
-    basis, moments = pixel_basis()
+def render(arrived, slots, target):
     return pl.pallas_call(
         render_kernel,
         out_shape=(
             jax.ShapeDtypeStruct((640, 128), F32),
             jax.ShapeDtypeStruct((16, 128), F32),
         ),
-        in_specs=[VMEM] * 7,
+        in_specs=[VMEM] * 3,
         out_specs=(VMEM, VMEM),
         scratch_shapes=[
+            pltpu.VMEM((27 * 32, 256), BF16),
             pltpu.VMEM((640, 128), F32),
             pltpu.VMEM((64 * 24, 128), F32),
-            pltpu.VMEM((4096, 256), F32),
-            pltpu.VMEM((4096, 256), F32),
+            pltpu.VMEM((8192, 256), F32),
+            pltpu.VMEM((8192, 256), F32),
             pltpu.VMEM((64 * 16, 128), F32),
             pltpu.VMEM((64 * 16, 128), F32),
+            pltpu.VMEM((2, 1024, 128), BF16),
+            pltpu.VMEM((8192, 1024), BF16),
         ],
         compiler_params=pltpu.CompilerParams(vmem_limit_bytes=48 * 1024 * 1024),
-    )(arrived, keys, rank, centre, target, basis, moments)
+    )(arrived, slots, target)
 
 
 def learn_rate(index):
@@ -599,16 +700,9 @@
     table_s[pl.ds(10, 64, stride=16), :] = (piece & 15).astype(F32)
 
     def scatter(index, total):
-        both = jnp.concatenate(
-            [
-                table_s[pl.ds(pl.multiple_of(index * 32, 8), 16), :],
-                table_s[pl.ds(pl.multiple_of(index * 32 + 16, 8), 16), :],
-            ],
-            axis=1,
-        )
-        return scatter_step(both, 16, total)
-
-    collected = lax.fori_loop(0, 32, scatter, jnp.zeros((144, 256), F32))
+        return scatter_step(two_rows(table_s, index), 16, total)
+
+    collected = lax.fori_loop(0, 32, scatter, jnp.zeros((144, 256), F32), unroll=SU)
 
     def grad_of(feature):
         part = collected[feature * 16 : (feature + 1) * 16]
@@ -692,14 +786,15 @@
 def shards(params, moment_one, moment_two, visible, counts, tile_pos, target):
     keys = slot_keys(visible, counts)
     keys_sorted = lax.sort(keys.reshape(-1), is_stable=False).reshape(64, 128)
-    request, rank = plan(keys_sorted, keys)
+    request, table = plan(keys_sorted)
+    wanted = exchange(request)
     feats = project(params)
-    wanted = exchange(request)
-    arrived = exchange(serve(feats, wanted))
     centre = jnp.tile(tile_pos.reshape(2, 8), (1, 16))
+    slots = find(table, keys, centre)
     colours = target.astype(F32).reshape(2, 8, 3, 256)
     colours = jnp.transpose(colours, (0, 2, 1, 3)).reshape(48, 256)
-    grads, loss = render(arrived, keys, rank, centre, colours)
+    arrived = exchange(serve(feats, wanted))
+    grads, loss = render(arrived, slots, colours)
     received = exchange(grads)
     outs = update(received, wanted, params, moment_one, moment_two)
     return (loss[:, 0], *outs)

time: 171 us -> 104 us (0.61)
  Pallas kernels: 104 us -> 38.8 us
  waiting for transfers between devices: 27.7 us -> 22.8 us
  starting transfers between devices: 20.7 us -> 22.8 us
    pallas_call x1, Pallas kernels: 77 us -> 23.3 us  [render(): pl.pallas_call(render_kernel, out_shape=(jax.ShapeDtypeStruct((640, 128),...]
    pallas_call x1, Pallas kernels: 11.6 us -> 5.85 us  [update(): pl.pallas_call(update_kernel, out_shape=(whole, whole, whole), in_specs=[...]
    all_to_all x3, waiting for transfers between devices: 27.7 us -> 22.8 us  [exchange(): flat = lax.all_to_all(flat, 'dev', split_axis=0, concat_axis=0, tiled=True)]
    pallas_call x1, Pallas kernels: 7.33 us -> 3.08 us  [plan(): pl.pallas_call(plan_kernel, out_shape=(jax.ShapeDtypeStruct((128, 128), j...]
    pallas_call x1, Pallas kernels: 7.57 us -> 4.29 us  [serve(): pl.pallas_call(serve_kernel, out_shape=jax.ShapeDtypeStruct((640, 128), F...]
    all_to_all x3, starting transfers between devices: 20.7 us -> 22.8 us  [exchange(): flat = lax.all_to_all(flat, 'dev', split_axis=0, concat_axis=0, tiled=True)]
    reshape x2, local copies, waits for them, and re-layouts: 0.45 us -> 2.16 us  [slot_keys(): return jnp.transpose(keys.reshape(2, 8, 512), (0, 2, 1)).reshape(64, 128)]
    unnamed x33 -> x31, local copies, waits for them, and re-layouts: 6.46 us -> 6.69 us
  transfers between devices with their start and end apart: 3 -> 3, of which waited for: 3 -> 3; matrix products, arithmetic and copies ran while one was open for 2% -> 5% of each run, Pallas kernels for 0% -> 2%
where the time goes in v2:
time: 104 us; the launch traced here: 103 us
  Pallas kernels  38.8 us (37%)
  starting transfers between devices  22.8 us (22%)
  waiting for transfers between devices  22.8 us (22%)
  local copies, waits for them, and re-layouts  11.9 us (11%)
  other arithmetic  6.35 us (6%)
    pallas_call x1, Pallas kernels, render(): pl.pallas_call(render_kernel, out_shape=(jax.ShapeDtypeStruct((640, 128),...  23.3 us
    all_to_all x3, starting transfers between devices, exchange(): flat = lax.all_to_all(flat, 'dev', split_axis=0, concat_axis=0, tiled=True)  22.8 us
    all_to_all x3, waiting for transfers between devices, exchange(): flat = lax.all_to_all(flat, 'dev', split_axis=0, concat_axis=0, tiled=True)  22.8 us
    unnamed x31, local copies, waits for them, and re-layouts  6.69 us
    pallas_call x1, Pallas kernels, update(): pl.pallas_call(update_kernel, out_shape=(whole, whole, whole), in_specs=[...  5.85 us
    sort x1, other arithmetic, shards(): keys_sorted = lax.sort(keys.reshape(-1), is_stable=False).reshape(64, 128)  5.59 us
    pallas_call x1, Pallas kernels, serve(): pl.pallas_call(serve_kernel, out_shape=jax.ShapeDtypeStruct((640, 128), F...  4.29 us
    pallas_call x1, Pallas kernels, plan(): pl.pallas_call(plan_kernel, out_shape=(jax.ShapeDtypeStruct((128, 128), j...  3.08 us
  transfers between devices with their start and end apart: 3, of which 3 were waited for; matrix products, arithmetic and copies ran while one was open for 5% of the time, Pallas kernels for 2%

profile of v2, /device:TPU:1, one launch (start us, length us, event | category | flops | bytes accessed | tf_op | source)
XLA Modules:
  0.0 103.4 jit_solution(18423626449139149604)
XLA Ops:
  0.7 0.6 copy-done.13
  2.0 5.6 %sort.7 = s32[8192]{0:T(1024)S(1)} sort(s32[8192]{0:T(1024)S(1)} %reshape_reshape.3), dimensions={0}, to_apply=%region_0.1 | sort | flops 106496 | bytes 65536 | tf_op jit(solution)/shard_map/sort | solution.py:788
  7.6 3.1 %shard_map.112 = (s32[128,128]{1,0:T(8,128)}, s32[64,128]{1,0:T(8,128)S(1)}) custom-call(s32[64,128]{1,0:T(8,128)S(1)} %bitcast.31), custom_call_target="tpu_custom_call" | custom-call | tf_op jit(solution)/shard_map/pallas_call | solution.py:225
  11.3 11.5 %all-to-all-start = ((s32[128,1,128]{2,1,0:T(1,128)}), s32[128,1,128]{2,1,0:T(1,128)S(1)}, u32[]{:S(2)}, u32[]{:S(2)}) async-start(s32[128,1,128]{2,1,0:T(1,128)} %bitcast.5), calls=%async_computation | async-start | bytes 131072 | tf_op jit(solution)/shard_map/all_to_all | solution.py:782
  22.8 0.7 shard_map.111.feats_ref
  23.5 8.7 %all-to-all-done = s32[128,1,128]{2,1,0:T(1,128)S(1)} async-done(((s32[128,1,128]{2,1,0:T(1,128)}), s32[128,1,128]{2,1,0:T(1,128)S(1)}, u32[]{:S(2)}, u32[]{:S(2)}) %all-to-all-start) | async-done | bytes 65568 | tf_op jit(solution)/shard_map/all_to_all | solution.py:782
  32.2 4.3 %shard_map.113 = f32[640,128]{1,0:T(8,128)} custom-call(f32[288,128]{1,0:T(8,128)S(1)} %shard_map.111.feats_ref, s32[128,128]{1,0:T(8,128)S(1)} %bitcast.27), custom_call_target="tpu_custom_call" | custom-call | tf_op jit(solution)/shard_map/pallas_call | solution.py:342
  36.5 4.6 %all-to-all-start.1 = ((f32[128,1,640]{2,1,0:T(1,128)}), f32[128,1,640]{2,1,0:T(1,128)S(1)}, u32[]{:S(2)}, u32[]{:S(2)}) async-start(f32[128,1,640]{2,1,0:T(1,128)} %bitcast.7), calls=%async_computation.1 | async-start | bytes 655360 | tf_op jit(solution)/shard_map/all_to_all | solution.py:782
  41.1 2.0 %reshape.58.keys_ref = s32[64,128]{1,0:T(8,128)} reshape(s32[2,512,8]{2,1,0:T(8,128)} %bitcast.33) | data formatting | bytes 65536 | tf_op jit(solution)/shard_map/reshape | solution.py:777
  43.8 0.8 tile.12.centre_ref
  44.6 0.7 bitcast_convert_fusion
  45.9 0.8 copy-done.7
  46.7 0.8 copy-done.10
  47.5 1.5 %shard_map.114.slots_ref = s32[192,128]{1,0:T(8,128)S(1)} custom-call(s32[64,128]{1,0:T(8,128)S(1)} %copy-done.10, s32[64,128]{1,0:T(8,128)S(1)} %copy-done.7, s32[2,128]{1,0:T(2,128)S(1)} %tile.12.centre_ref), custom_call_target="tpu_custom_call" | custom-call | tf_op jit(solution)/shard_map/pallas_call | solution.py:258
  49.0 0.6 copy-done.3
  49.6 3.1 %all-to-all-done.1 = f32[128,1,640]{2,1,0:T(1,128)S(1)} async-done(((f32[128,1,640]{2,1,0:T(1,128)}), f32[128,1,640]{2,1,0:T(1,128)S(1)}, u32[]{:S(2)}, u32[]{:S(2)}) %all-to-all-start.1) | async-done | bytes 327712 | tf_op jit(solution)/shard_map/all_to_all | solution.py:782
  52.7 0.9 copy-done.4
  53.6 0.8 copy-done.6
  54.4 23.3 %shard_map.115 = (f32[640,128]{1,0:T(8,128)S(1)}, f32[16,128]{1,0:T(8,128)S(1)}) custom-call(f32[640,128]{1,0:T(8,128)S(1)} %bitcast.26, s32[192,128]{1,0:T(8,128)S(1)} %copy-done.4, f32[48,256]{1,0:T(8,128)S(1)} %bitcast.30), custom_call_target="tpu_custom_call" | custom-call | tf_op jit(solution)/shard_map/pallas_call | solution.py:643
  77.7 0.7 copy-done.5
  78.5 6.7 %all-to-all-start.2 = ((f32[128,1,640]{2,1,0:T(1,128)}), f32[128,1,640]{2,1,0:T(1,128)S(1)}, u32[]{:S(2)}, u32[]{:S(2)}) async-start(f32[128,1,640]{2,1,0:T(1,128)} %bitcast.29), calls=%async_computation.2 | async-start | bytes 655360 | tf_op jit(solution)/shard_map/all_to_all | solution.py:782
  85.8 11.0 %all-to-all-done.2 = f32[128,1,640]{2,1,0:T(1,128)S(1)} async-done(((f32[128,1,640]{2,1,0:T(1,128)}), f32[128,1,640]{2,1,0:T(1,128)S(1)}, u32[]{:S(2)}, u32[]{:S(2)}) %all-to-all-start.2) | async-done | bytes 327712 | tf_op jit(solution)/shard_map/all_to_all | solution.py:782
  96.8 0.8 copy-done.8
  97.5 5.9 %shard_map.116 = (f32[59,4096]{1,0:T(8,128)}, f32[59,4096]{1,0:T(8,128)}, f32[59,4096]{1,0:T(8,128)}) custom-call(f32[640,128]{1,0:T(8,128)S(1)} %bitcast.25, s32[128,128]{1,0:T(8,128)S(1)} %bitcast.28, f32[59,4096]{1,0:T(8,128)S(1)} %copy-done, f32[59,4096]{1,0:T(8,128)S(1)} %copy-done.1, f32[59,4096]{1,0:T(8,128)S(1)} %copy-done.2, f32[64,128]{1,0:T(8,128)S(1)} %copy-done.8), custom_call_target="tpu_custom_call" | custom-call | tf_op jit(solution)/shard_map/pallas_call | solution.py:760
  (32 shorter events, 3.2 us)
Async XLA Ops:
  0.6 0.7 copy-start.13
  0.6 0.8 copy-start.12
  0.7 22.1 %copy-start = (f32[59,4096]{1,0:T(8,128)S(1)}, f32[59,4096]{1,0:T(8,128)}, u32[]{:S(2)}) copy-start(f32[59,4096]{1,0:T(8,128)} %params_ref.3) | copy-start | bytes 2899972
  1.7 9.6 %copy-start.11 = (s32[2,8,512]{1,2,0:T(8,128)}, s32[2,8,512]{1,2,0:T(8,128)S(1)}, u32[]{:S(2)}) copy-start(s32[2,8,512]{1,2,0:T(8,128)S(1)} %copy.19) | copy-start | bytes 98308
  10.6 0.6 copy-start.9
  11.3 20.9 %all-to-all-start = ((s32[128,1,128]{2,1,0:T(1,128)}), s32[128,1,128]{2,1,0:T(1,128)S(1)}, u32[]{:S(2)}, u32[]{:S(2)}) async-start(s32[128,1,128]{2,1,0:T(1,128)} %bitcast.5), calls=%async_computation | async-start | bytes 131072 | tf_op jit(solution)/shard_map/all_to_all | solution.py:782
  32.2 10.9 %copy-start.14 = (s32[16]{0:T(128)S(1)}, s32[16]{0:T(128)}, u32[]{:S(2)}) copy-start(s32[16]{0:T(128)} %param.13) | copy-start | bytes 196
  36.5 60.3 %copy-start.2 = (f32[59,4096]{1,0:T(8,128)S(1)}, f32[59,4096]{1,0:T(8,128)}, u32[]{:S(2)}) copy-start(f32[59,4096]{1,0:T(8,128)} %two_ref.1) | copy-start | bytes 2899972
  36.5 16.2 %all-to-all-start.1 = ((f32[128,1,640]{2,1,0:T(1,128)}), f32[128,1,640]{2,1,0:T(1,128)S(1)}, u32[]{:S(2)}, u32[]{:S(2)}) async-start(f32[128,1,640]{2,1,0:T(1,128)} %bitcast.7), calls=%async_computation.1 | async-start | bytes 655360 | tf_op jit(solution)/shard_map/all_to_all | solution.py:782
  41.1 55.7 %copy-start.1 = (f32[59,4096]{1,0:T(8,128)S(1)}, f32[59,4096]{1,0:T(8,128)}, u32[]{:S(2)}) copy-start(f32[59,4096]{1,0:T(8,128)} %one_ref.1) | copy-start | bytes 2899972
  45.9 0.8 copy-start.7
  46.7 0.8 copy-start.10
  49.0 0.6 copy-start.3
  52.7 0.9 copy-start.4
  53.6 0.8 copy-start.6
  77.7 0.7 copy-start.5
  78.5 18.3 %all-to-all-start.2 = ((f32[128,1,640]{2,1,0:T(1,128)}), f32[128,1,640]{2,1,0:T(1,128)S(1)}, u32[]{:S(2)}, u32[]{:S(2)}) async-start(f32[128,1,640]{2,1,0:T(1,128)} %bitcast.29), calls=%async_computation.2 | async-start | bytes 655360 | tf_op jit(solution)/shard_map/all_to_all | solution.py:782
  96.8 0.8 copy-start.8

commit v3 on v2

--- a/solution.py
+++ b/solution.py
@@ -1,4 +1,3 @@
-import numpy as np
 import jax
 import jax.numpy as jnp
 from jax import lax
@@ -41,6 +40,7 @@
 F32 = jnp.float32
 BF16 = jnp.bfloat16
 VMEM = pl.BlockSpec(memory_space=pltpu.VMEM)
+ANY = pl.BlockSpec(memory_space=pl.ANY)
 FU = 4
 BU = 4
 PU = 8
@@ -174,37 +174,97 @@
     )
 
 
-def plan_kernel(sorted_ref, request_ref, table_ref, owner_s, rank_s, local_s):
-    keys = sorted_ref[...]
-    lane = iota((64, 128), 1)
-    line = iota((64, 128), 0)
-
-    def earlier(value):
-        shifted = pltpu.roll(value, 1, 1)
-        return jnp.where(lane == 0, pltpu.roll(shifted, 1, 0), shifted)
-
-    first_slot = (lane == 0) & (line == 0)
-    before = earlier(keys)
-    fresh = ((keys != before) | first_slot) & (keys < SENTINEL)
-    fresh_h = jnp.where(fresh, 1.0, 0.0).astype(BF16)
-    upto = jnp.where(iota((128, 128), 0) <= iota((128, 128), 1), 1.0, 0.0).astype(BF16)
-    ones = jnp.ones((128, 128), BF16)
-    lower = jnp.where(iota((64, 64), 1) < iota((64, 64), 0), 1.0, 0.0).astype(BF16)
-    totals = dot_nn(fresh_h, ones).astype(BF16)
-    count = (dot_nn(fresh_h, upto) + dot_nn(lower, totals)).astype(jnp.int32) - 1
-    owner = keys >> 12
-    opens = (owner != (before >> 12)) | first_slot
-    base = jnp.where(opens, count, 0)
+def sort_all(parts):
+    sublane = iota((8, 128), 0)
+    lane = iota((8, 128), 1)
+
+    def bit_of(bit, number):
+        if bit < 3:
+            return (number >> bit) & 1
+        if bit < 6:
+            return (sublane >> (bit - 3)) & 1
+        return (lane >> (bit - 6)) & 1
+
+    flipped = [0] * 8
+    for level in range(1, 14):
+        for number in range(8):
+            turn = bit_of(level, number) if level < 13 else 0
+            change = flipped[number] ^ turn
+            if not isinstance(change, int):
+                parts[number] = parts[number] ^ (0 - change)
+            elif change:
+                parts[number] = ~parts[number]
+            flipped[number] = turn
+        for bit in range(level - 1, -1, -1):
+            if bit < 3:
+                stride = 1 << bit
+                for number in range(8):
+                    if not number & stride:
+                        one, two = parts[number], parts[number + stride]
+                        parts[number] = jnp.minimum(one, two)
+                        parts[number + stride] = jnp.maximum(one, two)
+            else:
+                axis, size = (0, 8) if bit < 6 else (1, 128)
+                stride = 1 << (bit - 3 if bit < 6 else bit - 6)
+                is_low = bit_of(bit, 0) == 0
+                for number in range(8):
+                    here = parts[number]
+                    up = pltpu.roll(here, size - stride, axis)
+                    down = pltpu.roll(here, stride, axis) if 2 * stride < size else up
+                    parts[number] = jnp.where(
+                        is_low, jnp.minimum(here, up), jnp.maximum(here, down)
+                    )
+    return parts
+
+
+def plan_kernel(visible_ref, counts_ref, request_ref, owner_s, rank_s, local_s):
+    lane = iota((8, 128), 1)
+    sublane = iota((8, 128), 0)
+    keys = []
+    for rows in (slice(0, 8), slice(8, 16)):
+        for block in range(4):
+            limit = jnp.broadcast_to(counts_ref[rows, block : block + 1], (8, 128))
+            ids = visible_ref[rows, block * 128 : (block + 1) * 128]
+            keys.append(jnp.where(lane < limit, ids, SENTINEL))
+    keys = sort_all(keys)
+
+    def earlier(value, fill):
+        shifted = pltpu.roll(value, 1, 0)
+        shifted = jnp.where(sublane == 0, pltpu.roll(shifted, 1, 1), shifted)
+        return jnp.where((sublane == 0) & (lane == 0), fill, shifted)
+
+    before = [earlier(keys[7], -1)] + keys[0:7]
+    fresh = [(keys[n] != before[n]) & (keys[n] < SENTINEL) for n in range(8)]
+    opens = [(keys[n] >> 12) != (before[n] >> 12) for n in range(8)]
+    counts = []
+    for number in range(8):
+        one = jnp.where(fresh[number], 1, 0)
+        counts.append(one if number == 0 else counts[-1] + one)
+    column = counts[7]
+    for step in (1, 2, 4):
+        column = column + jnp.where(sublane >= step, pltpu.roll(column, step, 0), 0)
+    whole = jnp.broadcast_to(column[7:8], (8, 128)).astype(F32).astype(BF16)
+    strictly = jnp.where(iota((128, 128), 0) < iota((128, 128), 1), 1.0, 0.0).astype(BF16)
+    offset = dot_nn(whole, strictly).astype(jnp.int32) + column - counts[7] - 1
+    counts = [count + offset for count in counts]
+    bases = []
+    for number in range(8):
+        one = jnp.where(opens[number], counts[number], 0)
+        bases.append(one if number == 0 else jnp.maximum(bases[-1], one))
+    column = bases[7]
+    for step in (1, 2, 4):
+        column = jnp.maximum(column, jnp.where(sublane >= step, pltpu.roll(column, step, 0), 0))
+    whole = jnp.broadcast_to(column[7:8], (8, 128))
     for step in (1, 2, 4, 8, 16, 32, 64):
-        base = jnp.maximum(base, jnp.where(lane >= step, pltpu.roll(base, step, 1), 0))
-    above = jnp.broadcast_to(jnp.max(base, axis=1, keepdims=True), (64, 128))
-    above = jnp.where(line >= 1, pltpu.roll(above, 1, 0), 0)
-    for step in (1, 2, 4, 8, 16, 32):
-        above = jnp.maximum(above, jnp.where(line >= step, pltpu.roll(above, step, 0), 0))
-    rank = count - jnp.maximum(base, above)
-    owner_s[...] = owner
-    rank_s[...] = jnp.where(fresh, rank, -1)
-    local_s[...] = keys & (G_DEV - 1)
+        whole = jnp.maximum(whole, jnp.where(lane >= step, pltpu.roll(whole, step, 1), 0))
+    whole = jnp.where(lane >= 1, pltpu.roll(whole, 1, 1), 0)
+    above = jnp.maximum(whole, jnp.where(sublane >= 1, pltpu.roll(column, 1, 0), 0))
+    for number in range(8):
+        rows = slice(number * 8, (number + 1) * 8)
+        rank = counts[number] - jnp.maximum(bases[number], above)
+        owner_s[rows, :] = keys[number] >> 12
+        rank_s[rows, :] = jnp.where(fresh[number], rank, -1)
+        local_s[rows, :] = keys[number] & (G_DEV - 1)
 
     def fill(index, total):
         local = pair(local_s, index)
@@ -216,32 +276,29 @@
 
     filled = lax.fori_loop(0, 32, fill, jnp.zeros((128, 128), F32), unroll=PU)
     locals_of = (filled[0:64] * 64.0 + filled[64:128]).astype(jnp.int32)
-    table_ref[...] = locals_of
     padded = jnp.concatenate([locals_of, jnp.zeros((64, 128), jnp.int32)], axis=0)
     request_ref[...] = jnp.transpose(padded)
 
 
-def plan(keys_sorted):
+def plan(visible, counts):
     return pl.pallas_call(
         plan_kernel,
-        out_shape=(
-            jax.ShapeDtypeStruct((128, 128), jnp.int32),
-            jax.ShapeDtypeStruct((64, 128), jnp.int32),
-        ),
-        in_specs=[VMEM],
-        out_specs=(VMEM, VMEM),
+        out_shape=jax.ShapeDtypeStruct((128, 128), jnp.int32),
+        in_specs=[VMEM] * 2,
+        out_specs=VMEM,
         scratch_shapes=[pltpu.VMEM((64, 128), jnp.int32)] * 3,
         compiler_params=pltpu.CompilerParams(vmem_limit_bytes=32 * 1024 * 1024),
-    )(keys_sorted)
-
-
-def find_kernel(table_ref, keys_ref, centre_ref, slots_ref):
+    )(visible, counts)
+
+
+def find_kernel(request_ref, keys_ref, centre_ref, slots_ref):
+    table = jnp.transpose(request_ref[...])
     keys = keys_ref[...]
     owner = (keys >> 12) & 127
     local = keys & (G_DEV - 1)
     rank = jnp.zeros((64, 128), jnp.int32)
     for place in range(63, -1, -1):
-        row = jnp.broadcast_to(table_ref[place : place + 1, :], (64, 128))
+        row = jnp.broadcast_to(table[place : place + 1], (64, 128))
         found = jnp.take_along_axis(row, owner, axis=1, mode="promise_in_bounds")
         rank = jnp.where(found == local, place, rank)
     tile = jnp.where(
@@ -254,14 +311,14 @@
     slots_ref[128:192, :] = jnp.where(keys < SENTINEL, tile, -1)
 
 
-def find(table, keys, centre):
+def find(request, keys, centre):
     return pl.pallas_call(
         find_kernel,
         out_shape=jax.ShapeDtypeStruct((192, 128), jnp.int32),
         in_specs=[VMEM] * 3,
         out_specs=VMEM,
         compiler_params=pltpu.CompilerParams(vmem_limit_bytes=32 * 1024 * 1024),
-    )(table, keys, centre)
+    )(request, keys, centre)
 
 
 def gather_all(table_ref, high_ref, low_ref, out_ref, size):
@@ -309,13 +366,14 @@
             total = total + basis[degree - 1] * row(11 + 3 * degree + channel)
         feats.append(total)
     for index in range(9):
-        feats_ref[index * 32 : (index + 1) * 32, :] = feats[index]
+        rows = feats[index]
+        three_parts(jnp.concatenate([rows[0:16], rows[16:32]], axis=1), feats_ref, index, 16)
 
 
 def project(params):
     return pl.pallas_call(
         project_kernel,
-        out_shape=jax.ShapeDtypeStruct((288, 128), F32),
+        out_shape=jax.ShapeDtypeStruct((27 * 16, 256), BF16),
         in_specs=[VMEM],
         out_specs=VMEM,
         scratch_shapes=[pltpu.VMEM((59 * 32, 128), F32)],
@@ -323,14 +381,11 @@
     )(params)
 
 
-def serve_kernel(feats_ref, wanted_ref, out_ref, place_s, table_s, high_s, low_s):
+def serve_kernel(table_ref, wanted_ref, out_ref, place_s, high_s, low_s):
     wanted = jnp.transpose(wanted_ref[...])[0:64]
     high_s[...] = (wanted >> 11) * 128 + (wanted & 127)
     low_s[...] = (wanted >> 7) & 15
-    for feature in range(9):
-        rows = feats_ref[feature * 32 : (feature + 1) * 32, :]
-        three_parts(jnp.concatenate([rows[0:16], rows[16:32]], axis=1), table_s, feature, 16)
-    gather_all(table_s, high_s, low_s, place_s, 16)
+    gather_all(table_ref, high_s, low_s, place_s, 16)
     place_s[576:640, :] = jnp.zeros((64, 128), F32)
     for part in range(5):
         out_ref[pl.ds(part, 128, stride=5), :] = jnp.transpose(
@@ -346,7 +401,6 @@
         out_specs=VMEM,
         scratch_shapes=[
             pltpu.VMEM((640, 128), F32),
-            pltpu.VMEM((27 * 16, 256), BF16),
             pltpu.VMEM((64, 128), jnp.int32),
             pltpu.VMEM((64, 128), jnp.int32),
         ],
@@ -374,8 +428,8 @@
 
 def render_kernel(
     arrived_ref,
-    slots_ref,
-    target_ref,
+    slots_hbm,
+    target_hbm,
     out_ref,
     loss_ref,
     places_s,
@@ -387,7 +441,14 @@
     grads_s,
     weights_s,
     parts_s,
+    slots_ref,
+    target_ref,
+    sems,
 ):
+    slots_copy = pltpu.make_async_copy(slots_hbm, slots_ref, sems.at[0])
+    target_copy = pltpu.make_async_copy(target_hbm, target_ref, sems.at[1])
+    slots_copy.start()
+    target_copy.start()
     for part in range(5):
         table_s[part * 128 : (part + 1) * 128, :] = jnp.transpose(
             arrived_ref[pl.ds(part, 128, stride=5), :]
@@ -402,6 +463,8 @@
             feature,
             32,
         )
+    slots_copy.wait()
+    target_copy.wait()
     gather_all(
         places_s, slots_ref.at[pl.ds(0, 64), :], slots_ref.at[pl.ds(64, 64), :], table_s, 32
     )
@@ -646,7 +709,7 @@
             jax.ShapeDtypeStruct((640, 128), F32),
             jax.ShapeDtypeStruct((16, 128), F32),
         ),
-        in_specs=[VMEM] * 3,
+        in_specs=[VMEM, ANY, ANY],
         out_specs=(VMEM, VMEM),
         scratch_shapes=[
             pltpu.VMEM((27 * 32, 256), BF16),
@@ -658,6 +721,9 @@
             pltpu.VMEM((64 * 16, 128), F32),
             pltpu.VMEM((2, 1024, 128), BF16),
             pltpu.VMEM((8192, 1024), BF16),
+            pltpu.VMEM((192, 128), jnp.int32),
+            pltpu.VMEM((48, 256), F32),
+            pltpu.SemaphoreType.DMA((2,)),
         ],
         compiler_params=pltpu.CompilerParams(vmem_limit_bytes=48 * 1024 * 1024),
     )(arrived, slots, target)
@@ -681,7 +747,6 @@
     params_ref,
     one_ref,
     two_ref,
-    rates_ref,
     new_params_ref,
     new_one_ref,
     new_two_ref,
@@ -741,7 +806,9 @@
     fix_two = 1.0 / (1.0 - BETA_TWO**ADAM_STEP)
     for base in range(0, 59, 8):
         size = min(8, 59 - base)
-        rate = jnp.broadcast_to(rates_ref[base : base + size, 0:1], (size, 128))
+        rate = jnp.zeros((size, 128), F32)
+        for index in range(size):
+            rate = jnp.where(iota((size, 128), 0) == index, learn_rate(base + index), rate)
         for piece in range(32):
             cut = (slice(base, base + size), slice(piece * 128, (piece + 1) * 128))
             grad = grads_s[pl.ds(base * 32 + piece, size, stride=32), :]
@@ -754,13 +821,11 @@
 
 
 def update(received, wanted, params, moment_one, moment_two):
-    rates = np.zeros((64, 128), np.float32)
-    rates[0:59] = np.array([learn_rate(index) for index in range(59)], np.float32)[:, None]
     whole = jax.ShapeDtypeStruct((59, G_DEV), F32)
     return pl.pallas_call(
         update_kernel,
         out_shape=(whole, whole, whole),
-        in_specs=[VMEM] * 6,
+        in_specs=[VMEM] * 5,
         out_specs=(VMEM, VMEM, VMEM),
         scratch_shapes=[
             pltpu.VMEM((59 * 32, 128), F32),
@@ -768,7 +833,7 @@
             pltpu.VMEM((64 * 16, 128), F32),
         ],
         compiler_params=pltpu.CompilerParams(vmem_limit_bytes=48 * 1024 * 1024),
-    )(received, wanted, params, moment_one, moment_two, jnp.asarray(rates))
+    )(received, wanted, params, moment_one, moment_two)
 
 
 def slot_keys(visible, counts):
@@ -785,12 +850,11 @@
 
 def shards(params, moment_one, moment_two, visible, counts, tile_pos, target):
     keys = slot_keys(visible, counts)
-    keys_sorted = lax.sort(keys.reshape(-1), is_stable=False).reshape(64, 128)
-    request, table = plan(keys_sorted)
+    request = plan(visible, counts)
     wanted = exchange(request)
     feats = project(params)
     centre = jnp.tile(tile_pos.reshape(2, 8), (1, 16))
-    slots = find(table, keys, centre)
+    slots = find(request, keys, centre)
     colours = target.astype(F32).reshape(2, 8, 3, 256)
     colours = jnp.transpose(colours, (0, 2, 1, 3)).reshape(48, 256)
     arrived = exchange(serve(feats, wanted))

time: 104 us -> 97.9 us (0.941)
  other arithmetic: 6.35 us -> 0.01 us
  Pallas kernels: 38.8 us -> 41.9 us
  starting transfers between devices: 22.8 us -> 21.2 us
  waiting for transfers between devices: 22.8 us -> 21.6 us
    sort x1 -> x0, other arithmetic: 5.59 us -> none  [shards(): keys_sorted = lax.sort(keys.reshape(-1), is_stable=False).reshape(64, 128)]
    pallas_call x2, Pallas kernels: 3.8 us -> 5.85 us  [the longest x1 5.1 us: plan(): pl.pallas_call(plan_kernel, out_shape=jax.ShapeDtypeStruct((128, 128), jn...]
    all_to_all x3, starting transfers between devices: 22.8 us -> 21.2 us  [exchange(): flat = lax.all_to_all(flat, 'dev', split_axis=0, concat_axis=0, tiled=True)]
    another operation x3, local copies, waits for them, and re-layouts: 1.49 us -> 0.18 us  [shards(): centre = jnp.tile(tile_pos.reshape(2, 8), (1, 16))]
    all_to_all x3, waiting for transfers between devices: 22.8 us -> 21.6 us  [exchange(): flat = lax.all_to_all(flat, 'dev', split_axis=0, concat_axis=0, tiled=True)]
    unnamed x31 -> x27, local copies, waits for them, and re-layouts: 6.69 us -> 7.2 us
  transfers between devices with their start and end apart: 3 -> 3, of which waited for: 3 -> 3; matrix products, arithmetic and copies ran while one was open for 5% -> 5% of each run, Pallas kernels for 2% -> 3%
where the time goes in v3:
time: 97.9 us; the launch traced here: 97.2 us
  Pallas kernels  41.9 us (43%)
  waiting for transfers between devices  21.6 us (22%)
  starting transfers between devices  21.2 us (22%)
  local copies, waits for them, and re-layouts  11.7 us (12%)
    pallas_call x1, Pallas kernels, render(): pl.pallas_call(render_kernel, out_shape=(jax.ShapeDtypeStruct((640, 128),...  23.4 us
    all_to_all x3, waiting for transfers between devices, exchange(): flat = lax.all_to_all(flat, 'dev', split_axis=0, concat_axis=0, tiled=True)  21.6 us
    all_to_all x3, starting transfers between devices, exchange(): flat = lax.all_to_all(flat, 'dev', split_axis=0, concat_axis=0, tiled=True)  21.2 us
    unnamed x27, local copies, waits for them, and re-layouts  7.2 us
    pallas_call x1, Pallas kernels, update(): pl.pallas_call(update_kernel, out_shape=(whole, whole, whole), in_specs=[...  5.9 us
    pallas_call x1, Pallas kernels, plan(): pl.pallas_call(plan_kernel, out_shape=jax.ShapeDtypeStruct((128, 128), jn...  5.1 us
    pallas_call x1, Pallas kernels, serve(): pl.pallas_call(serve_kernel, out_shape=jax.ShapeDtypeStruct((640, 128), F...  4.29 us
    reshape x2, local copies, waits for them, and re-layouts, slot_keys(): return jnp.transpose(keys.reshape(2, 8, 512), (0, 2, 1)).reshape(64, 128)  2.96 us
  transfers between devices with their start and end apart: 3, of which 3 were waited for; matrix products, arithmetic and copies ran while one was open for 5% of the time, Pallas kernels for 3%

profile of v3, /device:TPU:1, one launch (start us, length us, event | category | flops | bytes accessed | tf_op | source)
XLA Modules:
  0.0 97.2 jit_solution(5486204837024654800)
XLA Ops:
  0.6 0.8 copy.19.counts_ref
  1.4 0.8 copy-done.8
  2.1 5.1 %shard_map.103.request_ref = s32[128,128]{1,0:T(8,128)} custom-call(s32[16,512]{1,0:T(8,128)S(1)} %copy-done.8, s32[16,4]{1,0:T(8,128)S(1)} %copy.19.counts_ref), custom_call_target="tpu_custom_call" | custom-call | tf_op jit(solution)/shard_map/pallas_call | solution.py:284
  7.3 11.5 %all-to-all-start = ((s32[128,1,128]{2,1,0:T(1,128)}), s32[128,1,128]{2,1,0:T(1,128)S(1)}, u32[]{:S(2)}, u32[]{:S(2)}) async-start(s32[128,1,128]{2,1,0:T(1,128)} %bitcast.1), calls=%async_computation | async-start | bytes 131072 | tf_op jit(solution)/shard_map/all_to_all | solution.py:847
  18.8 0.6 copy-done.12
  19.6 0.6 copy.24
  20.2 1.2 %copy-done = f32[59,4096]{1,0:T(8,128)S(1)} copy-done((f32[59,4096]{1,0:T(8,128)S(1)}, f32[59,4096]{1,0:T(8,128)}, u32[]{:S(2)}) %copy-start) | copy-done | bytes 966680
  21.5 0.8 shard_map.102.table_ref
  22.2 6.0 %all-to-all-done = s32[128,1,128]{2,1,0:T(1,128)S(1)} async-done(((s32[128,1,128]{2,1,0:T(1,128)}), s32[128,1,128]{2,1,0:T(1,128)S(1)}, u32[]{:S(2)}, u32[]{:S(2)}) %all-to-all-start) | async-done | bytes 65568 | tf_op jit(solution)/shard_map/all_to_all | solution.py:847
  28.2 4.3 %shard_map.104 = f32[640,128]{1,0:T(8,128)} custom-call(bf16[432,256]{1,0:T(8,128)(2,1)S(1)} %shard_map.102.table_ref, s32[128,128]{1,0:T(8,128)S(1)} %bitcast.26), custom_call_target="tpu_custom_call" | custom-call | tf_op jit(solution)/shard_map/pallas_call | solution.py:397
  32.5 4.6 %all-to-all-start.1 = ((f32[128,1,640]{2,1,0:T(1,128)}), f32[128,1,640]{2,1,0:T(1,128)S(1)}, u32[]{:S(2)}, u32[]{:S(2)}) async-start(f32[128,1,640]{2,1,0:T(1,128)} %bitcast.3), calls=%async_computation.1 | async-start | bytes 655360 | tf_op jit(solution)/shard_map/all_to_all | solution.py:847
  37.2 1.0 %copy.23 = s32[2,8,512]{1,2,0:T(8,128)} copy(s32[2,8,512]{2,1,0:T(8,128)S(1)} %select_bitcast_fusion) | data formatting | bytes 65536 | tf_op jit(solution)/shard_map/reshape | solution.py:842
  38.2 2.0 %reshape.54.keys_ref = s32[64,128]{1,0:T(8,128)} reshape(s32[2,512,8]{2,1,0:T(8,128)} %bitcast.30) | data formatting | bytes 65536 | tf_op jit(solution)/shard_map/reshape | solution.py:842
  40.2 0.8 copy-done.10
  40.9 2.5 %shard_map.105.slots_hbm = s32[192,128]{1,0:T(8,128)S(1)} custom-call(s32[128,128]{1,0:T(8,128)} %shard_map.103.request_ref, s32[64,128]{1,0:T(8,128)S(1)} %copy-done.10, s32[2,128]{1,0:T(2,128)S(1)} %tile.12.centre_ref), custom_call_target="tpu_custom_call" | custom-call | tf_op jit(solution)/shard_map/pallas_call | solution.py:315
  43.4 0.6 copy-done.4
  44.0 4.7 %all-to-all-done.1 = f32[128,1,640]{2,1,0:T(1,128)S(1)} async-done(((f32[128,1,640]{2,1,0:T(1,128)}), f32[128,1,640]{2,1,0:T(1,128)S(1)}, u32[]{:S(2)}, u32[]{:S(2)}) %all-to-all-start.1) | async-done | bytes 327712 | tf_op jit(solution)/shard_map/all_to_all | solution.py:847
  48.7 0.9 copy-done.5
  49.6 0.8 copy-done.7
  50.4 23.4 %shard_map.106 = (f32[640,128]{1,0:T(8,128)S(1)}, f32[16,128]{1,0:T(8,128)S(1)}) custom-call(f32[640,128]{1,0:T(8,128)S(1)} %bitcast.25, s32[192,128]{1,0:T(8,128)S(1)} %copy-done.5, f32[48,256]{1,0:T(8,128)S(1)} %bitcast.29), custom_call_target="tpu_custom_call" | custom-call | tf_op jit(solution)/shard_map/pallas_call | solution.py:706
  73.9 0.7 copy-done.6
  74.6 5.1 %all-to-all-start.2 = ((f32[128,1,640]{2,1,0:T(1,128)}), f32[128,1,640]{2,1,0:T(1,128)S(1)}, u32[]{:S(2)}, u32[]{:S(2)}) async-start(f32[128,1,640]{2,1,0:T(1,128)} %bitcast.28), calls=%async_computation.2 | async-start | bytes 655360 | tf_op jit(solution)/shard_map/all_to_all | solution.py:847
  80.3 11.0 %all-to-all-done.2 = f32[128,1,640]{2,1,0:T(1,128)S(1)} async-done(((f32[128,1,640]{2,1,0:T(1,128)}), f32[128,1,640]{2,1,0:T(1,128)S(1)}, u32[]{:S(2)}, u32[]{:S(2)}) %all-to-all-start.2) | async-done | bytes 327712 | tf_op jit(solution)/shard_map/all_to_all | solution.py:847
  91.3 5.9 %shard_map.107 = (f32[59,4096]{1,0:T(8,128)}, f32[59,4096]{1,0:T(8,128)}, f32[59,4096]{1,0:T(8,128)}) custom-call(f32[640,128]{1,0:T(8,128)S(1)} %bitcast.24, s32[128,128]{1,0:T(8,128)S(1)} %bitcast.27, f32[59,4096]{1,0:T(8,128)S(1)} %copy-done.1, f32[59,4096]{1,0:T(8,128)S(1)} %copy-done.2, f32[59,4096]{1,0:T(8,128)S(1)} %copy-done.3), custom_call_target="tpu_custom_call" | custom-call | tf_op jit(solution)/shard_map/pallas_call | solution.py:825
  (26 shorter events, 0.9 us)
Async XLA Ops:
  1.4 0.8 copy-start.8
  7.2 11.5 %copy-start.11 = (bf16[16,3,256]{2,0,1:T(8,128)(2,1)S(1)}, bf16[16,3,256]{2,0,1:T(8,128)(2,1)}, u32[]{:S(2)}) copy-start(bf16[16,3,256]{2,0,1:T(8,128)(2,1)} %param.13) | copy-start | bytes 73732
  7.3 20.9 %all-to-all-start = ((s32[128,1,128]{2,1,0:T(1,128)}), s32[128,1,128]{2,1,0:T(1,128)S(1)}, u32[]{:S(2)}, u32[]{:S(2)}) async-start(s32[128,1,128]{2,1,0:T(1,128)} %bitcast.1), calls=%async_computation | async-start | bytes 131072 | tf_op jit(solution)/shard_map/all_to_all | solution.py:847
  18.8 0.7 copy-start.12
  20.2 1.2 %copy-start = (f32[59,4096]{1,0:T(8,128)S(1)}, f32[59,4096]{1,0:T(8,128)}, u32[]{:S(2)}) copy-start(f32[59,4096]{1,0:T(8,128)} %params_ref.3) | copy-start | bytes 2899972
  28.2 9.0 %copy-start.9 = (s32[16,512]{1,0:T(8,128)S(1)}, s32[16,512]{1,0:T(8,128)}, u32[]{:S(2)}) copy-start(s32[16,512]{1,0:T(8,128)} %visible_ref.1) | copy-start | bytes 98308
  32.5 58.8 %copy-start.3 = (f32[59,4096]{1,0:T(8,128)S(1)}, f32[59,4096]{1,0:T(8,128)}, u32[]{:S(2)}) copy-start(f32[59,4096]{1,0:T(8,128)} %two_ref.1) | copy-start | bytes 2899972
  32.5 16.2 %all-to-all-start.1 = ((f32[128,1,640]{2,1,0:T(1,128)}), f32[128,1,640]{2,1,0:T(1,128)S(1)}, u32[]{:S(2)}, u32[]{:S(2)}) async-start(f32[128,1,640]{2,1,0:T(1,128)} %bitcast.3), calls=%async_computation.1 | async-start | bytes 655360 | tf_op jit(solution)/shard_map/all_to_all | solution.py:847
  37.2 54.1 %copy-start.2 = (f32[59,4096]{1,0:T(8,128)S(1)}, f32[59,4096]{1,0:T(8,128)}, u32[]{:S(2)}) copy-start(f32[59,4096]{1,0:T(8,128)} %one_ref.1) | copy-start | bytes 2899972
  38.2 53.1 %copy-start.1 = (f32[59,4096]{1,0:T(8,128)S(1)}, f32[59,4096]{1,0:T(8,128)}, u32[]{:S(2)}) copy-start(f32[59,4096]{1,0:T(8,128)} %params_ref.3) | copy-start | bytes 2899972
  40.2 0.8 copy-start.10
  43.4 0.6 copy-start.4
  48.7 0.9 copy-start.5
  49.6 0.8 copy-start.7
  73.9 0.7 copy-start.6
  74.6 16.7 %all-to-all-start.2 = ((f32[128,1,640]{2,1,0:T(1,128)}), f32[128,1,640]{2,1,0:T(1,128)S(1)}, u32[]{:S(2)}, u32[]{:S(2)}) async-start(f32[128,1,640]{2,1,0:T(1,128)} %bitcast.28), calls=%async_computation.2 | async-start | bytes 655360 | tf_op jit(solution)/shard_map/all_to_all | solution.py:847

commit v4 on v3

--- a/solution.py
+++ b/solution.py
@@ -40,14 +40,9 @@
 F32 = jnp.float32
 BF16 = jnp.bfloat16
 VMEM = pl.BlockSpec(memory_space=pltpu.VMEM)
-ANY = pl.BlockSpec(memory_space=pl.ANY)
-FU = 4
-BU = 4
+HBM = pl.BlockSpec(memory_space=pltpu.HBM)
 PU = 8
 GU = 4
-SU = 8
-MROWS = 1024
-MU = 1
 
 
 def harmonics(dir_x, dir_y, dir_z):
@@ -217,15 +212,14 @@
     return parts
 
 
-def plan_kernel(visible_ref, counts_ref, request_ref, owner_s, rank_s, local_s):
+def plan_kernel(visible_ref, request_ref, owner_s, rank_s, local_s):
     lane = iota((8, 128), 1)
     sublane = iota((8, 128), 0)
     keys = []
     for rows in (slice(0, 8), slice(8, 16)):
         for block in range(4):
-            limit = jnp.broadcast_to(counts_ref[rows, block : block + 1], (8, 128))
             ids = visible_ref[rows, block * 128 : (block + 1) * 128]
-            keys.append(jnp.where(lane < limit, ids, SENTINEL))
+            keys.append(jnp.where(ids < 0, SENTINEL, ids))
     keys = sort_all(keys)
 
     def earlier(value, fill):
@@ -280,15 +274,15 @@
     request_ref[...] = jnp.transpose(padded)
 
 
-def plan(visible, counts):
+def plan(visible):
     return pl.pallas_call(
         plan_kernel,
         out_shape=jax.ShapeDtypeStruct((128, 128), jnp.int32),
-        in_specs=[VMEM] * 2,
+        in_specs=[VMEM],
         out_specs=VMEM,
         scratch_shapes=[pltpu.VMEM((64, 128), jnp.int32)] * 3,
         compiler_params=pltpu.CompilerParams(vmem_limit_bytes=32 * 1024 * 1024),
-    )(visible, counts)
+    )(visible)
 
 
 def find_kernel(request_ref, keys_ref, centre_ref, slots_ref):
@@ -321,23 +315,19 @@
     )(request, keys, centre)
 
 
-def gather_all(table_ref, high_ref, low_ref, out_ref, size):
-    def step(index, carry):
-        lanes = one_hot(pair(high_ref, index), 256)
-        match = pair(low_ref, index) == iota((size, 256), 0)
-        found = dot_nn(table_ref[...], lanes)
-        for feature in range(9):
-            parts = [
-                found[(9 * part + feature) * size : (9 * part + feature + 1) * size]
-                for part in range(3)
-            ]
-            picked = jnp.where(match, (parts[0] + parts[1]) + parts[2], 0.0)
-            line = jnp.sum(picked, axis=0, keepdims=True)
-            out_ref[pl.ds(64 * feature + 2 * index, 1), :] = line[:, 0:128]
-            out_ref[pl.ds(64 * feature + 2 * index + 1, 1), :] = line[:, 128:256]
-        return carry
-
-    lax.fori_loop(0, 32, step, 0, unroll=GU)
+def gather_one(table_ref, high_ref, low_ref, out_ref, size, index):
+    lanes = one_hot(pair(high_ref, index), 256)
+    match = pair(low_ref, index) == iota((size, 256), 0)
+    found = dot_nn(table_ref[...], lanes)
+    for feature in range(9):
+        parts = [
+            found[(9 * part + feature) * size : (9 * part + feature + 1) * size]
+            for part in range(3)
+        ]
+        picked = jnp.where(match, (parts[0] + parts[1]) + parts[2], 0.0)
+        line = jnp.sum(picked, axis=0, keepdims=True)
+        out_ref[pl.ds(64 * feature + 2 * index, 1), :] = line[:, 0:128]
+        out_ref[pl.ds(64 * feature + 2 * index + 1, 1), :] = line[:, 128:256]
 
 
 def three_parts(value, table_ref, feature, size):
@@ -385,7 +375,12 @@
     wanted = jnp.transpose(wanted_ref[...])[0:64]
     high_s[...] = (wanted >> 11) * 128 + (wanted & 127)
     low_s[...] = (wanted >> 7) & 15
-    gather_all(table_ref, high_s, low_s, place_s, 16)
+
+    def step(index, carry):
+        gather_one(table_ref, high_s, low_s, place_s, 16, index)
+        return carry
+
+    lax.fori_loop(0, 32, step, 0, unroll=GU)
     place_s[576:640, :] = jnp.zeros((64, 128), F32)
     for part in range(5):
         out_ref[pl.ds(part, 128, stride=5), :] = jnp.transpose(
@@ -438,7 +433,7 @@
     alpha_s,
     weight_s,
     sums_s,
-    grads_s,
+    feats_s,
     weights_s,
     parts_s,
     slots_ref,
@@ -465,51 +460,69 @@
         )
     slots_copy.wait()
     target_copy.wait()
-    gather_all(
-        places_s, slots_ref.at[pl.ds(0, 64), :], slots_ref.at[pl.ds(64, 64), :], table_s, 32
-    )
-    feats = [table_s[feature * 64 : (feature + 1) * 64, :] for feature in range(9)]
-    tile = slots_ref[128:192, :]
-    live = tile >= 0
-    rel_u = feats[0] - ((tile & (TILES_X - 1)).astype(F32) * 16.0 + 7.5)
-    rel_v = feats[1] - ((tile >> 6).astype(F32) * 16.0 + 7.5)
-    conic_1, conic_2, conic_3 = (feats[2], feats[3], feats[4])
-    h_1 = 0.5 * conic_1
-    h_3 = 0.5 * conic_3
-    pull_u = conic_1 * rel_u + conic_2 * rel_v
-    pull_v = conic_3 * rel_v + conic_2 * rel_u
-    centre_e = 0.5 * (conic_1 * rel_u * rel_u + conic_3 * rel_v * rel_v) + conic_2 * rel_u * rel_v
-    level = jnp.log2(0.99 * feats[5])
-    coefs = [
-        -LOG2_E * h_1,
-        -LOG2_E * conic_2,
-        -LOG2_E * h_3,
-        LOG2_E * pull_u,
-        LOG2_E * pull_v,
-        level - LOG2_E * centre_e,
-    ]
-    for index in range(6):
-        value = jnp.where(live, coefs[index], -1024.0 if index == 5 else 0.0)
-        high = value.astype(BF16).astype(F32)
-        rest = value - high
-        middle = rest.astype(BF16).astype(F32)
-        coef_s[pl.ds(index, 64, stride=24), :] = high
-        coef_s[pl.ds(index + 6, 64, stride=24), :] = middle
-        coef_s[pl.ds(index + 12, 64, stride=24), :] = rest - middle
-    for channel in range(3):
-        value = feats[6 + channel]
-        high = value.astype(BF16).astype(F32)
-        coef_s[pl.ds(18 + channel, 64, stride=24), :] = high
-        coef_s[pl.ds(21 + channel, 64, stride=24), :] = value - high
+    def gather(stage):
+        for group in range(2):
+            for step in range(4):
+                gather_one(
+                    places_s,
+                    slots_ref.at[pl.ds(0, 64), :],
+                    slots_ref.at[pl.ds(64, 64), :],
+                    feats_s,
+                    32,
+                    group * 16 + stage * 4 + step,
+                )
+
+    def slot_values(first):
+        feats = [feats_s[64 * f + first : 64 * f + first + 8, :] for f in range(9)]
+        tile = slots_ref[128 + first : 136 + first, :]
+        rel_u = feats[0] - ((tile & (TILES_X - 1)).astype(F32) * 16.0 + 7.5)
+        rel_v = feats[1] - ((tile >> 6).astype(F32) * 16.0 + 7.5)
+        return (feats, rel_u, rel_v, tile >= 0)
+
+    def prepare(first):
+        feats, rel_u, rel_v, live = slot_values(first)
+        conic_1, conic_2, conic_3 = (feats[2], feats[3], feats[4])
+        pull_u = conic_1 * rel_u + conic_2 * rel_v
+        pull_v = conic_3 * rel_v + conic_2 * rel_u
+        centre_e = (
+            0.5 * (conic_1 * rel_u * rel_u + conic_3 * rel_v * rel_v) + conic_2 * rel_u * rel_v
+        )
+        level = jnp.log2(0.99 * feats[5])
+        coefs = [
+            -0.5 * LOG2_E * conic_1,
+            -LOG2_E * conic_2,
+            -0.5 * LOG2_E * conic_3,
+            LOG2_E * pull_u,
+            LOG2_E * pull_v,
+            level - LOG2_E * centre_e,
+        ]
+        for index in range(6):
+            value = jnp.where(live, coefs[index], -1024.0 if index == 5 else 0.0)
+            high = value.astype(BF16).astype(F32)
+            rest = value - high
+            middle = rest.astype(BF16).astype(F32)
+            coef_s[pl.ds(first * 24 + index, 8, stride=24), :] = high
+            coef_s[pl.ds(first * 24 + index + 6, 8, stride=24), :] = middle
+            coef_s[pl.ds(first * 24 + index + 12, 8, stride=24), :] = rest - middle
+        for channel in range(3):
+            value = feats[6 + channel]
+            high = value.astype(BF16).astype(F32)
+            coef_s[pl.ds(first * 24 + 18 + channel, 8, stride=24), :] = high
+            coef_s[pl.ds(first * 24 + 21 + channel, 8, stride=24), :] = value - high
+
+    def chunk_of(number, size):
+        base = number * size
+        return pl.ds(base if isinstance(base, int) else pl.multiple_of(base, 8), size)
 
     def chunk_rows(group, index):
-        return pl.ds(pl.multiple_of(group * 4096 + index * 256, 256), 256)
+        base = group * 4096 + index * 256
+        return pl.ds(base if isinstance(base, int) else pl.multiple_of(base, 256), 256)
 
     def coef_of(group, index):
         base = group * 32 + index * 2
         return jnp.concatenate(
             [
-                coef_s[pl.ds(pl.multiple_of((base + half) * 24, 8), 24), :]
+                coef_s[chunk_of(base + half, 24), :]
                 for half in range(2)
             ],
             axis=1,
@@ -562,7 +575,15 @@
         return tuple(results)
 
     start = (jnp.ones((8, 256), F32), jnp.zeros((24, 256), F32))
-    state = lax.fori_loop(0, 16, forward, start + start, unroll=FU)
+    state = start + start
+    gather(0)
+    for stage in range(4):
+        if stage < 3:
+            gather(stage + 1)
+        for group in range(2):
+            prepare(group * 32 + stage * 8)
+        for step in range(4):
+            state = forward(4 * stage + step, state)
     err_all = []
     for group in range(2):
         errors = state[2 * group + 1] - target_ref[group * 24 : (group + 1) * 24, :]
@@ -612,61 +633,70 @@
         return tuple(results)
 
     zero = jnp.zeros((8, 256), F32)
-    lax.fori_loop(0, 16, backward, (zero, zero), unroll=BU)
-
-    for group in range(2):
-
-        def reduce_pixels(index, carry):
-            rows = pl.ds(pl.multiple_of(group * 4096 + index * MROWS, MROWS), MROWS)
-            sums = dot_nn(parts_s[rows, :], weights_s[group])
-            for part in range(MROWS // 128):
+    def reduce_pixels(stage):
+        for group in range(2):
+            first = group * 4096 + (3 - stage) * 1024
+            sums = dot_nn(parts_s[first : first + 1024, :], weights_s[group])
+            for part in range(8):
                 turned = jnp.transpose(sums[part * 128 : (part + 1) * 128])
-                base = (group * 32 + index * (MROWS // 128) + part) * 16
+                base = (first // 128 + part) * 16
                 tints = turned[8:32] + turned[32:56]
-                own = [
-                    jnp.sum(
-                        jnp.where(diagonal[:, 0:128], tints[ch * 8 : (ch + 1) * 8], 0.0),
-                        axis=0,
-                        keepdims=True,
+                sums_s[base : base + 8, :] = turned[0:8]
+                for channel in range(3):
+                    own = jnp.where(
+                        diagonal[:, 0:128], tints[channel * 8 : (channel + 1) * 8], 0.0
                     )
-                    for ch in range(3)
-                ]
-                sums_s[pl.ds(pl.multiple_of(base, 8), 8), :] = turned[0:8]
-                for channel in range(3):
-                    sums_s[pl.ds(base + 8 + channel, 1), :] = own[channel]
-            return carry
-
-        lax.fori_loop(0, 4096 // MROWS, reduce_pixels, 0, unroll=MU)
-
-    def sums_of(index):
-        return sums_s[pl.ds(index, 64, stride=16), :]
-
-    m_xx, m_xy, m_yy, m_x, m_y, m_0 = [sums_of(index) for index in range(6)]
-    s_x = m_x - rel_u * m_0
-    s_y = m_y - rel_v * m_0
-    s_xx = m_xx - 2.0 * rel_u * m_x + rel_u * rel_u * m_0
-    s_yy = m_yy - 2.0 * rel_v * m_y + rel_v * rel_v * m_0
-    s_xy = m_xy - rel_u * m_y - rel_v * m_x + rel_u * rel_v * m_0
-    slot_grads = [
-        conic_1 * s_x + conic_2 * s_y,
-        conic_3 * s_y + conic_2 * s_x,
-        -0.5 * s_xx,
-        -s_xy,
-        -0.5 * s_yy,
-        m_0,
-        sums_of(8),
-        sums_of(9),
-        sums_of(10),
-    ]
-    for index in range(9):
-        grads_s[pl.ds(index, 64, stride=16), :] = jnp.where(live, slot_grads[index], 0.0)
-    grads_s[pl.ds(9, 64, stride=16), :] = slots_ref[0:64, :].astype(F32)
-    grads_s[pl.ds(10, 64, stride=16), :] = slots_ref[64:128, :].astype(F32)
-
-    def scatter(index, total):
-        return scatter_step(two_rows(grads_s, index), 32, total)
-
-    collected = lax.fori_loop(0, 32, scatter, jnp.zeros((288, 256), F32), unroll=SU)
+                    sums_s[base + 8 + channel : base + 9 + channel, :] = jnp.sum(
+                        own, axis=0, keepdims=True
+                    )
+
+    def scatter(stage, total):
+        steps = []
+        for group in range(2):
+            first = group * 32 + (3 - stage) * 8
+            feats, rel_u, rel_v, live = slot_values(first)
+            conic_1, conic_2, conic_3 = (feats[2], feats[3], feats[4])
+
+            def sums_of(index):
+                return sums_s[pl.ds(first * 16 + index, 8, stride=16), :]
+
+            m_xx, m_xy, m_yy, m_x, m_y, m_0 = [sums_of(index) for index in range(6)]
+            s_x = m_x - rel_u * m_0
+            s_y = m_y - rel_v * m_0
+            s_xx = m_xx - 2.0 * rel_u * m_x + rel_u * rel_u * m_0
+            s_yy = m_yy - 2.0 * rel_v * m_y + rel_v * rel_v * m_0
+            s_xy = m_xy - rel_u * m_y - rel_v * m_x + rel_u * rel_v * m_0
+            slot_grads = [
+                conic_1 * s_x + conic_2 * s_y,
+                conic_3 * s_y + conic_2 * s_x,
+                -0.5 * s_xx,
+                -s_xy,
+                -0.5 * s_yy,
+                m_0,
+                sums_of(8),
+                sums_of(9),
+                sums_of(10),
+            ]
+            slot_grads = [jnp.where(live, grad, 0.0) for grad in slot_grads]
+            steps.append(
+                (
+                    slot_grads,
+                    slots_ref[first : first + 8, :],
+                    slots_ref[64 + first : 72 + first, :],
+                )
+            )
+        return total + scatter_rows(steps, 32)
+
+    state = (zero, zero)
+    collected = jnp.zeros((288, 256), F32)
+    for stage in range(6):
+        if stage >= 2:
+            collected = scatter(stage - 2, collected)
+        if 1 <= stage < 5:
+            reduce_pixels(stage - 1)
+        if stage < 4:
+            for step in range(4):
+                state = backward(4 * stage + step, state)
     for feature in range(9):
         piece = collected[feature * 32 : (feature + 1) * 32]
         table_s[feature * 64 : feature * 64 + 32, :] = piece[:, 0:128]
@@ -678,28 +708,30 @@
         )
 
 
-def two_rows(ref, index):
-    return jnp.concatenate(
-        [
-            ref[pl.ds(pl.multiple_of(index * 32, 16), 16), :],
-            ref[pl.ds(pl.multiple_of(index * 32 + 16, 16), 16), :],
-        ],
-        axis=1,
-    )
-
-
-def scatter_step(both, size, total):
-    lanes = one_hot(both[9:10].astype(jnp.int32), 256)
-    match = iota((size, 256), 0) == both[10:11].astype(jnp.int32)
-    high = both.astype(BF16).astype(F32)
-    low = both - high
-    masked = [
-        jnp.where(match, jnp.broadcast_to(part[feature : feature + 1], (size, 256)), 0.0)
-        for part in (high, low)
-        for feature in range(9)
-    ]
-    found = dot_nt(jnp.concatenate(masked, axis=0).astype(BF16), lanes)
-    return total + found[0 : 9 * size] + found[9 * size : 18 * size]
+def scatter_rows(steps, size):
+    lanes, masked_high, masked_low = [], [], []
+    for values, high, low in steps:
+        tops = [value.astype(BF16).astype(F32) for value in values]
+        rests = [value - top for value, top in zip(values, tops)]
+        for row in range(8):
+            cut = slice(row, row + 1)
+            lanes.append(one_hot(high[cut], 256))
+            match = low[cut] == iota((size, 128), 0)
+            for parts, found in ((tops, masked_high), (rests, masked_low)):
+                found.append(
+                    jnp.concatenate(
+                        [
+                            jnp.where(match, jnp.broadcast_to(part[cut], (size, 128)), 0.0)
+                            for part in parts
+                        ],
+                        axis=0,
+                    ).astype(BF16)
+                )
+    masked = jnp.concatenate(
+        [jnp.concatenate(masked_high, axis=1), jnp.concatenate(masked_low, axis=1)], axis=0
+    )
+    found = dot_nt(masked, jnp.concatenate(lanes, axis=1))
+    return found[0 : 9 * size] + found[9 * size : 18 * size]
 
 
 def render(arrived, slots, target):
@@ -709,7 +741,7 @@
             jax.ShapeDtypeStruct((640, 128), F32),
             jax.ShapeDtypeStruct((16, 128), F32),
         ),
-        in_specs=[VMEM, ANY, ANY],
+        in_specs=[VMEM, HBM, HBM],
         out_specs=(VMEM, VMEM),
         scratch_shapes=[
             pltpu.VMEM((27 * 32, 256), BF16),
@@ -718,7 +750,7 @@
             pltpu.VMEM((8192, 256), F32),
             pltpu.VMEM((8192, 256), F32),
             pltpu.VMEM((64 * 16, 128), F32),
-            pltpu.VMEM((64 * 16, 128), F32),
+            pltpu.VMEM((576, 128), F32),
             pltpu.VMEM((2, 1024, 128), BF16),
             pltpu.VMEM((8192, 1024), BF16),
             pltpu.VMEM((192, 128), jnp.int32),
@@ -758,16 +790,17 @@
     piece = wanted >> 7
     for part in range(5):
         turned = jnp.transpose(received_ref[pl.ds(part, 128, stride=5), :])
-        table_s[pl.ds(2 * part, 64, stride=16), :] = turned[0:64]
-        if part < 4:
-            table_s[pl.ds(2 * part + 1, 64, stride=16), :] = turned[64:128]
-    table_s[pl.ds(9, 64, stride=16), :] = ((piece >> 4) * 128 + (wanted & 127)).astype(F32)
-    table_s[pl.ds(10, 64, stride=16), :] = (piece & 15).astype(F32)
-
-    def scatter(index, total):
-        return scatter_step(two_rows(table_s, index), 16, total)
-
-    collected = lax.fori_loop(0, 32, scatter, jnp.zeros((144, 256), F32), unroll=SU)
+        table_s[part * 128 : (part + 1) * 128, :] = turned
+    high = (piece >> 4) * 128 + (wanted & 127)
+    low = piece & 15
+    collected = jnp.zeros((144, 256), F32)
+    for group in range(4):
+        steps = []
+        for first in (group * 16, group * 16 + 8):
+            rows = slice(first, first + 8)
+            values = [table_s[f * 64 + first : f * 64 + first + 8, :] for f in range(9)]
+            steps.append((values, high[rows], low[rows]))
+        collected = collected + scatter_rows(steps, 16)
 
     def grad_of(feature):
         part = collected[feature * 16 : (feature + 1) * 16]
@@ -830,15 +863,14 @@
         scratch_shapes=[
             pltpu.VMEM((59 * 32, 128), F32),
             pltpu.VMEM((59 * 32, 128), F32),
-            pltpu.VMEM((64 * 16, 128), F32),
+            pltpu.VMEM((640, 128), F32),
         ],
         compiler_params=pltpu.CompilerParams(vmem_limit_bytes=48 * 1024 * 1024),
     )(received, wanted, params, moment_one, moment_two)
 
 
-def slot_keys(visible, counts):
-    live = jnp.arange(128, dtype=jnp.int32)[None, None, :] < counts[:, :, None]
-    keys = jnp.where(live.reshape(visible.shape), visible, SENTINEL)
+def slot_keys(visible):
+    keys = jnp.where(visible < 0, SENTINEL, visible)
     return jnp.transpose(keys.reshape(2, 8, 512), (0, 2, 1)).reshape(64, 128)
 
 
@@ -849,8 +881,8 @@
 
 
 def shards(params, moment_one, moment_two, visible, counts, tile_pos, target):
-    keys = slot_keys(visible, counts)
-    request = plan(visible, counts)
+    keys = slot_keys(visible)
+    request = plan(visible)
     wanted = exchange(request)
     feats = project(params)
     centre = jnp.tile(tile_pos.reshape(2, 8), (1, 16))

time: 97.9 us -> 94.5 us (0.965)
  Pallas kernels: 41.9 us -> 38.7 us
  local copies, waits for them, and re-layouts: 11.7 us -> 10.2 us
    pallas_call x1, Pallas kernels: 23.4 us -> 21.1 us  [render(): pl.pallas_call(render_kernel, out_shape=(jax.ShapeDtypeStruct((640, 128),...]
    unnamed x27 -> x26, local copies, waits for them, and re-layouts: 7.2 us -> 5.8 us
where the time goes in v4:
time: 94.5 us; the launch traced here: 93.9 us
  Pallas kernels  38.7 us (41%)
  waiting for transfers between devices  22.4 us (24%)
  starting transfers between devices  21.9 us (23%)
  local copies, waits for them, and re-layouts  10.2 us (11%)
    all_to_all x3, waiting for transfers between devices, exchange(): flat = lax.all_to_all(flat, 'dev', split_axis=0, concat_axis=0, tiled=True)  22.4 us
    all_to_all x3, starting transfers between devices, exchange(): flat = lax.all_to_all(flat, 'dev', split_axis=0, concat_axis=0, tiled=True)  21.9 us
    pallas_call x1, Pallas kernels, render(): pl.pallas_call(render_kernel, out_shape=(jax.ShapeDtypeStruct((640, 128),...  21.1 us
    unnamed x26, local copies, waits for them, and re-layouts  5.8 us
    pallas_call x1, Pallas kernels, update(): pl.pallas_call(update_kernel, out_shape=(whole, whole, whole), in_specs=[...  5.05 us
    pallas_call x1, Pallas kernels, plan(): pl.pallas_call(plan_kernel, out_shape=jax.ShapeDtypeStruct((128, 128), jn...  5.03 us
    pallas_call x1, Pallas kernels, serve(): pl.pallas_call(serve_kernel, out_shape=jax.ShapeDtypeStruct((640, 128), F...  4.29 us
    reshape x2, local copies, waits for them, and re-layouts, slot_keys(): return jnp.transpose(keys.reshape(2, 8, 512), (0, 2, 1)).reshape(64, 128)  2.96 us
  transfers between devices with their start and end apart: 3, of which 3 were waited for; matrix products, arithmetic and copies ran while one was open for 5% of the time, Pallas kernels for 3%

profile of v4, /device:TPU:1, one launch (start us, length us, event | category | flops | bytes accessed | tf_op | source)
XLA Modules:
  0.0 93.9 jit_solution(4086510897555229929)
XLA Ops:
  0.6 0.7 copy-done.8
  1.4 5.0 %shard_map.94.request_ref = s32[128,128]{1,0:T(8,128)} custom-call(s32[16,512]{1,0:T(8,128)S(1)} %copy-done.8), custom_call_target="tpu_custom_call" | custom-call | tf_op jit(solution)/shard_map/pallas_call | solution.py:278
  6.4 11.5 %all-to-all-start = ((s32[128,1,128]{2,1,0:T(1,128)}), s32[128,1,128]{2,1,0:T(1,128)S(1)}, u32[]{:S(2)}, u32[]{:S(2)}) async-start(s32[128,1,128]{2,1,0:T(1,128)} %bitcast.1), calls=%async_computation | async-start | bytes 131072 | tf_op jit(solution)/shard_map/all_to_all | solution.py:879
  17.9 1.2 %copy-done = f32[59,4096]{1,0:T(8,128)S(1)} copy-done((f32[59,4096]{1,0:T(8,128)S(1)}, f32[59,4096]{1,0:T(8,128)}, u32[]{:S(2)}) %copy-start) | copy-done | bytes 966680
  19.2 0.8 shard_map.93.table_ref
  19.9 7.4 %all-to-all-done = s32[128,1,128]{2,1,0:T(1,128)S(1)} async-done(((s32[128,1,128]{2,1,0:T(1,128)}), s32[128,1,128]{2,1,0:T(1,128)S(1)}, u32[]{:S(2)}, u32[]{:S(2)}) %all-to-all-start) | async-done | bytes 65568 | tf_op jit(solution)/shard_map/all_to_all | solution.py:879
  27.4 4.3 %shard_map.95 = f32[640,128]{1,0:T(8,128)} custom-call(bf16[432,256]{1,0:T(8,128)(2,1)S(1)} %shard_map.93.table_ref, s32[128,128]{1,0:T(8,128)S(1)} %bitcast.19), custom_call_target="tpu_custom_call" | custom-call | tf_op jit(solution)/shard_map/pallas_call | solution.py:392
  31.6 4.6 %all-to-all-start.1 = ((f32[128,1,640]{2,1,0:T(1,128)}), f32[128,1,640]{2,1,0:T(1,128)S(1)}, u32[]{:S(2)}, u32[]{:S(2)}) async-start(f32[128,1,640]{2,1,0:T(1,128)} %bitcast.3), calls=%async_computation.1 | async-start | bytes 655360 | tf_op jit(solution)/shard_map/all_to_all | solution.py:879
  36.4 0.1 tile.12.centre_ref
  36.5 0.6 copy.17
  37.1 1.0 %copy.16 = s32[2,8,512]{1,2,0:T(8,128)} copy(s32[2,8,512]{2,1,0:T(8,128)S(1)} %fusion) | data formatting | bytes 65536 | tf_op jit(solution)/shard_map/reshape | solution.py:874
  38.1 2.0 %reshape.50.keys_ref = s32[64,128]{1,0:T(8,128)} reshape(s32[2,512,8]{2,1,0:T(8,128)} %bitcast.23) | data formatting | bytes 65536 | tf_op jit(solution)/shard_map/reshape | solution.py:874
  40.1 0.8 copy-done.10
  40.8 2.5 %shard_map.96.slots_hbm = s32[192,128]{1,0:T(8,128)S(1)} custom-call(s32[128,128]{1,0:T(8,128)} %shard_map.94.request_ref, s32[64,128]{1,0:T(8,128)S(1)} %copy-done.10, s32[2,128]{1,0:T(2,128)S(1)} %tile.12.centre_ref), custom_call_target="tpu_custom_call" | custom-call | tf_op jit(solution)/shard_map/pallas_call | solution.py:309
  43.3 0.6 copy-done.4
  44.0 3.9 %all-to-all-done.1 = f32[128,1,640]{2,1,0:T(1,128)S(1)} async-done(((f32[128,1,640]{2,1,0:T(1,128)}), f32[128,1,640]{2,1,0:T(1,128)S(1)}, u32[]{:S(2)}, u32[]{:S(2)}) %all-to-all-start.1) | async-done | bytes 327712 | tf_op jit(solution)/shard_map/all_to_all | solution.py:879
  47.9 0.9 copy-done.5
  48.8 0.8 copy-done.7
  49.6 21.1 %shard_map.97 = (f32[640,128]{1,0:T(8,128)S(1)}, f32[16,128]{1,0:T(8,128)S(1)}) custom-call(f32[640,128]{1,0:T(8,128)S(1)} %bitcast.18, s32[192,128]{1,0:T(8,128)S(1)} %copy-done.5, f32[48,256]{1,0:T(8,128)S(1)} %bitcast.22), custom_call_target="tpu_custom_call" | custom-call | tf_op jit(solution)/shard_map/pallas_call | solution.py:738
  70.7 0.7 copy-done.6
  71.4 5.8 %all-to-all-start.2 = ((f32[128,1,640]{2,1,0:T(1,128)}), f32[128,1,640]{2,1,0:T(1,128)S(1)}, u32[]{:S(2)}, u32[]{:S(2)}) async-start(f32[128,1,640]{2,1,0:T(1,128)} %bitcast.21), calls=%async_computation.2 | async-start | bytes 655360 | tf_op jit(solution)/shard_map/all_to_all | solution.py:879
  77.3 0.6 slice_reduce_fusion
  77.9 11.0 %all-to-all-done.2 = f32[128,1,640]{2,1,0:T(1,128)S(1)} async-done(((f32[128,1,640]{2,1,0:T(1,128)}), f32[128,1,640]{2,1,0:T(1,128)S(1)}, u32[]{:S(2)}, u32[]{:S(2)}) %all-to-all-start.2) | async-done | bytes 327712 | tf_op jit(solution)/shard_map/all_to_all | solution.py:879
  88.9 5.0 %shard_map.98 = (f32[59,4096]{1,0:T(8,128)}, f32[59,4096]{1,0:T(8,128)}, f32[59,4096]{1,0:T(8,128)}) custom-call(f32[640,128]{1,0:T(8,128)S(1)} %bitcast.17, s32[128,128]{1,0:T(8,128)S(1)} %bitcast.20, f32[59,4096]{1,0:T(8,128)S(1)} %copy-done.1, f32[59,4096]{1,0:T(8,128)S(1)} %copy-done.2, f32[59,4096]{1,0:T(8,128)S(1)} %copy-done.3), custom_call_target="tpu_custom_call" | custom-call | tf_op jit(solution)/shard_map/pallas_call | solution.py:858
  (23 shorter events, 0.1 us)
Async XLA Ops:
  0.6 0.8 copy-start.8
  6.4 20.9 %all-to-all-start = ((s32[128,1,128]{2,1,0:T(1,128)}), s32[128,1,128]{2,1,0:T(1,128)S(1)}, u32[]{:S(2)}, u32[]{:S(2)}) async-start(s32[128,1,128]{2,1,0:T(1,128)} %bitcast.1), calls=%async_computation | async-start | bytes 131072 | tf_op jit(solution)/shard_map/all_to_all | solution.py:879
  17.9 1.2 %copy-start = (f32[59,4096]{1,0:T(8,128)S(1)}, f32[59,4096]{1,0:T(8,128)}, u32[]{:S(2)}) copy-start(f32[59,4096]{1,0:T(8,128)} %params_ref.3) | copy-start | bytes 2899972
  27.3 8.9 %copy-start.11 = (bf16[16,3,256]{2,0,1:T(8,128)(2,1)S(1)}, bf16[16,3,256]{2,0,1:T(8,128)(2,1)}, u32[]{:S(2)}) copy-start(bf16[16,3,256]{2,0,1:T(8,128)(2,1)} %param.12) | copy-start | bytes 73732
  27.3 8.9 %copy-start.12 = (s32[16]{0:T(128)S(1)}, s32[16]{0:T(128)}, u32[]{:S(2)}) copy-start(s32[16]{0:T(128)} %param.11) | copy-start | bytes 196
  27.4 9.8 %copy-start.9 = (s32[16,512]{1,0:T(8,128)S(1)}, s32[16,512]{1,0:T(8,128)}, u32[]{:S(2)}) copy-start(s32[16,512]{1,0:T(8,128)} %visible_ref.1) | copy-start | bytes 98308
  31.6 57.2 %copy-start.3 = (f32[59,4096]{1,0:T(8,128)S(1)}, f32[59,4096]{1,0:T(8,128)}, u32[]{:S(2)}) copy-start(f32[59,4096]{1,0:T(8,128)} %two_ref.1) | copy-start | bytes 2899972
  31.6 16.2 %all-to-all-start.1 = ((f32[128,1,640]{2,1,0:T(1,128)}), f32[128,1,640]{2,1,0:T(1,128)S(1)}, u32[]{:S(2)}, u32[]{:S(2)}) async-start(f32[128,1,640]{2,1,0:T(1,128)} %bitcast.3), calls=%async_computation.1 | async-start | bytes 655360 | tf_op jit(solution)/shard_map/all_to_all | solution.py:879
  37.1 51.8 %copy-start.2 = (f32[59,4096]{1,0:T(8,128)S(1)}, f32[59,4096]{1,0:T(8,128)}, u32[]{:S(2)}) copy-start(f32[59,4096]{1,0:T(8,128)} %one_ref.1) | copy-start | bytes 2899972
  38.1 50.8 %copy-start.1 = (f32[59,4096]{1,0:T(8,128)S(1)}, f32[59,4096]{1,0:T(8,128)}, u32[]{:S(2)}) copy-start(f32[59,4096]{1,0:T(8,128)} %params_ref.3) | copy-start | bytes 2899972
  40.1 0.8 copy-start.10
  43.3 0.6 copy-start.4
  47.9 0.9 copy-start.5
  48.8 0.8 copy-start.7
  70.7 0.7 copy-start.6
  71.4 17.5 %all-to-all-start.2 = ((f32[128,1,640]{2,1,0:T(1,128)}), f32[128,1,640]{2,1,0:T(1,128)S(1)}, u32[]{:S(2)}, u32[]{:S(2)}) async-start(f32[128,1,640]{2,1,0:T(1,128)} %bitcast.21), calls=%async_computation.2 | async-start | bytes 655360 | tf_op jit(solution)/shard_map/all_to_all | solution.py:879

commit v5 on v4

--- a/solution.py
+++ b/solution.py
@@ -41,8 +41,8 @@
 BF16 = jnp.bfloat16
 VMEM = pl.BlockSpec(memory_space=pltpu.VMEM)
 HBM = pl.BlockSpec(memory_space=pltpu.HBM)
-PU = 8
-GU = 4
+GU = 8
+TABLE_ROWS = 27
 
 
 def harmonics(dir_x, dir_y, dir_z):
@@ -212,7 +212,7 @@
     return parts
 
 
-def plan_kernel(visible_ref, request_ref, owner_s, rank_s, local_s):
+def plan_kernel(visible_ref, request_ref):
     lane = iota((8, 128), 1)
     sublane = iota((8, 128), 0)
     keys = []
@@ -253,22 +253,25 @@
         whole = jnp.maximum(whole, jnp.where(lane >= step, pltpu.roll(whole, step, 1), 0))
     whole = jnp.where(lane >= 1, pltpu.roll(whole, 1, 1), 0)
     above = jnp.maximum(whole, jnp.where(sublane >= 1, pltpu.roll(column, 1, 0), 0))
-    for number in range(8):
-        rows = slice(number * 8, (number + 1) * 8)
-        rank = counts[number] - jnp.maximum(bases[number], above)
-        owner_s[rows, :] = keys[number] >> 12
-        rank_s[rows, :] = jnp.where(fresh[number], rank, -1)
-        local_s[rows, :] = keys[number] & (G_DEV - 1)
-
-    def fill(index, total):
-        local = pair(local_s, index)
-        match = pair(rank_s, index) == iota((64, 256), 0)
-        high = jnp.where(match, (local >> 6).astype(F32), 0.0)
-        low = jnp.where(match, (local & 63).astype(F32), 0.0)
-        parts = jnp.concatenate([high, low], axis=0).astype(BF16)
-        return total + dot_nt(parts, one_hot(pair(owner_s, index), 128))
-
-    filled = lax.fori_loop(0, 32, fill, jnp.zeros((128, 128), F32), unroll=PU)
+    filled = jnp.zeros((128, 128), F32)
+    for half in range(4):
+        lanes, marks = [], []
+        for number in (2 * half, 2 * half + 1):
+            rank = counts[number] - jnp.maximum(bases[number], above)
+            rank = jnp.where(fresh[number], rank, -1)
+            owner = keys[number] >> 12
+            local = keys[number] & (G_DEV - 1)
+            high, low = ((local >> 6).astype(F32), (local & 63).astype(F32))
+            for row in range(8):
+                cut = slice(row, row + 1)
+                match = iota((64, 128), 0) == rank[cut]
+                pieces = [
+                    jnp.where(match, jnp.broadcast_to(part[cut], (64, 128)), 0.0)
+                    for part in (high, low)
+                ]
+                marks.append(jnp.concatenate(pieces, axis=0).astype(BF16))
+                lanes.append(one_hot(owner[cut], 128))
+        filled = filled + dot_nt(jnp.concatenate(marks, axis=1), jnp.concatenate(lanes, axis=1))
     locals_of = (filled[0:64] * 64.0 + filled[64:128]).astype(jnp.int32)
     padded = jnp.concatenate([locals_of, jnp.zeros((64, 128), jnp.int32)], axis=0)
     request_ref[...] = jnp.transpose(padded)
@@ -280,7 +283,6 @@
         out_shape=jax.ShapeDtypeStruct((128, 128), jnp.int32),
         in_specs=[VMEM],
         out_specs=VMEM,
-        scratch_shapes=[pltpu.VMEM((64, 128), jnp.int32)] * 3,
         compiler_params=pltpu.CompilerParams(vmem_limit_bytes=32 * 1024 * 1024),
     )(visible)
 
@@ -321,23 +323,33 @@
     found = dot_nn(table_ref[...], lanes)
     for feature in range(9):
         parts = [
-            found[(9 * part + feature) * size : (9 * part + feature + 1) * size]
-            for part in range(3)
+            found[part_row(part, feature) * size : (part_row(part, feature) + 1) * size]
+            for part in range(parts_of(feature))
         ]
-        picked = jnp.where(match, (parts[0] + parts[1]) + parts[2], 0.0)
+        total = parts[0] + parts[1]
+        if len(parts) == 3:
+            total = total + parts[2]
+        picked = jnp.where(match, total, 0.0)
         line = jnp.sum(picked, axis=0, keepdims=True)
         out_ref[pl.ds(64 * feature + 2 * index, 1), :] = line[:, 0:128]
         out_ref[pl.ds(64 * feature + 2 * index + 1, 1), :] = line[:, 128:256]
 
 
-def three_parts(value, table_ref, feature, size):
-    high = value.astype(BF16)
-    rest = value - high.astype(F32)
-    middle = rest.astype(BF16)
-    low = (rest - middle.astype(F32)).astype(BF16)
-    for part, piece in enumerate((high, middle, low)):
-        base = (9 * part + feature) * size
+def parts_of(feature):
+    return 3
+
+
+def part_row(part, feature):
+    return part * 9 + feature
+
+
+def put_parts(value, table_ref, feature, size):
+    rest = value
+    for part in range(parts_of(feature)):
+        piece = rest.astype(BF16)
+        base = part_row(part, feature) * size
         table_ref[base : base + size, :] = piece
+        rest = rest - piece.astype(F32)
 
 
 def project_kernel(params_ref, feats_ref, rows_s):
@@ -357,13 +369,13 @@
         feats.append(total)
     for index in range(9):
         rows = feats[index]
-        three_parts(jnp.concatenate([rows[0:16], rows[16:32]], axis=1), feats_ref, index, 16)
+        put_parts(jnp.concatenate([rows[0:16], rows[16:32]], axis=1), feats_ref, index, 16)
 
 
 def project(params):
     return pl.pallas_call(
         project_kernel,
-        out_shape=jax.ShapeDtypeStruct((27 * 16, 256), BF16),
+        out_shape=jax.ShapeDtypeStruct((TABLE_ROWS * 16, 256), BF16),
         in_specs=[VMEM],
         out_specs=VMEM,
         scratch_shapes=[pltpu.VMEM((59 * 32, 128), F32)],
@@ -422,7 +434,7 @@
 
 
 def render_kernel(
-    arrived_ref,
+    arrived_hbm,
     slots_hbm,
     target_hbm,
     out_ref,
@@ -438,19 +450,23 @@
     parts_s,
     slots_ref,
     target_ref,
+    arrived_ref,
     sems,
 ):
     slots_copy = pltpu.make_async_copy(slots_hbm, slots_ref, sems.at[0])
     target_copy = pltpu.make_async_copy(target_hbm, target_ref, sems.at[1])
+    arrived_copy = pltpu.make_async_copy(arrived_hbm, arrived_ref, sems.at[2])
+    arrived_copy.start()
     slots_copy.start()
     target_copy.start()
+    arrived_copy.wait()
     for part in range(5):
         table_s[part * 128 : (part + 1) * 128, :] = jnp.transpose(
             arrived_ref[pl.ds(part, 128, stride=5), :]
         )
     for feature in range(9):
         base = feature * 64
-        three_parts(
+        put_parts(
             jnp.concatenate(
                 [table_s[base : base + 32, :], table_s[base + 32 : base + 64, :]], axis=1
             ),
@@ -554,23 +570,27 @@
         for group in range(2):
             left, colors = state[2 * group : 2 * group + 2]
             coef = coef_of(group, index)
-            alpha = jnp.exp2(dot_nn(jnp.transpose(coef).astype(BF16), basis))
+            turned = jnp.transpose(coef)
+            alpha = jnp.exp2(dot_nn(turned.astype(BF16), basis))
+            tones = [
+                turned[:, 18 + ch : 19 + ch] + turned[:, 21 + ch : 22 + ch] for ch in range(3)
+            ]
             rows = chunk_rows(group, index)
             alpha_s[rows, :] = alpha
             parts = []
+            sums = [colors[ch * 8 : (ch + 1) * 8] for ch in range(3)]
             for slot in range(32):
-                weight = alpha[slot * 8 : (slot + 1) * 8] * left
+                cut = slice(slot * 8, (slot + 1) * 8)
+                weight = alpha[cut] * left
                 left = left - weight
                 parts.append(weight)
+                sums = [sums[ch] + weight * tones[ch][cut] for ch in range(3)]
+            colors = jnp.concatenate(sums, axis=0)
             weights = jnp.concatenate(parts, axis=0)
             weight_s[rows, :] = weights
             high, low = split(weights)
             parts_s[rows, 512:768] = high
             parts_s[rows, 768:1024] = low
-            col_high = spread(coef, 18)
-            col_low = spread(coef, 21)
-            both = dot_nn(jnp.concatenate([col_high, col_low], axis=0).astype(BF16), high)
-            colors = colors + both[0:24] + both[24:48] + dot_nn(col_high.astype(BF16), low)
             results += [left, colors]
         return tuple(results)
 
@@ -741,10 +761,10 @@
             jax.ShapeDtypeStruct((640, 128), F32),
             jax.ShapeDtypeStruct((16, 128), F32),
         ),
-        in_specs=[VMEM, HBM, HBM],
+        in_specs=[HBM, HBM, HBM],
         out_specs=(VMEM, VMEM),
         scratch_shapes=[
-            pltpu.VMEM((27 * 32, 256), BF16),
+            pltpu.VMEM((TABLE_ROWS * 32, 256), BF16),
             pltpu.VMEM((640, 128), F32),
             pltpu.VMEM((64 * 24, 128), F32),
             pltpu.VMEM((8192, 256), F32),
@@ -755,9 +775,10 @@
             pltpu.VMEM((8192, 1024), BF16),
             pltpu.VMEM((192, 128), jnp.int32),
             pltpu.VMEM((48, 256), F32),
-            pltpu.SemaphoreType.DMA((2,)),
+            pltpu.VMEM((640, 128), F32),
+            pltpu.SemaphoreType.DMA((3,)),
         ],
-        compiler_params=pltpu.CompilerParams(vmem_limit_bytes=48 * 1024 * 1024),
+        compiler_params=pltpu.CompilerParams(vmem_limit_bytes=62 * 1024 * 1024),
     )(arrived, slots, target)
 
 

time: 94.5 us -> 93 us (0.984)
  waiting for transfers between devices: 22.4 us -> 24.6 us
  local copies, waits for them, and re-layouts: 10.2 us -> 8.43 us
  Pallas kernels: 38.7 us -> 37.7 us
  starting transfers between devices: 21.9 us -> 20.9 us
    reshape x2, local copies, waits for them, and re-layouts: 2.96 us -> 0.45 us  [slot_keys(): return jnp.transpose(keys.reshape(2, 8, 512), (0, 2, 1)).reshape(64, 128)]
    all_to_all x3, waiting for transfers between devices: 22.4 us -> 24.6 us  [exchange(): flat = lax.all_to_all(flat, 'dev', split_axis=0, concat_axis=0, tiled=True)]
    all_to_all x3, starting transfers between devices: 21.9 us -> 20.9 us  [exchange(): flat = lax.all_to_all(flat, 'dev', split_axis=0, concat_axis=0, tiled=True)]
    unnamed x26 -> x22, local copies, waits for them, and re-layouts: 5.8 us -> 6.58 us
  transfers between devices with their start and end apart: 3 -> 3, of which waited for: 3 -> 3; matrix products, arithmetic and copies ran while one was open for 5% -> 2% of each run, Pallas kernels for 3% -> 4%
where the time goes in v5:
time: 93 us; the launch traced here: 92.4 us
  Pallas kernels  37.7 us (41%)
  waiting for transfers between devices  24.6 us (26%)
  starting transfers between devices  20.9 us (22%)
  local copies, waits for them, and re-layouts  8.43 us (9%)
    all_to_all x3, waiting for transfers between devices, exchange(): flat = lax.all_to_all(flat, 'dev', split_axis=0, concat_axis=0, tiled=True)  24.6 us
    pallas_call x1, Pallas kernels, render(): pl.pallas_call(render_kernel, out_shape=(jax.ShapeDtypeStruct((640, 128),...  21.2 us
    all_to_all x3, starting transfers between devices, exchange(): flat = lax.all_to_all(flat, 'dev', split_axis=0, concat_axis=0, tiled=True)  20.9 us
    unnamed x22, local copies, waits for them, and re-layouts  6.58 us
    pallas_call x1, Pallas kernels, update(): pl.pallas_call(update_kernel, out_shape=(whole, whole, whole), in_specs=[...  5.05 us
    pallas_call x1, Pallas kernels, plan(): pl.pallas_call(plan_kernel, out_shape=jax.ShapeDtypeStruct((128, 128), jn...  4.58 us
    pallas_call x1, Pallas kernels, serve(): pl.pallas_call(serve_kernel, out_shape=jax.ShapeDtypeStruct((640, 128), F...  3.57 us
    pallas_call x1, Pallas kernels, find(): pl.pallas_call(find_kernel, out_shape=jax.ShapeDtypeStruct((192, 128), jn...  2.51 us
  transfers between devices with their start and end apart: 3, of which 3 were waited for; matrix products, arithmetic and copies ran while one was open for 2% of the time, Pallas kernels for 4%

profile of v5, /device:TPU:1, one launch (start us, length us, event | category | flops | bytes accessed | tf_op | source)
XLA Modules:
  0.0 92.4 jit_solution(6938253769909055037)
XLA Ops:
  0.6 0.7 copy-done.5
  1.4 4.6 %shard_map.94.request_ref = s32[128,128]{1,0:T(8,128)} custom-call(s32[16,512]{1,0:T(8,128)S(1)} %copy-done.5), custom_call_target="tpu_custom_call" | custom-call | tf_op jit(solution)/shard_map/pallas_call | solution.py:281
  6.0 11.5 %all-to-all-start = ((s32[128,1,128]{2,1,0:T(1,128)}), s32[128,1,128]{2,1,0:T(1,128)S(1)}, u32[]{:S(2)}, u32[]{:S(2)}) async-start(s32[128,1,128]{2,1,0:T(1,128)} %bitcast.1), calls=%async_computation | async-start | bytes 131072 | tf_op jit(solution)/shard_map/all_to_all | solution.py:900
  17.5 1.2 %copy-done = f32[59,4096]{1,0:T(8,128)S(1)} copy-done((f32[59,4096]{1,0:T(8,128)S(1)}, f32[59,4096]{1,0:T(8,128)}, u32[]{:S(2)}) %copy-start) | copy-done | bytes 966680
  18.7 0.8 shard_map.93.table_ref
  19.5 7.4 %all-to-all-done = s32[128,1,128]{2,1,0:T(1,128)S(1)} async-done(((s32[128,1,128]{2,1,0:T(1,128)}), s32[128,1,128]{2,1,0:T(1,128)S(1)}, u32[]{:S(2)}, u32[]{:S(2)}) %all-to-all-start) | async-done | bytes 65568 | tf_op jit(solution)/shard_map/all_to_all | solution.py:900
  26.9 3.6 %shard_map.95 = f32[640,128]{1,0:T(8,128)} custom-call(bf16[432,256]{1,0:T(8,128)(2,1)S(1)} %shard_map.93.table_ref, s32[128,128]{1,0:T(8,128)S(1)} %bitcast.18), custom_call_target="tpu_custom_call" | custom-call | tf_op jit(solution)/shard_map/pallas_call | solution.py:404
  30.5 4.8 %all-to-all-start.1 = ((f32[128,1,640]{2,1,0:T(1,128)}), f32[128,1,640]{2,1,0:T(1,128)S(1)}, u32[]{:S(2)}, u32[]{:S(2)}) async-start(f32[128,1,640]{2,1,0:T(1,128)} %bitcast.3), calls=%async_computation.1 | async-start | bytes 655360 | tf_op jit(solution)/shard_map/all_to_all | solution.py:900
  35.3 0.6 copy-done.10
  36.1 0.6 copy.17
  36.7 0.1 copy-done.6
  36.9 0.2 copy.16
  37.1 0.3 reshape.50.keys_ref
  37.3 2.5 %shard_map.96.slots_hbm = s32[192,128]{1,0:T(8,128)S(1)} custom-call(s32[128,128]{1,0:T(8,128)} %shard_map.94.request_ref, s32[64,128]{1,0:T(8,128)S(1)} %reshape.50.keys_ref, s32[2,128]{1,0:T(2,128)S(1)} %tile.12.centre_ref), custom_call_target="tpu_custom_call" | custom-call | tf_op jit(solution)/shard_map/pallas_call | solution.py:311
  39.9 0.6 copy-done.4
  40.5 6.2 %all-to-all-done.1 = f32[128,1,640]{2,1,0:T(1,128)S(1)} async-done(((f32[128,1,640]{2,1,0:T(1,128)}), f32[128,1,640]{2,1,0:T(1,128)S(1)}, u32[]{:S(2)}, u32[]{:S(2)}) %all-to-all-start.1) | async-done | bytes 327712 | tf_op jit(solution)/shard_map/all_to_all | solution.py:900
  46.7 0.7 copy-done.7
  47.4 21.2 %shard_map.97 = (f32[640,128]{1,0:T(8,128)}, f32[16,128]{1,0:T(8,128)}) custom-call(f32[640,128]{1,0:T(8,128)} %bitcast.21, s32[192,128]{1,0:T(8,128)} %copy-done.4, f32[48,256]{1,0:T(8,128)} %bitcast.23), custom_call_target="tpu_custom_call" | custom-call | tf_op jit(solution)/shard_map/pallas_call | solution.py:758
  68.7 4.6 %all-to-all-start.2 = ((f32[128,1,640]{2,1,0:T(1,128)}), f32[128,1,640]{2,1,0:T(1,128)S(1)}, u32[]{:S(2)}, u32[]{:S(2)}) async-start(f32[128,1,640]{2,1,0:T(1,128)} %bitcast.22), calls=%async_computation.2 | async-start | bytes 655360 | tf_op jit(solution)/shard_map/all_to_all | solution.py:900
  73.3 0.6 slice_reduce_fusion
  73.9 11.0 %all-to-all-done.2 = f32[128,1,640]{2,1,0:T(1,128)S(1)} async-done(((f32[128,1,640]{2,1,0:T(1,128)}), f32[128,1,640]{2,1,0:T(1,128)S(1)}, u32[]{:S(2)}, u32[]{:S(2)}) %all-to-all-start.2) | async-done | bytes 327712 | tf_op jit(solution)/shard_map/all_to_all | solution.py:900
  84.9 1.2 %copy-done.2 = f32[59,4096]{1,0:T(8,128)S(1)} copy-done((f32[59,4096]{1,0:T(8,128)S(1)}, f32[59,4096]{1,0:T(8,128)}, u32[]{:S(2)}) %copy-start.2) | copy-done | bytes 966680
  86.1 1.2 %copy-done.3 = f32[59,4096]{1,0:T(8,128)S(1)} copy-done((f32[59,4096]{1,0:T(8,128)S(1)}, f32[59,4096]{1,0:T(8,128)}, u32[]{:S(2)}) %copy-start.3) | copy-done | bytes 966680
  87.3 5.0 %shard_map.98 = (f32[59,4096]{1,0:T(8,128)}, f32[59,4096]{1,0:T(8,128)}, f32[59,4096]{1,0:T(8,128)}) custom-call(f32[640,128]{1,0:T(8,128)S(1)} %bitcast.17, s32[128,128]{1,0:T(8,128)S(1)} %bitcast.19, f32[59,4096]{1,0:T(8,128)S(1)} %copy-done.1, f32[59,4096]{1,0:T(8,128)S(1)} %copy-done.2, f32[59,4096]{1,0:T(8,128)S(1)} %copy-done.3), custom_call_target="tpu_custom_call" | custom-call | tf_op jit(solution)/shard_map/pallas_call | solution.py:879
  (19 shorter events, 0.2 us)
Async XLA Ops:
  0.6 0.8 copy-start.5
  6.0 20.9 %all-to-all-start = ((s32[128,1,128]{2,1,0:T(1,128)}), s32[128,1,128]{2,1,0:T(1,128)S(1)}, u32[]{:S(2)}, u32[]{:S(2)}) async-start(s32[128,1,128]{2,1,0:T(1,128)} %bitcast.1), calls=%async_computation | async-start | bytes 131072 | tf_op jit(solution)/shard_map/all_to_all | solution.py:900
  17.5 1.2 %copy-start = (f32[59,4096]{1,0:T(8,128)S(1)}, f32[59,4096]{1,0:T(8,128)}, u32[]{:S(2)}) copy-start(f32[59,4096]{1,0:T(8,128)} %params_ref.3) | copy-start | bytes 2899972
  30.5 4.8 %copy-start.8 = (bf16[16,3,256]{2,0,1:T(8,128)(2,1)S(1)}, bf16[16,3,256]{2,0,1:T(8,128)(2,1)}, u32[]{:S(2)}) copy-start(bf16[16,3,256]{2,0,1:T(8,128)(2,1)} %param.12) | copy-start | bytes 73732
  30.5 16.2 %all-to-all-start.1 = ((f32[128,1,640]{2,1,0:T(1,128)}), f32[128,1,640]{2,1,0:T(1,128)S(1)}, u32[]{:S(2)}, u32[]{:S(2)}) async-start(f32[128,1,640]{2,1,0:T(1,128)} %bitcast.3), calls=%async_computation.1 | async-start | bytes 655360 | tf_op jit(solution)/shard_map/all_to_all | solution.py:900
  35.3 0.7 copy-start.10
  36.1 0.8 copy-start.6
  37.1 47.8 %copy-start.1 = (f32[59,4096]{1,0:T(8,128)S(1)}, f32[59,4096]{1,0:T(8,128)}, u32[]{:S(2)}) copy-start(f32[59,4096]{1,0:T(8,128)} %params_ref.3) | copy-start | bytes 2899972
  39.9 0.6 copy-start.4
  46.7 0.7 copy-start.7
  68.7 4.6 %copy-start.9 = (f32[16,128]{1,0:T(8,128)S(1)}, f32[16,128]{1,0:T(8,128)}, u32[]{:S(2)}) copy-start(f32[16,128]{1,0:T(8,128)} %get-tuple-element.9) | copy-start | bytes 24580
  68.7 16.2 %all-to-all-start.2 = ((f32[128,1,640]{2,1,0:T(1,128)}), f32[128,1,640]{2,1,0:T(1,128)S(1)}, u32[]{:S(2)}, u32[]{:S(2)}) async-start(f32[128,1,640]{2,1,0:T(1,128)} %bitcast.22), calls=%async_computation.2 | async-start | bytes 655360 | tf_op jit(solution)/shard_map/all_to_all | solution.py:900
  84.9 1.2 %copy-start.2 = (f32[59,4096]{1,0:T(8,128)S(1)}, f32[59,4096]{1,0:T(8,128)}, u32[]{:S(2)}) copy-start(f32[59,4096]{1,0:T(8,128)} %one_ref.1) | copy-start | bytes 2899972
  86.1 1.2 %copy-start.3 = (f32[59,4096]{1,0:T(8,128)S(1)}, f32[59,4096]{1,0:T(8,128)}, u32[]{:S(2)}) copy-start(f32[59,4096]{1,0:T(8,128)} %two_ref.1) | copy-start | bytes 2899972

commit v6 on v5

--- a/solution.py
+++ b/solution.py
@@ -778,7 +778,7 @@
             pltpu.VMEM((640, 128), F32),
             pltpu.SemaphoreType.DMA((3,)),
         ],
-        compiler_params=pltpu.CompilerParams(vmem_limit_bytes=62 * 1024 * 1024),
+        compiler_params=pltpu.CompilerParams(vmem_limit_bytes=56 * 1024 * 1024),
     )(arrived, slots, target)
 
 

time: 93 us -> 90.7 us (0.975)
  local copies, waits for them, and re-layouts: 8.43 us -> 6.42 us
  waiting for transfers between devices: 24.6 us -> 23.4 us
  starting transfers between devices: 20.9 us -> 22 us
    unnamed x22 -> x20, local copies, waits for them, and re-layouts: 6.58 us -> 2.64 us
    reshape x2, local copies, waits for them, and re-layouts: 0.45 us -> 2.36 us  [slot_keys(): return jnp.transpose(keys.reshape(2, 8, 512), (0, 2, 1)).reshape(64, 128)]
    all_to_all x3, waiting for transfers between devices: 24.6 us -> 23.4 us  [exchange(): flat = lax.all_to_all(flat, 'dev', split_axis=0, concat_axis=0, tiled=True)]
    all_to_all x3, starting transfers between devices: 20.9 us -> 22 us  [exchange(): flat = lax.all_to_all(flat, 'dev', split_axis=0, concat_axis=0, tiled=True)]
  transfers between devices with their start and end apart: 3 -> 3, of which waited for: 3 -> 3; matrix products, arithmetic and copies ran while one was open for 2% -> 4% of each run, Pallas kernels for 4% -> 4%
where the time goes in v6:
time: 90.7 us; the launch traced here: 90.2 us
  Pallas kernels  37.6 us (41%)
  waiting for transfers between devices  23.4 us (26%)
  starting transfers between devices  22 us (24%)
  local copies, waits for them, and re-layouts  6.42 us (7%)
    all_to_all x3, waiting for transfers between devices, exchange(): flat = lax.all_to_all(flat, 'dev', split_axis=0, concat_axis=0, tiled=True)  23.4 us
    all_to_all x3, starting transfers between devices, exchange(): flat = lax.all_to_all(flat, 'dev', split_axis=0, concat_axis=0, tiled=True)  22 us
    pallas_call x1, Pallas kernels, render(): pl.pallas_call(render_kernel, out_shape=(jax.ShapeDtypeStruct((640, 128),...  21.2 us
    pallas_call x1, Pallas kernels, update(): pl.pallas_call(update_kernel, out_shape=(whole, whole, whole), in_specs=[...  5.05 us
    pallas_call x1, Pallas kernels, plan(): pl.pallas_call(plan_kernel, out_shape=jax.ShapeDtypeStruct((128, 128), jn...  4.58 us
    pallas_call x1, Pallas kernels, serve(): pl.pallas_call(serve_kernel, out_shape=jax.ShapeDtypeStruct((640, 128), F...  3.57 us
    unnamed x20, local copies, waits for them, and re-layouts  2.64 us
    pallas_call x1, Pallas kernels, find(): pl.pallas_call(find_kernel, out_shape=jax.ShapeDtypeStruct((192, 128), jn...  2.46 us
  transfers between devices with their start and end apart: 3, of which 3 were waited for; matrix products, arithmetic and copies ran while one was open for 4% of the time, Pallas kernels for 4%

profile of v6, /device:TPU:1, one launch (start us, length us, event | category | flops | bytes accessed | tf_op | source)
XLA Modules:
  0.0 90.2 jit_solution(12332304046276908048)
XLA Ops:
  0.6 0.0 copy-start.5
  0.6 0.7 copy-done.5
  1.4 4.6 %shard_map.94.request_ref = s32[128,128]{1,0:T(8,128)} custom-call(s32[16,512]{1,0:T(8,128)S(1)} %copy-done.5), custom_call_target="tpu_custom_call" | custom-call | tf_op jit(solution)/shard_map/pallas_call | solution.py:281
  6.0 11.5 %all-to-all-start = ((s32[128,1,128]{2,1,0:T(1,128)}), s32[128,1,128]{2,1,0:T(1,128)S(1)}, u32[]{:S(2)}, u32[]{:S(2)}) async-start(s32[128,1,128]{2,1,0:T(1,128)} %bitcast.1), calls=%async_computation | async-start | bytes 131072 | tf_op jit(solution)/shard_map/all_to_all | solution.py:900
  17.5 0.0 copy-start
  17.5 1.2 %copy-done = f32[59,4096]{1,0:T(8,128)S(1)} copy-done((f32[59,4096]{1,0:T(8,128)S(1)}, f32[59,4096]{1,0:T(8,128)}, u32[]{:S(2)}) %copy-start) | copy-done | bytes 966680
  18.7 0.8 shard_map.93.table_ref
  19.5 7.4 %all-to-all-done = s32[128,1,128]{2,1,0:T(1,128)S(1)} async-done(((s32[128,1,128]{2,1,0:T(1,128)}), s32[128,1,128]{2,1,0:T(1,128)S(1)}, u32[]{:S(2)}, u32[]{:S(2)}) %all-to-all-start) | async-done | bytes 65568 | tf_op jit(solution)/shard_map/all_to_all | solution.py:900
  26.9 3.6 %shard_map.95 = f32[640,128]{1,0:T(8,128)} custom-call(bf16[432,256]{1,0:T(8,128)(2,1)S(1)} %shard_map.93.table_ref, s32[128,128]{1,0:T(8,128)S(1)} %bitcast.18), custom_call_target="tpu_custom_call" | custom-call | tf_op jit(solution)/shard_map/pallas_call | solution.py:404
  30.5 5.6 %all-to-all-start.1 = ((f32[128,1,640]{2,1,0:T(1,128)}), f32[128,1,640]{2,1,0:T(1,128)}, u32[]{:S(2)}, u32[]{:S(2)}) async-start(f32[128,1,640]{2,1,0:T(1,128)} %bitcast.3), calls=%async_computation.1 | async-start | bytes 655360 | tf_op jit(solution)/shard_map/all_to_all | solution.py:900
  36.1 0.1 tile.10
  36.2 0.1 tile.12.centre_ref
  36.3 0.6 copy.17
  36.9 1.0 %copy.16 = s32[2,8,512]{1,2,0:T(8,128)} copy(s32[2,8,512]{2,1,0:T(8,128)S(1)} %fusion) | data formatting | bytes 65536 | tf_op jit(solution)/shard_map/reshape | solution.py:895
  37.9 1.4 %reshape.50.keys_ref = s32[64,128]{1,0:T(8,128)S(1)} reshape(s32[2,512,8]{2,1,0:T(8,128)} %bitcast.20) | data formatting | bytes 65536 | tf_op jit(solution)/shard_map/reshape | solution.py:895
  39.3 2.5 %shard_map.96.slots_hbm = s32[192,128]{1,0:T(8,128)S(1)} custom-call(s32[128,128]{1,0:T(8,128)} %shard_map.94.request_ref, s32[64,128]{1,0:T(8,128)S(1)} %reshape.50.keys_ref, s32[2,128]{1,0:T(2,128)S(1)} %tile.12.centre_ref), custom_call_target="tpu_custom_call" | custom-call | tf_op jit(solution)/shard_map/pallas_call | solution.py:311
  41.7 0.6 copy-done.4
  42.4 5.0 %all-to-all-done.1 = f32[128,1,640]{2,1,0:T(1,128)} async-done(((f32[128,1,640]{2,1,0:T(1,128)}), f32[128,1,640]{2,1,0:T(1,128)}, u32[]{:S(2)}, u32[]{:S(2)}) %all-to-all-start.1) | async-done | bytes 327712 | tf_op jit(solution)/shard_map/all_to_all | solution.py:900
  47.3 21.2 %shard_map.97 = (f32[640,128]{1,0:T(8,128)}, f32[16,128]{1,0:T(8,128)}) custom-call(f32[640,128]{1,0:T(8,128)} %bitcast.4.arrived_hbm, s32[192,128]{1,0:T(8,128)} %copy-done.4, f32[48,256]{1,0:T(8,128)} %bitcast.22), custom_call_target="tpu_custom_call" | custom-call | tf_op jit(solution)/shard_map/pallas_call | solution.py:758
  68.6 0.0 copy-start.8
  68.6 4.9 %all-to-all-start.2 = ((f32[128,1,640]{2,1,0:T(1,128)}), f32[128,1,640]{2,1,0:T(1,128)S(1)}, u32[]{:S(2)}, u32[]{:S(2)}) async-start(f32[128,1,640]{2,1,0:T(1,128)} %bitcast.21), calls=%async_computation.2 | async-start | bytes 655360 | tf_op jit(solution)/shard_map/all_to_all | solution.py:900
  73.5 0.6 slice_reduce_fusion
  74.2 11.0 %all-to-all-done.2 = f32[128,1,640]{2,1,0:T(1,128)S(1)} async-done(((f32[128,1,640]{2,1,0:T(1,128)}), f32[128,1,640]{2,1,0:T(1,128)S(1)}, u32[]{:S(2)}, u32[]{:S(2)}) %all-to-all-start.2) | async-done | bytes 327712 | tf_op jit(solution)/shard_map/all_to_all | solution.py:900
  85.2 5.1 %shard_map.98 = (f32[59,4096]{1,0:T(8,128)}, f32[59,4096]{1,0:T(8,128)}, f32[59,4096]{1,0:T(8,128)}) custom-call(f32[640,128]{1,0:T(8,128)S(1)} %bitcast.17, s32[128,128]{1,0:T(8,128)S(1)} %bitcast.19, f32[59,4096]{1,0:T(8,128)S(1)} %copy-done.1, f32[59,4096]{1,0:T(8,128)S(1)} %copy-done.2, f32[59,4096]{1,0:T(8,128)S(1)} %copy-done.3), custom_call_target="tpu_custom_call" | custom-call | tf_op jit(solution)/shard_map/pallas_call | solution.py:879
  (17 shorter events, 0.0 us)
Async XLA Ops:
  0.6 0.8 copy-start.5
  6.0 20.9 %all-to-all-start = ((s32[128,1,128]{2,1,0:T(1,128)}), s32[128,1,128]{2,1,0:T(1,128)S(1)}, u32[]{:S(2)}, u32[]{:S(2)}) async-start(s32[128,1,128]{2,1,0:T(1,128)} %bitcast.1), calls=%async_computation | async-start | bytes 131072 | tf_op jit(solution)/shard_map/all_to_all | solution.py:900
  17.5 1.2 %copy-start = (f32[59,4096]{1,0:T(8,128)S(1)}, f32[59,4096]{1,0:T(8,128)}, u32[]{:S(2)}) copy-start(f32[59,4096]{1,0:T(8,128)} %params_ref.3) | copy-start | bytes 2899972
  26.9 9.2 %copy-start.7 = (bf16[16,3,256]{2,0,1:T(8,128)(2,1)S(1)}, bf16[16,3,256]{2,0,1:T(8,128)(2,1)}, u32[]{:S(2)}) copy-start(bf16[16,3,256]{2,0,1:T(8,128)(2,1)} %param.12) | copy-start | bytes 73732
  26.9 9.2 %copy-start.9 = (s32[16]{0:T(128)S(1)}, s32[16]{0:T(128)}, u32[]{:S(2)}) copy-start(s32[16]{0:T(128)} %param.11) | copy-start | bytes 196
  26.9 10.0 %copy-start.6 = (s32[16,512]{1,0:T(8,128)S(1)}, s32[16,512]{1,0:T(8,128)}, u32[]{:S(2)}) copy-start(s32[16,512]{1,0:T(8,128)} %visible_ref.1) | copy-start | bytes 98308
  30.5 54.7 %copy-start.3 = (f32[59,4096]{1,0:T(8,128)S(1)}, f32[59,4096]{1,0:T(8,128)}, u32[]{:S(2)}) copy-start(f32[59,4096]{1,0:T(8,128)} %two_ref.1) | copy-start | bytes 2899972
  30.5 16.9 %all-to-all-start.1 = ((f32[128,1,640]{2,1,0:T(1,128)}), f32[128,1,640]{2,1,0:T(1,128)}, u32[]{:S(2)}, u32[]{:S(2)}) async-start(f32[128,1,640]{2,1,0:T(1,128)} %bitcast.3), calls=%async_computation.1 | async-start | bytes 655360 | tf_op jit(solution)/shard_map/all_to_all | solution.py:900
  36.9 48.3 %copy-start.2 = (f32[59,4096]{1,0:T(8,128)S(1)}, f32[59,4096]{1,0:T(8,128)}, u32[]{:S(2)}) copy-start(f32[59,4096]{1,0:T(8,128)} %one_ref.1) | copy-start | bytes 2899972
  37.9 47.3 %copy-start.1 = (f32[59,4096]{1,0:T(8,128)S(1)}, f32[59,4096]{1,0:T(8,128)}, u32[]{:S(2)}) copy-start(f32[59,4096]{1,0:T(8,128)} %params_ref.3) | copy-start | bytes 2899972
  41.7 0.6 copy-start.4
  68.6 5.0 %copy-start.8 = (f32[16,128]{1,0:T(8,128)S(1)}, f32[16,128]{1,0:T(8,128)}, u32[]{:S(2)}) copy-start(f32[16,128]{1,0:T(8,128)} %get-tuple-element.9) | copy-start | bytes 24580
  68.6 16.6 %all-to-all-start.2 = ((f32[128,1,640]{2,1,0:T(1,128)}), f32[128,1,640]{2,1,0:T(1,128)S(1)}, u32[]{:S(2)}, u32[]{:S(2)}) async-start(f32[128,1,640]{2,1,0:T(1,128)} %bitcast.21), calls=%async_computation.2 | async-start | bytes 655360 | tf_op jit(solution)/shard_map/all_to_all | solution.py:900
